TPU v7x, 512 devices: a whole 4x8x8 slice. The times are simulated.
512 devices in a mesh: alpha: 32 (over x, z), beta: 16 (over y, core).
Axes of the slice: x: 4, y: 8, z: 8, core: 2. Of those that a mesh axis runs over, the one named last changes fastest.
Arguments:
- coeffs: bfloat16 [8192, 16384], P('alpha', 'beta'), may hold values from -6 to 6
- a_blocks: bfloat16 [2, 8192, 11, 128], P(None, 'alpha'), may hold values from -0.15625 to 0.15625
- a_list: int32 [2, 64, 11], replicated, may hold values from 0 to 63, as said below
- a_count: int32 [2, 64], replicated, may hold values from 4 to 11, as said below
- b_blocks: bfloat16 [2, 16384, 11, 128], P(None, 'beta'), may hold values from -0.15625 to 0.15625
- b_list: int32 [2, 128, 11], replicated, may hold values from 0 to 127, as said below
- b_count: int32 [2, 128], replicated, may hold values from 4 to 11, as said below
Outputs:
- sigma: float32 [8192, 16384], P('alpha', 'beta')
Inputs may be any that keep to these rules, and one draw needn't show every extreme that they name: `a_list`: every entry, valid slot or not, is an alpha block number. For each index r of alpha and each index o of alpha, the entries of all operators in the rows of blocks r * 2 to r * 2 + 1 that lie in blocks o * 2 to o * 2 + 1 name at most 1 distinct blocks, and some pair names exactly 1. `b_list`: the same with beta, 8 and 2. `a_count`: some row has all 11 slots valid. `b_count`: some row has all 11 slots valid.
All inputs are finite; a program needn't handle non-finite values.
Results may differ from a plain program's by a relative error of at most 0.0029.
Values may be sent and summed in bfloat16 or wider, within the bound.
No kernel may reach another device: no remote copies, remote signals or barrier semaphores. Data moves between devices by JAX's collectives and lax.ppermute only.
A program may use at most 128 MiB of HBM per device.

v0:
```python
import jax
import jax.numpy as jnp
from jax import lax
from jax.sharding import PartitionSpec as P

FROM_B = 2


def arrange(entries, owners, per_owner, capacity):
    operators, total, list_slots = entries.shape
    flattened = entries.reshape(operators, owners, per_owner * list_slots)
    matches = flattened[..., None] == jnp.arange(total, dtype=jnp.int32)
    present = jnp.any(matches, axis=(0, 2)).reshape(owners, owners, per_owner).astype(jnp.int32)
    ranking = jnp.cumsum(present, axis=2)
    position = jnp.arange(capacity, dtype=jnp.int32) + 1
    chosen_bits = (present[..., None] == 1) & (ranking[..., None] == position)
    local_ids = jnp.arange(per_owner, dtype=jnp.int32)[None, None, :, None]
    wanted = jnp.sum(local_ids * chosen_bits.astype(jnp.int32), axis=2)
    return (wanted, ranking)


def locate(entries, ranking_here, per_owner, capacity):
    owner = entries // per_owner
    local_id = entries % per_owner
    return owner * capacity + ranking_here[owner, local_id] - 1


def pick_columns(pool_piece, index_piece):
    return pool_piece[:, index_piece]


def on_device(coeffs, a_blocks, a_list, a_count, b_blocks, b_list, b_count):
    operators, local_rows, list_slots, block_size = a_blocks.shape
    local_cols = coeffs.shape[1]
    row_blocks = local_rows // block_size
    col_blocks = local_cols // block_size
    col_capacity = FROM_B
    alpha_size = lax.axis_size("alpha")
    beta_size = lax.axis_size("beta")
    alpha_here = lax.axis_index("alpha")
    beta_here = lax.axis_index("beta")
    slot_ids = jnp.arange(list_slots, dtype=jnp.int32)
    alpha_mine = lax.dynamic_slice_in_dim(a_list, alpha_here * row_blocks, row_blocks, 1)
    alpha_counts = lax.dynamic_slice_in_dim(a_count, alpha_here * row_blocks, row_blocks, 1)
    alpha_valid = slot_ids < alpha_counts[..., None]
    alpha_kept = jnp.where(
        alpha_valid[:, :, None, :, None],
        a_blocks.reshape(operators, row_blocks, block_size, list_slots, block_size),
        jnp.zeros((), jnp.bfloat16),
    )
    gathered = lax.all_gather(coeffs, "alpha", axis=0, tiled=True)
    chosen = gathered.reshape(alpha_size * row_blocks, block_size, local_cols)[alpha_mine]
    inter = jnp.einsum("kbrsi,kbsic->kbrc", alpha_kept, chosen, preferred_element_type=jnp.float32)
    inter = inter.astype(jnp.bfloat16).reshape(operators, local_rows, col_blocks, block_size)
    wanted_cols, ranking_cols = arrange(b_list, beta_size, col_blocks, col_capacity)
    outgoing_cols = inter[:, :, wanted_cols[:, beta_here, :], :]
    incoming_cols = lax.all_to_all(outgoing_cols, "beta", split_axis=2, concat_axis=2, tiled=True)
    beta_mine = lax.dynamic_slice_in_dim(b_list, beta_here * col_blocks, col_blocks, 1)
    beta_counts = lax.dynamic_slice_in_dim(b_count, beta_here * col_blocks, col_blocks, 1)
    beta_valid = slot_ids < beta_counts[..., None]
    beta_kept = jnp.where(
        beta_valid[:, :, None, :, None],
        b_blocks.reshape(operators, col_blocks, block_size, list_slots, block_size),
        jnp.zeros((), jnp.bfloat16),
    )
    source_cols = locate(beta_mine, ranking_cols[beta_here], col_blocks, col_capacity)
    pooled = incoming_cols.reshape(operators, local_rows, beta_size * col_capacity, block_size)
    picked = jax.vmap(pick_columns)(pooled, source_cols)
    sigma = jnp.einsum("kabsj,kbrsj->abr", picked, beta_kept, preferred_element_type=jnp.float32)
    return sigma.reshape(local_rows, local_cols)


def solution(mesh):
    in_specs = (
        P("alpha", "beta"),
        P(None, "alpha", None, None),
        P(),
        P(),
        P(None, "beta", None, None),
        P(),
        P(),
    )
    out_specs = P("alpha", "beta")
    return jax.shard_map(
        on_device, mesh=mesh, in_specs=in_specs, out_specs=out_specs, check_vma=False
    )
```

profile of v0, /device:TPU:1, one launch (start us, length us, event | category | flops | bytes accessed | tf_op | source)
XLA Modules:
  0.0 320.6 jit_solution(14596276022803924358)
XLA Ops:
  6.5 0.7 all-gather.2.cloned.1.call-update
  7.3 0.8 compare_select_fusion
  8.1 0.1 copy.32
  8.2 0.8 copy.33
  9.2 0.5 fusion.3
  9.7 0.1 copy.34
  10.0 0.1 copy.35
  10.1 0.1 select_reduce_fusion
  10.6 0.1 reshape.87
  10.7 0.8 constant_dynamic-slice_fusion.2
  11.5 150.9 %all-gather.2.cloned.1.call-done = bf16[8192,1024]{1,0:T(8,128)(2,1)} async-done(((bf16[256,1024]{1,0:T(8,128)(2,1)}), bf16[8192,1024]{1,0:T(8,128)(2,1)}) %all-gather.2.cloned.1.call-update) | async-done | bytes 16777232 | tf_op jit(solution)/shard_map/all_gather | solution.py:51
  162.5 12.0 %gather_fusion = bf16[44,128,1024]{2,1,0:T(8,128)(2,1)} fusion(bf16[64,128,1024]{2,1,0:T(8,128)(2,1)} %bitcast.48, s32[1024]{0:T(1024)S(1)} %pad_clamp_fusion.1), kind=kCustom, calls=%fused_computation | custom fusion | bytes 23068848 | tf_op jit(solution)/shard_map/gather | solution.py:52
  174.5 6.2 %bitcast_convert_fusion = bf16[2,2,128,1024]{3,2,1,0:T(8,128)(2,1)S(1)} fusion(bf16[2,2,11,128,1024]{4,3,2,1,0:T(8,128)(2,1)} %bitcast.45, bf16[2,2,128,11,128]{4,2,1,3,0:T(8,128)(2,1)S(1)} %bitcast.51, pred[2,2,11]{2,1,0:T(4,128)(4,1)S(1)} %iota_compare_fusion.2), kind=kOutput, calls=%fused_computation.8 | convolution fusion | flops 1477640192 | bytes 14024748 | tf_op jit(solution)/shard_map/kbrsi,kbsic->kbrc/dot_general | solution.py:53
  180.7 0.3 copy.46
  180.9 0.2 copy.39
  181.1 3.1 gather_fusion.1
  184.2 7.8 %all-to-all-start = ((bf16[2,256,16,2,128]{4,1,0,3,2:T(8,128)(2,1)}), bf16[2,256,16,2,128]{4,1,0,3,2:T(8,128)(2,1)}, u32[]{:S(2)}, u32[]{:S(2)}) async-start(bf16[2,256,16,2,128]{4,1,0,3,2:T(8,128)(2,1)} %bitcast.47), calls=%async_computation | async-start | bytes 8388608 | tf_op jit(solution)/shard_map/all_to_all | solution.py:57
  192.1 0.1 copy.42
  192.3 1.7 gather_fusion.2
  194.3 91.2 %all-to-all-done = bf16[2,256,16,2,128]{4,1,0,3,2:T(8,128)(2,1)} async-done(((bf16[2,256,16,2,128]{4,1,0,3,2:T(8,128)(2,1)}), bf16[2,256,16,2,128]{4,1,0,3,2:T(8,128)(2,1)}, u32[]{:S(2)}, u32[]{:S(2)}) %all-to-all-start) | async-done | bytes 4194336 | tf_op jit(solution)/shard_map/all_to_all | solution.py:57
  285.6 4.7 %copy.40 = bf16[2,256,16,2,128]{4,1,3,2,0:T(8,128)(2,1)} copy(bf16[2,256,16,2,128]{4,1,0,3,2:T(8,128)(2,1)} %all-to-all-done) | data formatting | bytes 8388608 | tf_op jit(solution)/shard_map/all_to_all | solution.py:57
  290.3 12.3 %gather_fusion.3 = bf16[176,256,128]{2,1,0:T(8,128)(2,1)} fusion(bf16[2,256,32,128]{3,1,2,0:T(8,128)(2,1)} %bitcast.44, s32[176]{0:T(256)S(1)} %reshape.99), kind=kCustom, calls=%fused_computation.3 | custom fusion | bytes 23070080 | tf_op jit(solution)/shard_map/vmap()/gather | solution.py:29
  302.6 9.8 %fusion = f32[8,128,256,1,1]{2,1,4,0,3:T(8,128)S(1)} fusion(bf16[2,256,8,11,128]{4,1,3,2,0:T(8,128)(2,1)} %bitcast.46, bf16[2,8,128,11,128]{4,2,1,3,0:T(8,128)(2,1)} %bitcast.54, pred[2,8,11]{2,1,0:T(8,128)(4,1)S(1)} %iota_compare_fusion.1), kind=kOutput, calls=%fused_computation.5 | convolution fusion | flops 1479278592 | bytes 18350256 | tf_op jit(solution)/shard_map/kabsj,kbrsj->abr/dot_general | solution.py:69
  312.5 1.3 copy.43
  (27 shorter events, 1.3 us)
Async XLA Ops:
  6.5 187.6 %copy-start = (s32[2,128]{1,0:T(2,128)S(1)}, s32[2,128]{1,0:T(2,128)}, u32[]{:S(2)}) copy-start(s32[2,128]{1,0:T(2,128)} %param.13) | copy-start | bytes 3076
  6.5 155.9 %all-gather.2.cloned.1.call-start = ((), (), s32[]{:S(2)}) async-start(), calls=%async_computation.1 | async-start | bytes 17301504 | tf_op jit(solution)/shard_map/all_gather | solution.py:51
  162.4 12.0 %copy-start.1 = (bf16[2,256,11,128]{3,1,2,0:T(8,128)(2,1)S(1)}, bf16[2,256,11,128]{3,1,2,0:T(8,128)(2,1)}, u32[]{:S(2)}) copy-start(bf16[2,256,11,128]{3,1,2,0:T(8,128)(2,1)} %param.8) | copy-start | bytes 4325380
  184.2 101.4 %all-to-all-start = ((bf16[2,256,16,2,128]{4,1,0,3,2:T(8,128)(2,1)}), bf16[2,256,16,2,128]{4,1,0,3,2:T(8,128)(2,1)}, u32[]{:S(2)}, u32[]{:S(2)}) async-start(bf16[2,256,16,2,128]{4,1,0,3,2:T(8,128)(2,1)} %bitcast.47), calls=%async_computation | async-start | bytes 8388608 | tf_op jit(solution)/shard_map/all_to_all | solution.py:57
Sparse Core Ops, SparseCore 0:
  10.5 151.8 all-gather.1
where the time goes:
time: 321 us
  waiting for transfers between devices  243 us (76%)
  local copies, waits for them, and re-layouts  38.6 us (12%)
  matrix products  16 us (5%)
  between operations  13.5 us (4%)
  starting transfers between devices  7.79 us (2%)
    all_gather x1, waiting for transfers between devices, on_device(): gathered = lax.all_gather(coeffs, 'alpha', axis=0, tiled=True)  151 us
    all_to_all x1, waiting for transfers between devices, on_device(): lax.all_to_all(outgoing_cols, 'beta', split_axis=2, concat_axis=2, tiled=...  91.2 us
    gather x2, local copies, waits for them, and re-layouts, pick_columns(): return pool_piece[:, index_piece]  12.4 us
    gather x1, local copies, waits for them, and re-layouts, on_device(): gathered.reshape(alpha_size * row_blocks, block_size, local_cols)  12 us
    dot_general x1, matrix products, on_device(): jnp.einsum('kabsj,kbrsj->abr', picked, beta_kept, preferred_element_type=...  9.82 us
    all_to_all x1, starting transfers between devices, on_device(): lax.all_to_all(outgoing_cols, 'beta', split_axis=2, concat_axis=2, tiled=...  7.79 us
  transfers between devices with their start and end apart: 2, of which 2 were waited for; matrix products, arithmetic and copies ran while one was open for 2% of the time, Pallas kernels for 0%

commit v1 on v0

v1 whole, which is shorter than its diff:
```python
import functools

import jax
import jax.numpy as jnp
from jax import lax
from jax.experimental import pallas as pl
from jax.experimental.pallas import tpu as pltpu
from jax.sharding import PartitionSpec as P

X, Z = 4, 8
Y, CORES = 8, 2
NBETA = Y * CORES
BLK = 128
FROM_B = 2
VMEM_LIMIT = 40 * 1024 * 1024

Z_GROUPS = [[x * Z + z for z in range(Z)] for x in range(X)]
X_GROUPS = [[x * Z + z for x in range(X)] for z in range(Z)]


def shift_x(step):
    return [(x * Z + z, (x + step) % X * Z + z) for x in range(X) for z in range(Z)]


SWAP_CORES = [(y * CORES + c, y * CORES + 1 - c) for y in range(Y) for c in range(CORES)]


def params():
    return pltpu.CompilerParams(vmem_limit_bytes=VMEM_LIMIT)


def pack_kernel(wanted, c_ref, out_ref, sems):
    def each(action):
        for t in range(NBETA * FROM_B):
            column = pl.multiple_of(wanted[t] * BLK, BLK)
            copy = pltpu.make_async_copy(
                c_ref.at[:, pl.ds(column, BLK)], out_ref.at[t], sems.at[t]
            )
            action(copy)

    each(lambda copy: copy.start())
    each(lambda copy: copy.wait())


def pack(wanted, c):
    rows = c.shape[0]
    total = NBETA * FROM_B
    return pl.pallas_call(
        pack_kernel,
        grid_spec=pltpu.PrefetchScalarGridSpec(
            num_scalar_prefetch=1,
            grid=(1,),
            in_specs=[pl.BlockSpec(c.shape, lambda i, w: (0, 0))],
            out_specs=pl.BlockSpec(memory_space=pl.ANY),
            scratch_shapes=[pltpu.SemaphoreType.DMA((total,))],
        ),
        out_shape=jax.ShapeDtypeStruct((total, rows, BLK), c.dtype),
        compiler_params=params(),
        cost_estimate=pl.CostEstimate(flops=0, bytes_accessed=5 << 20, transcendentals=0),
        name="pack",
    )(wanted, c)


def sum_pack_kernel(wanted, parts_ref, out_ref, inter, sems):
    for b in range(inter.shape[0]):
        columns = slice(b * BLK, (b + 1) * BLK)
        total = parts_ref[0, :, columns].astype(jnp.float32)
        for x in range(1, X):
            total += parts_ref[x, :, columns].astype(jnp.float32)
        inter[b] = total.astype(inter.dtype)

    def each(action):
        for t in range(NBETA * FROM_B):
            action(pltpu.make_async_copy(inter.at[wanted[t]], out_ref.at[t], sems.at[t]))

    each(lambda copy: copy.start())
    each(lambda copy: copy.wait())


def sum_pack(wanted, parts):
    _, rows, cols = parts.shape
    total = NBETA * FROM_B
    return pl.pallas_call(
        sum_pack_kernel,
        grid_spec=pltpu.PrefetchScalarGridSpec(
            num_scalar_prefetch=1,
            grid=(1,),
            in_specs=[pl.BlockSpec(parts.shape, lambda i, w: (0, 0, 0))],
            out_specs=pl.BlockSpec(memory_space=pl.ANY),
            scratch_shapes=[
                pltpu.VMEM((cols // BLK, rows, BLK), jnp.bfloat16),
                pltpu.SemaphoreType.DMA((total,)),
            ],
        ),
        out_shape=jax.ShapeDtypeStruct((total, rows, BLK), jnp.bfloat16),
        compiler_params=params(),
        cost_estimate=pl.CostEstimate(flops=1 << 20, bytes_accessed=6 << 20, transcendentals=0),
        name="sum_pack",
    )(wanted, parts)


def beta_kernel(op, slots, place, pool_ref, b_ref, *rest):
    out_ref = rest[-1]
    block = pl.program_id(0)
    picked = [pool_ref[place[op, block, s]] for s in range(slots)]
    total = lax.dot_general(
        jnp.concatenate(picked, axis=1),
        b_ref[...],
        (((1,), (1,)), ((), ())),
        preferred_element_type=jnp.float32,
    )
    if len(rest) == 2:
        total += rest[0][...]
    out_ref[...] = total.astype(out_ref.dtype)


def beta_product(op, place, pool, b_flat, added, dtype):
    _, cols, depth = b_flat.shape
    rows = pool.shape[1]
    in_specs = [
        pl.BlockSpec(pool.shape, lambda i, p: (0, 0, 0)),
        pl.BlockSpec((None, BLK, depth), lambda i, p: (op, i, 0)),
    ]
    operands = [pool, b_flat]
    if added is not None:
        in_specs.append(pl.BlockSpec((rows, BLK), lambda i, p: (0, i)))
        operands.append(added)
    return pl.pallas_call(
        functools.partial(beta_kernel, op, depth // BLK),
        grid_spec=pltpu.PrefetchScalarGridSpec(
            num_scalar_prefetch=1,
            grid=(cols // BLK,),
            in_specs=in_specs,
            out_specs=pl.BlockSpec((rows, BLK), lambda i, p: (0, i)),
        ),
        out_shape=jax.ShapeDtypeStruct((rows, cols), dtype),
        compiler_params=params(),
        cost_estimate=pl.CostEstimate(
            flops=2 * rows * cols * depth, bytes_accessed=7 << 20, transcendentals=0
        ),
        name="beta_product",
    )(place, *operands)


def alpha_kernel(op, slots, block, core, place, pool_ref, own, near, far, *rest):
    out_ref, factors, total, sems = rest
    step = pl.program_id(0)

    def copy_of(source, t):
        return pltpu.make_async_copy(source, factors.at[t], sems.at[t])

    @pl.when(step == 0)
    def _():
        copy_of(own.at[op], 0).start()

        @pl.when(core[0] == op)
        def _():
            for t in range(1, X):
                copy_of(near.at[t - 1], t).start()

        @pl.when(core[0] != op)
        def _():
            for t in range(1, X):
                copy_of(far.at[t - 1], t).start()

    copy_of(own.at[op], step).wait()
    for b in range(block):
        rows = slice(b * BLK, (b + 1) * BLK)
        total[...] = jnp.zeros_like(total)
        for s in range(slots):
            chosen = place[op, step, b, s]

            @pl.when(chosen >= 0)
            def _():
                total[...] += jnp.dot(
                    factors[step, rows, s * BLK : (s + 1) * BLK],
                    pool_ref[chosen],
                    preferred_element_type=jnp.float32,
                )

        out_ref[rows, :] = total[...].astype(out_ref.dtype)


def alpha_partials(op, core, target, place, gathered, own, near, far, dtype):
    _, rows, depth = own.shape
    cols = gathered.shape[1]
    pool = gathered.reshape(gathered.shape[0] // BLK, BLK, cols)
    anywhere = pl.BlockSpec(memory_space=pl.ANY)
    return pl.pallas_call(
        functools.partial(alpha_kernel_entry, op, depth // BLK, rows // BLK),
        grid_spec=pltpu.PrefetchScalarGridSpec(
            num_scalar_prefetch=3,
            grid=(X,),
            in_specs=[
                pl.BlockSpec(pool.shape, lambda i, c, t, p: (0, 0, 0)),
                anywhere,
                anywhere,
                anywhere,
            ],
            out_specs=pl.BlockSpec((None, rows, cols), lambda i, c, t, p: (t[i], 0, 0)),
            scratch_shapes=[
                pltpu.VMEM((X, rows, depth), own.dtype),
                pltpu.VMEM((BLK, cols), jnp.float32),
                pltpu.SemaphoreType.DMA((X,)),
            ],
        ),
        out_shape=jax.ShapeDtypeStruct((X, rows, cols), dtype),
        compiler_params=params(),
        cost_estimate=pl.CostEstimate(
            flops=2 * rows * cols * depth, bytes_accessed=9 << 20, transcendentals=0
        ),
        name="alpha_partials",
    )(core, target, place, pool, own, near, far)


def alpha_kernel_entry(op, slots, block, core, target, place, *refs):
    alpha_kernel(op, slots, block, core, place, *refs)


def on_device(coeffs, a_blocks, a_list, a_count, b_blocks, b_list, b_count):
    operators, local_rows, slots, _ = a_blocks.shape
    local_cols = coeffs.shape[1]
    row_blocks = local_rows // BLK
    col_blocks = local_cols // BLK
    alpha_here = lax.axis_index("alpha")
    beta_here = lax.axis_index("beta")
    x_here = alpha_here // Z
    z_here = alpha_here % Z
    core_here = beta_here % CORES
    slot_ids = jnp.arange(slots, dtype=jnp.int32)

    local = b_list.reshape(operators, NBETA, col_blocks * slots) - beta_here * col_blocks
    inside = (local >= 0) & (local < col_blocks)
    lowest = jnp.min(jnp.where(inside, local, col_blocks - 1), axis=(0, 2))
    highest = jnp.max(jnp.where(inside, local, 0), axis=(0, 2))
    wanted = jnp.stack([lowest, highest], axis=1).reshape(NBETA * FROM_B)

    mine = lax.dynamic_slice_in_dim(b_list, beta_here * col_blocks, col_blocks, 1)
    owner = mine // col_blocks
    local_id = mine % col_blocks
    is_owner = owner[..., None] == jnp.arange(NBETA, dtype=jnp.int32)
    first = jnp.min(jnp.where(is_owner, local_id[..., None], col_blocks - 1), axis=(0, 1, 2))
    first_here = jnp.sum(jnp.where(is_owner, first, 0), axis=-1)
    beta_place = owner * FROM_B + (local_id != first_here).astype(jnp.int32)

    order = (x_here - jnp.arange(X, dtype=jnp.int32)) % X
    lists = a_list.reshape(operators, X, Z, row_blocks, slots)
    lists = lax.dynamic_index_in_dim(lists, z_here, 2, keepdims=False)
    counts = a_count.reshape(operators, X, Z, row_blocks)
    counts = lax.dynamic_index_in_dim(counts, z_here, 2, keepdims=False)
    per_x = Z * row_blocks
    here = (slot_ids < counts[..., None]) & (lists // per_x == x_here)
    by_x = jnp.where(here, lists % per_x, -1)
    pick = order[:, None] == jnp.arange(X, dtype=jnp.int32)
    alpha_place = jnp.sum(
        jnp.where(pick[None, :, :, None, None], by_x[:, None], 0), axis=2
    )

    a_flat = a_blocks.reshape(operators, local_rows, slots * BLK)
    a_half = lax.dynamic_index_in_dim(a_flat, core_here, 0, keepdims=False)
    near = [lax.ppermute(a_half, "alpha", shift_x(d)) for d in range(1, X)]
    near = jnp.stack(near)
    far = lax.ppermute(near, "beta", SWAP_CORES)
    beta_counts = lax.dynamic_slice_in_dim(b_count, beta_here * col_blocks, col_blocks, 1)
    beta_valid = slot_ids < beta_counts[..., None]
    b_flat = jnp.where(
        beta_valid[:, :, None, :, None],
        b_blocks.reshape(operators, col_blocks, BLK, slots, BLK),
        jnp.zeros((), b_blocks.dtype),
    ).reshape(operators, local_cols, slots * BLK)

    core = core_here.reshape(1)

    sent = pack(wanted, coeffs)
    pool_c = lax.all_to_all(sent, "beta", split_axis=0, concat_axis=0, tiled=True)
    d_one = beta_product(1, beta_place, pool_c, b_flat, None, jnp.bfloat16)

    c_along_z = lax.all_gather(coeffs, "alpha", axis=0, tiled=True, axis_index_groups=Z_GROUPS)
    inter_parts = alpha_partials(
        0, core, order, alpha_place, c_along_z, a_flat, near, far, jnp.bfloat16
    )
    inter_parts = lax.all_to_all(
        inter_parts, "alpha", split_axis=0, concat_axis=0, tiled=True, axis_index_groups=X_GROUPS
    )
    sent = sum_pack(wanted, inter_parts)
    pool_inter = lax.all_to_all(sent, "beta", split_axis=0, concat_axis=0, tiled=True)

    d_along_z = lax.all_gather(d_one, "alpha", axis=0, tiled=True, axis_index_groups=Z_GROUPS)
    sigma_parts = alpha_partials(
        1, core, order, alpha_place, d_along_z, a_flat, near, far, jnp.float32
    )
    sigma_one = lax.psum_scatter(
        sigma_parts.reshape(X * local_rows, local_cols),
        "alpha",
        scatter_dimension=0,
        tiled=True,
        axis_index_groups=X_GROUPS,
    )
    return beta_product(0, beta_place, pool_inter, b_flat, sigma_one, jnp.float32)


def solution(mesh):
    in_specs = (
        P("alpha", "beta"),
        P(None, "alpha", None, None),
        P(),
        P(),
        P(None, "beta", None, None),
        P(),
        P(),
    )
    return jax.shard_map(
        on_device, mesh=mesh, in_specs=in_specs, out_specs=P("alpha", "beta"), check_vma=False
    )
```

time: 321 us -> 337 us (1.050)
  waiting for transfers between devices: 243 us -> 95.9 us
  blocking collectives: 0 us -> 111 us
  Pallas kernels: 0 us -> 26.5 us
  local copies, waits for them, and re-layouts: 38.6 us -> 58.1 us
  matrix products: 16 us -> 0 us
  starting transfers between devices: 7.79 us -> 21.4 us
  other arithmetic: 1.78 us -> 9.16 us
    all_to_all x0 -> x2, blocking collectives: none -> 111 us  [the longest x1 62.9 us: on_device(): lax.all_to_all(sent, 'beta', split_axis=0, concat_axis=0, tiled=True)]
    all_gather x1 -> x2, waiting for transfers between devices: 151 us -> 60.1 us  [the longest x1 47.4 us: on_device(): lax.all_gather(coeffs, 'alpha', axis=0, tiled=True, axis_index_groups=Z_G...]
    all_to_all x1, waiting for transfers between devices: 91.2 us -> 5.48 us  [on_device(): lax.all_to_all(sent, 'beta', split_axis=0, concat_axis=0, tiled=True)]
    ppermute x0 -> x4, waiting for transfers between devices: none -> 29.5 us  [the longest x3 28.9 us: on_device(): near = [lax.ppermute(a_half, 'alpha', shift_x(d)) for d in range(1, X)]]
    gather x6 -> x0, local copies, waits for them, and re-layouts: 29.3 us -> none  [the longest x2 12.4 us: pick_columns(): return pool_piece[:, index_piece]]
    pallas_call x0 -> x6, Pallas kernels: none -> 26.5 us  [the longest x2 10.6 us: alpha_partials(): pl.pallas_call(functools.partial(alpha_kernel_entry, op, depth // BLK, ro...]
    unnamed x6 -> x38, local copies, waits for them, and re-layouts: 1.09 us -> 27.2 us
    broadcast_in_dim x1 -> x3, local copies, waits for them, and re-layouts: 0.09 us -> 18.6 us  [on_device(): jnp.where(beta_valid[:, :, None, :, None], b_blocks.reshape(operators, co...]
  transfers between devices with their start and end apart: 2 -> 8, of which waited for: 2 -> 7; matrix products, arithmetic and copies ran while one was open for 2% -> 14% of each run, Pallas kernels for 0% -> 4%
where the time goes in v1:
time: 337 us; the launch traced here: 336 us
  blocking collectives  111 us (33%)
  waiting for transfers between devices  95.9 us (28%)
  local copies, waits for them, and re-layouts  58.1 us (17%)
  Pallas kernels  26.5 us (8%)
  starting transfers between devices  21.4 us (6%)
  between operations  13.4 us (4%)
  other arithmetic  9.16 us (3%)
    all_to_all x1, blocking collectives, on_device(): lax.all_to_all(sent, 'beta', split_axis=0, concat_axis=0, tiled=True)  62.9 us
    all_to_all x1, blocking collectives, on_device(): lax.all_to_all(inter_parts, 'alpha', split_axis=0, concat_axis=0, tiled=T...  48.3 us
    all_gather x1, waiting for transfers between devices, on_device(): lax.all_gather(coeffs, 'alpha', axis=0, tiled=True, axis_index_groups=Z_G...  47.4 us
    ppermute x3, waiting for transfers between devices, on_device(): near = [lax.ppermute(a_half, 'alpha', shift_x(d)) for d in range(1, X)]  28.9 us
    unnamed x38, local copies, waits for them, and re-layouts  27.2 us
    broadcast_in_dim x3, local copies, waits for them, and re-layouts, on_device(): jnp.where(beta_valid[:, :, None, :, None], b_blocks.reshape(operators, co...  18.6 us
    all_gather x1, waiting for transfers between devices, on_device(): lax.all_gather(d_one, 'alpha', axis=0, tiled=True, axis_index_groups=Z_GR...  12.8 us
    pallas_call x2, Pallas kernels, alpha_partials(): pl.pallas_call(functools.partial(alpha_kernel_entry, op, depth // BLK, ro...  10.6 us
  transfers between devices with their start and end apart: 8, of which 7 were waited for; matrix products, arithmetic and copies ran while one was open for 14% of the time, Pallas kernels for 4%

profile of v1, /device:TPU:1, one launch (start us, length us, event | category | flops | bytes accessed | tf_op | source)
XLA Modules:
  0.0 335.6 jit_solution(4400437848700892688)
XLA Ops:
  11.9 10.5 %all-to-all-start.2 = ((bf16[32,256,128]{2,1,0:T(8,128)(2,1)}), bf16[32,256,128]{2,1,0:T(8,128)(2,1)S(1)}, u32[]{:S(2)}, u32[]{:S(2)}) async-start(bf16[32,256,128]{2,1,0:T(8,128)(2,1)} %copy-done.7), calls=%async_computation.2 | async-start | bytes 4194304 | tf_op jit(solution)/shard_map/all_to_all | solution.py:275
  26.1 8.6 %broadcast_in_dim.82 = pred[2,1024,1408]{1,2,0:T(8,128)(4,1)} reshape(pred[2,8,128,11,128]{2,1,4,3,0:T(8,128)(4,1)} %broadcast_in_dim.81) | data formatting | bytes 5767168 | tf_op jit(solution)/shard_map/jit(_where)/broadcast_in_dim | solution.py:266
  34.7 7.5 %copy.47 = pred[2,1024,1408]{2,1,0:T(8,128)(4,1)} copy(pred[2,1024,1408]{1,2,0:T(8,128)(4,1)} %broadcast_in_dim.82) | data formatting | bytes 5767168 | tf_op jit(solution)/shard_map/jit(_where)/broadcast_in_dim | solution.py:266
  42.2 8.3 %copy.46 = bf16[2,1024,11,128]{1,3,2,0:T(8,128)(2,1)} copy(bf16[2,1024,11,128]{3,1,2,0:T(8,128)(2,1)} %param.11) | data formatting | bytes 11534336 | tf_op args[4]
  50.6 8.4 %copy.48 = bf16[2,1024,1408]{2,1,0:T(8,128)(2,1)} copy(bf16[2,1024,1408]{1,2,0:T(8,128)(2,1)} %bitcast.29) | data formatting | bytes 11534336 | tf_op jit(solution)/shard_map/reshape | solution.py:268
  59.0 6.9 %broadcast_select_fusion.b_ref = bf16[2,1024,1408]{2,1,0:T(8,128)(2,1)} fusion(pred[2,1024,1408]{2,1,0:T(8,128)(4,1)} %copy.47, bf16[2,1024,1408]{2,1,0:T(8,128)(2,1)} %copy.48), kind=kLoop, calls=%fused_computation | loop fusion | flops 2883584 | bytes 14417920 | tf_op jit(solution)/shard_map/jit(_where)/select_n | solution.py:266
  65.9 5.5 %all-to-all-done.2.pool_ref = bf16[32,256,128]{2,1,0:T(8,128)(2,1)S(1)} async-done(((bf16[32,256,128]{2,1,0:T(8,128)(2,1)}), bf16[32,256,128]{2,1,0:T(8,128)(2,1)S(1)}, u32[]{:S(2)}, u32[]{:S(2)}) %all-to-all-start.2) | async-done | bytes 2097184 | tf_op jit(solution)/shard_map/all_to_all | solution.py:275
  71.4 2.6 copy-done.2
  74.0 5.0 %beta_product.2 = bf16[256,1024]{1,0:T(8,128)(2,1)} custom-call(s32[2,8,11]{2,1,0:T(8,128)S(1)} %convert_add_fusion.place, bf16[32,256,128]{2,1,0:T(8,128)(2,1)S(1)} %all-to-all-done.2.pool_ref, bf16[2,1024,1408]{2,1,0:T(8,128)(2,1)S(1)} %copy-done.2), custom_call_target="tpu_custom_call" | custom-call | flops 738197504 | bytes 7340032 | tf_op jit(solution)/shard_map/beta_product/pallas_call | solution.py:128
  81.0 2.9 collective-permute-start.1
  83.9 2.8 collective-permute-start.2
  89.2 12.6 %collective-permute-done.1 = bf16[256,1408]{1,0:T(8,128)(2,1)S(1)} collective-permute-done((bf16[256,1408]{1,0:T(8,128)(2,1)S(1)}, bf16[256,1408]{1,0:T(8,128)(2,1)S(1)}, u32[]{:S(2)}, u32[]{:S(2)}) %collective-permute-start.1) | collective-permute-done | bytes 720928 | tf_op jit(solution)/shard_map/ppermute | solution.py:261
  101.8 13.9 %collective-permute-done.2 = bf16[256,1408]{1,0:T(8,128)(2,1)S(1)} collective-permute-done((bf16[256,1408]{1,0:T(8,128)(2,1)S(1)}, bf16[256,1408]{1,0:T(8,128)(2,1)S(1)}, u32[]{:S(2)}, u32[]{:S(2)}) %collective-permute-start.2) | collective-permute-done | bytes 720928 | tf_op jit(solution)/shard_map/ppermute | solution.py:261
  118.4 2.6 collective-permute-start.3
  121.0 2.6 copy.45.refs_1_
  124.8 12.8 %all-gather.5.cloned.1.call-done = bf16[2048,1024]{1,0:T(8,128)(2,1)} async-done(((bf16[256,1024]{1,0:T(8,128)(2,1)}), bf16[2048,1024]{1,0:T(8,128)(2,1)}) %all-gather.5.cloned.1.call-update) | async-done | bytes 4194320 | tf_op jit(solution)/shard_map/all_gather | solution.py:288
  141.1 5.5 %alpha_partials.3 = f32[4,256,1024]{2,1,0:T(8,128)S(1)} custom-call(s32[1]{0:T(128)} %bitcast.2.core, s32[4]{0:T(128)S(1)} %and_select_fusion.3.target, s32[2,4,2,11]{3,2,1,0:T(2,128)S(1)} %select_reduce_fusion.2.place, bf16[16,128,1024]{2,1,0:T(8,128)(2,1)S(1)} %bitcast.27, bf16[2,256,1408]{2,1,0:T(8,128)(2,1)S(1)} %copy-done.5, ...), custom_call_target="tpu_custom_call" | custom-call | flops 738197504 | bytes 9437184 | tf_op jit(solution)/shard_map/alpha_partials/pallas_call | solution.py:189
  148.6 47.4 %all-gather.3.cloned.1.call-done = bf16[2048,1024]{1,0:T(8,128)(2,1)} async-done(((bf16[256,1024]{1,0:T(8,128)(2,1)}), bf16[2048,1024]{1,0:T(8,128)(2,1)}) %all-gather.3.cloned.1.call-update) | async-done | bytes 4194320 | tf_op jit(solution)/shard_map/all_gather | solution.py:278
  199.5 5.1 %alpha_partials.2 = bf16[4,256,1024]{2,1,0:T(8,128)(2,1)S(1)} custom-call(s32[1]{0:T(128)} %bitcast.2.core, s32[4]{0:T(128)S(1)} %and_select_fusion.3.target, s32[2,4,2,11]{3,2,1,0:T(2,128)S(1)} %select_reduce_fusion.2.place, bf16[16,128,1024]{2,1,0:T(8,128)(2,1)S(1)} %bitcast.28, bf16[2,256,1408]{2,1,0:T(8,128)(2,1)S(1)} %copy-done.6, ...), custom_call_target="tpu_custom_call" | custom-call | flops 738197504 | bytes 9437184 | tf_op jit(solution)/shard_map/alpha_partials/pallas_call | solution.py:189
  204.7 48.3 %all_to_all.15.parts_ref = bf16[4,256,1024]{2,1,0:T(8,128)(2,1)S(1)} all-to-all(bf16[4,256,1024]{2,1,0:T(8,128)(2,1)S(1)} %alpha_partials.2), channel_id=1, replica_groups={{0,128,256,384},{16,144,272,400},{32,160,288,416},{48,176,304,432},{64,..., dimensions={0} | all-to-all | bytes 4194304 | tf_op jit(solution)/shard_map/all_to_all | solution.py:282
  253.0 4.0 %sum_pack.1 = bf16[32,256,128]{2,1,0:T(8,128)(2,1)S(1)} custom-call(s32[32]{0:T(128)S(1)} %reshape.132.wanted, bf16[4,256,1024]{2,1,0:T(8,128)(2,1)S(1)} %all_to_all.15.parts_ref), custom_call_target="tpu_custom_call" | custom-call | flops 1048576 | bytes 6291456 | tf_op jit(solution)/shard_map/sum_pack/pallas_call | solution.py:83
  257.0 62.9 %all_to_all.16.pool_ref = bf16[32,256,128]{2,1,0:T(8,128)(2,1)S(1)} all-to-all(bf16[32,256,128]{2,1,0:T(8,128)(2,1)S(1)} %sum_pack.1), channel_id=1, replica_groups=mesh['alpha'=32,'beta'=16] {'beta'}, dimensions={0} | all-to-all | bytes 4194304 | tf_op jit(solution)/shard_map/all_to_all | solution.py:286
  320.0 2.6 copy-done.3
  323.8 5.3 %beta_product.3 = f32[256,1024]{1,0:T(8,128)} custom-call(s32[2,8,11]{2,1,0:T(8,128)S(1)} %convert_add_fusion.place, bf16[32,256,128]{2,1,0:T(8,128)(2,1)S(1)} %all_to_all.16.pool_ref, bf16[2,1024,1408]{2,1,0:T(8,128)(2,1)S(1)} %copy-done.3, f32[256,1024]{1,0:T(8,128)S(1)} %copy-done.11), custom_call_target="tpu_custom_call" | custom-call | flops 738197504 | bytes 7340032 | tf_op jit(solution)/shard_map/beta_product/pallas_call | solution.py:128
  (75 shorter events, 27.5 us)
Async XLA Ops:
  6.5 17.0 %copy-start = (s32[2,128]{1,0:T(2,128)S(1)}, s32[2,128]{1,0:T(2,128)}, u32[]{:S(2)}) copy-start(s32[2,128]{1,0:T(2,128)} %param.13) | copy-start | bytes 3076
  10.5 1.3 copy-start.7
  11.9 10.6 %copy-start.14 = (s32[2,128,11]{1,0,2:T(2,128)S(1)}, s32[2,128,11]{1,0,2:T(2,128)}, u32[]{:S(2)}) copy-start(s32[2,128,11]{1,0,2:T(2,128)} %param.12) | copy-start | bytes 33796
  11.9 59.5 %all-to-all-start.2 = ((bf16[32,256,128]{2,1,0:T(8,128)(2,1)}), bf16[32,256,128]{2,1,0:T(8,128)(2,1)S(1)}, u32[]{:S(2)}, u32[]{:S(2)}) async-start(bf16[32,256,128]{2,1,0:T(8,128)(2,1)} %copy-done.7), calls=%async_computation.2 | async-start | bytes 4194304 | tf_op jit(solution)/shard_map/all_to_all | solution.py:275
  22.4 115.2 %all-gather.5.cloned.1.call-start = ((), (), s32[]{:S(2)}) async-start(), calls=%async_computation.5 | async-start | bytes 4718592 | tf_op jit(solution)/shard_map/all_gather | solution.py:288
  71.4 2.6 copy-start.2
  74.0 5.9 %copy-start.13 = (bf16[2,256,11,128]{3,1,2,0:T(8,128)(2,1)S(1)}, bf16[2,256,11,128]{3,1,2,0:T(8,128)(2,1)}, u32[]{:S(2)}) copy-start(bf16[2,256,11,128]{3,1,2,0:T(8,128)(2,1)} %param.8) | copy-start | bytes 4325380
  79.1 116.9 %all-gather.3.cloned.1.call-start = ((), (), s32[]{:S(2)}) async-start(), calls=%async_computation.4 | async-start | bytes 4718592 | tf_op jit(solution)/shard_map/all_gather | solution.py:278
  79.9 240.1 %reduce-scatter.2.cloned.1.call-start = ((), (), s32[]{:S(2)}) async-start(), calls=%async_computation.6 | async-start | bytes 5242880 | tf_op jit(solution)/shard_map/reduce_scatter | solution.py:292
  80.6 37.4 %copy-start.12 = (bf16[2,256,11,128]{1,3,2,0:T(8,128)(2,1)}, bf16[2,256,11,128]{1,3,2,0:T(8,128)(2,1)S(1)}, u32[]{:S(2)}) copy-start(bf16[2,256,11,128]{1,3,2,0:T(8,128)(2,1)S(1)} %copy.43) | copy-start | bytes 4325380
  81.0 20.8 %collective-permute-start.1 = (bf16[256,1408]{1,0:T(8,128)(2,1)S(1)}, bf16[256,1408]{1,0:T(8,128)(2,1)S(1)}, u32[]{:S(2)}, u32[]{:S(2)}) collective-permute-start(bf16[256,1408]{1,0:T(8,128)(2,1)S(1)} %bitcast.32), channel_id=1, source_target_pairs={{0,256},{16,272},{32,288},{48,304},{64,320},{80,336},{96,352},{112... | collective-permute-start | bytes 2162696 | tf_op jit(solution)/shard_map/ppermute | solution.py:261
  83.9 31.8 %collective-permute-start.2 = (bf16[256,1408]{1,0:T(8,128)(2,1)S(1)}, bf16[256,1408]{1,0:T(8,128)(2,1)S(1)}, u32[]{:S(2)}, u32[]{:S(2)}) collective-permute-start(bf16[256,1408]{1,0:T(8,128)(2,1)S(1)} %bitcast.33), channel_id=1, source_target_pairs={{0,384},{16,400},{32,416},{48,432},{64,448},{80,464},{96,480},{112... | collective-permute-start | bytes 2162696 | tf_op jit(solution)/shard_map/ppermute | solution.py:261
  86.7 31.4 %collective-permute-start = (bf16[256,1408]{1,0:T(8,128)(2,1)S(1)}, bf16[256,1408]{1,0:T(8,128)(2,1)S(1)}, u32[]{:S(2)}, u32[]{:S(2)}) collective-permute-start(bf16[256,1408]{1,0:T(8,128)(2,1)S(1)} %bitcast.34), channel_id=1, source_target_pairs={{0,128},{16,144},{32,160},{48,176},{64,192},{80,208},{96,224},{112... | collective-permute-start | bytes 2162696 | tf_op jit(solution)/shard_map/ppermute | solution.py:261
  118.3 5.2 %copy-start.16 = (s32[2,64]{1,0:T(2,128)S(1)}, s32[2,64]{1,0:T(2,128)}, u32[]{:S(2)}) copy-start(s32[2,64]{1,0:T(2,128)} %param.10) | copy-start | bytes 1540
  118.3 5.3 %copy-start.15 = (s32[2,64,11]{1,0,2:T(2,128)S(1)}, s32[2,64,11]{1,0,2:T(2,128)}, u32[]{:S(2)}) copy-start(s32[2,64,11]{1,0,2:T(2,128)} %param.9) | copy-start | bytes 16900
  118.4 6.4 %collective-permute-start.3 = (bf16[3,256,1408]{2,1,0:T(8,128)(2,1)S(1)}, bf16[3,256,1408]{2,1,0:T(8,128)(2,1)}, u32[]{:S(2)}, u32[]{:S(2)}) collective-permute-start(bf16[3,256,1408]{2,1,0:T(8,128)(2,1)S(1)} %pad_maximum_fusion.refs_2_), channel_id=1, source_target_pairs={{0,1},{1,0},{2,3},{3,2},{4,5},{5,4},{6,7},{7,6},{8,9},{9,8},{10,11... | collective-permute-start | bytes 6488072 | tf_op jit(solution)/shard_map/ppermute | solution.py:263
  137.6 1.4 copy-start.5
  138.9 2.2 copy-start.8
  146.6 2.0 copy-start.4
  196.0 1.4 copy-start.6
  197.4 2.2 copy-start.9
  320.0 2.6 copy-start.3
  322.6 1.2 copy-start.11
  323.8 5.3 %copy-start.1 = (s32[2,128]{1,0:T(2,128)S(1)}, s32[2,128]{1,0:T(2,128)}, u32[]{:S(2)}) copy-start(s32[2,128]{1,0:T(2,128)} %param.13) | copy-start | bytes 3076
  (1 other events, 1.0 us)
Sparse Core Ops, SparseCore 0:
  79.2 58.2 all-gather.4
  139.6 56.3 all-gather.2
  198.8 71.3 reduce-scatter.1

commit v2 on v1

v2 whole, which is shorter than its diff:
```python
import functools

import jax
import jax.numpy as jnp
from jax import lax
from jax.experimental import pallas as pl
from jax.experimental.pallas import tpu as pltpu
from jax.sharding import PartitionSpec as P

X, Z = 4, 8
Y, CORES = 8, 2
NBETA = Y * CORES
BLK = 128
FROM_B = 2
VMEM_LIMIT = 52 * 1024 * 1024

Z_GROUPS = [[x * Z + z for z in range(Z)] for x in range(X)]
X_GROUPS = [[x * Z + z for x in range(X)] for z in range(Z)]


def shift_x(step):
    return [(x * Z + z, (x + step) % X * Z + z) for x in range(X) for z in range(Z)]


SWAP_CORES = [(y * CORES + c, y * CORES + 1 - c) for y in range(Y) for c in range(CORES)]


def params():
    return pltpu.CompilerParams(vmem_limit_bytes=VMEM_LIMIT)


def pack_kernel(wanted, c_ref, out_ref, blocks, sems):
    for b in range(blocks.shape[0]):
        blocks[b] = c_ref[:, b * BLK : (b + 1) * BLK]

    def each(action):
        for t in range(NBETA * FROM_B):
            action(pltpu.make_async_copy(blocks.at[wanted[t]], out_ref.at[t], sems.at[t]))

    each(lambda copy: copy.start())
    each(lambda copy: copy.wait())


def pack(wanted, c):
    rows, cols = c.shape
    total = NBETA * FROM_B
    return pl.pallas_call(
        pack_kernel,
        grid_spec=pltpu.PrefetchScalarGridSpec(
            num_scalar_prefetch=1,
            grid=(1,),
            in_specs=[pl.BlockSpec(c.shape, lambda i, w: (0, 0))],
            out_specs=pl.BlockSpec(memory_space=pl.ANY),
            scratch_shapes=[
                pltpu.VMEM((cols // BLK, rows, BLK), c.dtype),
                pltpu.SemaphoreType.DMA((total,)),
            ],
        ),
        out_shape=jax.ShapeDtypeStruct((total, rows, BLK), c.dtype),
        compiler_params=params(),
        cost_estimate=pl.CostEstimate(flops=0, bytes_accessed=5 << 20, transcendentals=0),
        name="pack",
    )(wanted, c)


def sum_pack_kernel(wanted, *refs):
    parts, (out_ref, inter, sems) = refs[:X], refs[X:]
    step = pl.program_id(0)
    per_step = parts[0].shape[1] // BLK
    for b in range(per_step):
        columns = slice(b * BLK, (b + 1) * BLK)
        total = parts[0][:, columns]
        for part in parts[1:]:
            total += part[:, columns].astype(jnp.float32)
        inter[step * per_step + b] = total.astype(inter.dtype)

    def each(action):
        for t in range(NBETA * FROM_B):
            action(pltpu.make_async_copy(inter.at[wanted[t]], out_ref.at[t], sems.at[t]))

    @pl.when(step == pl.num_programs(0) - 1)
    def _():
        each(lambda copy: copy.start())
        each(lambda copy: copy.wait())


def sum_pack(wanted, parts, steps=2):
    rows, cols = parts[0].shape
    total = NBETA * FROM_B
    return pl.pallas_call(
        sum_pack_kernel,
        grid_spec=pltpu.PrefetchScalarGridSpec(
            num_scalar_prefetch=1,
            grid=(steps,),
            in_specs=[pl.BlockSpec((rows, cols // steps), lambda i, w: (0, i))] * X,
            out_specs=pl.BlockSpec(memory_space=pl.ANY),
            scratch_shapes=[
                pltpu.VMEM((cols // BLK, rows, BLK), jnp.bfloat16),
                pltpu.SemaphoreType.DMA((total,)),
            ],
        ),
        out_shape=jax.ShapeDtypeStruct((total, rows, BLK), jnp.bfloat16),
        compiler_params=params(),
        cost_estimate=pl.CostEstimate(flops=1 << 20, bytes_accessed=6 << 20, transcendentals=0),
        name="sum_pack",
    )(wanted, *parts)


def beta_kernel(op, place, count, pool_any, b_any, *rest):
    n = len(rest) // 2 - 2
    added_any, out_any, pool_ref, b_ref, added, out_ref, sems = (
        rest[:n],
        rest[n],
        rest[n + 1],
        rest[n + 2],
        rest[n + 3 : 2 * n + 3],
        rest[2 * n + 3],
        rest[2 * n + 4],
    )
    slots, cols, _ = b_ref.shape
    parts = 4
    width = cols // parts

    def factor_copy(i):
        span = pl.ds(i * width, width)
        return pltpu.make_async_copy(
            b_any.at[op, :, span, :], b_ref.at[:, span, :], sems.at[i]
        )

    def out_copy(i):
        span = pl.ds(i * width, width)
        return pltpu.make_async_copy(
            out_ref.at[:, span], out_any.at[:, span], sems.at[parts + i]
        )

    pool_copy = pltpu.make_async_copy(pool_any, pool_ref, sems.at[2 * parts])
    added_copies = [
        pltpu.make_async_copy(added_any[i], added[i], sems.at[2 * parts + 1 + i])
        for i in range(n)
    ]
    pool_copy.start()
    factor_copy(0).start()
    for copy in added_copies:
        copy.start()
    for i in range(1, parts):
        factor_copy(i).start()
    pool_copy.wait()
    for i in range(parts):
        factor_copy(i).wait()
        if i == 0:
            for copy in added_copies:
                copy.wait()
        for block in range(i * width // BLK, (i + 1) * width // BLK):
            columns = slice(block * BLK, (block + 1) * BLK)
            valid = count[op, block]
            picked = [pool_ref[place[op, block, s]] for s in range(slots)]
            factor = [
                jnp.where(s < valid, b_ref[s, columns], jnp.zeros((), b_ref.dtype))
                for s in range(slots)
            ]
            total = lax.dot_general(
                jnp.concatenate(picked, axis=1),
                jnp.concatenate(factor, axis=1),
                (((1,), (1,)), ((), ())),
                preferred_element_type=jnp.float32,
            )
            for part in added:
                total += part[:, columns].astype(jnp.float32)
            out_ref[:, columns] = total.astype(out_ref.dtype)
        out_copy(i).start()
    for i in range(parts):
        out_copy(i).wait()


def beta_product(op, place, count, pool, b_slots, added, dtype):
    _, slots, cols, _ = b_slots.shape
    rows = pool.shape[1]
    anywhere = pl.BlockSpec(memory_space=pl.ANY)
    return pl.pallas_call(
        functools.partial(beta_kernel, op),
        grid_spec=pltpu.PrefetchScalarGridSpec(
            num_scalar_prefetch=2,
            grid=(1,),
            in_specs=[
                anywhere,
                pl.BlockSpec(memory_space=pltpu.HBM),
                *([anywhere] * len(added)),
            ],
            out_specs=anywhere,
            scratch_shapes=[
                pltpu.VMEM(pool.shape, pool.dtype),
                pltpu.VMEM((slots, cols, BLK), b_slots.dtype),
                *[pltpu.VMEM(part.shape, part.dtype) for part in added],
                pltpu.VMEM((rows, cols), dtype),
                pltpu.SemaphoreType.DMA((9 + len(added),)),
            ],
        ),
        out_shape=jax.ShapeDtypeStruct((rows, cols), dtype),
        compiler_params=params(),
        cost_estimate=pl.CostEstimate(
            flops=2 * rows * cols * slots * BLK, bytes_accessed=7 << 20, transcendentals=0
        ),
        name="beta_product",
    )(place, count, pool, b_slots, *added)


FEW = 6
POOL_COPIES = 4


def alpha_kernel(op, core, lists, sizes, pool_any, own, *rest):
    near, far = rest[: X - 1], rest[X - 1 : 2 * (X - 1)]
    outs = rest[-X - 7 : -7]
    factors, pool_ref, own_out, sent_out, factor_sems, pool_sems, out_sems = rest[-7:]
    row_count, slots, _, _ = factors.shape
    blocks = row_count // X
    pool_blocks = pool_ref.shape[0]
    order = [*range(1, X), 0]

    def pool_copy(i):
        span = pl.ds(i * (pool_blocks // POOL_COPIES), pool_blocks // POOL_COPIES)
        return pltpu.make_async_copy(pool_any.at[span], pool_ref.at[span], pool_sems.at[i])

    def out_copy(t):
        source = sent_out.at[t - 1] if t else own_out
        return pltpu.make_async_copy(source, outs[t], out_sems.at[t])

    def fetch(source, t):
        for b in range(blocks):
            row = t * blocks + b

            def start(q, carry):
                pltpu.make_async_copy(
                    source.at[lists[op, row, q] // pool_blocks, pl.ds(b * BLK, BLK), :],
                    factors.at[row, q],
                    factor_sems.at[row, q],
                ).start()
                return carry

            lax.fori_loop(0, sizes[op, row], start, 0)

    for i in range(POOL_COPIES):
        pool_copy(i).start()

    @pl.when(core[0] == op)
    def _():
        for t in range(1, X):
            fetch(near[t - 1], t)

    @pl.when(core[0] != op)
    def _():
        for t in range(1, X):
            fetch(far[t - 1], t)

    fetch(own.at[op], 0)
    largest = sizes[op, 0]
    for row in range(row_count):

        def arrive(q, carry):
            pltpu.make_async_copy(
                own.at[op, 0, pl.ds(0, BLK), :], factors.at[row, q], factor_sems.at[row, q]
            ).wait()
            return carry

        lax.fori_loop(0, sizes[op, row], arrive, 0)
        largest = jnp.maximum(largest, sizes[op, row])
    for i in range(POOL_COPIES):
        pool_copy(i).wait()

    def multiply(depth):
        for t in order:
            for b in range(blocks):
                row = t * blocks + b
                size = sizes[op, row]
                left = [
                    jnp.where(q < size, factors[row, q], jnp.zeros((), factors.dtype))
                    for q in range(depth)
                ]
                right = [pool_ref[lists[op, row, q] % pool_blocks] for q in range(depth)]
                total = jnp.dot(
                    jnp.concatenate(left, axis=1),
                    jnp.concatenate(right, axis=0),
                    preferred_element_type=jnp.float32,
                )
                rows = slice(b * BLK, (b + 1) * BLK)
                if t:
                    sent_out[t - 1, rows, :] = total.astype(sent_out.dtype)
                else:
                    own_out[rows, :] = total
            out_copy(t).start()

    @pl.when(largest <= FEW)
    def _():
        multiply(FEW)

    @pl.when(largest > FEW)
    def _():
        multiply(slots)

    for t in order:
        out_copy(t).wait()


def alpha_partials(op, core, lists, sizes, gathered, own, near, far, after=()):
    _, slots, rows, _ = own.shape
    cols = gathered.shape[1]
    pool = gathered.reshape(gathered.shape[0] // BLK, BLK, cols)
    operands = [own, *near, *far, *after]
    row_count = X * rows // BLK
    anywhere = pl.BlockSpec(memory_space=pl.ANY)
    return pl.pallas_call(
        functools.partial(alpha_kernel, op),
        grid_spec=pltpu.PrefetchScalarGridSpec(
            num_scalar_prefetch=3,
            grid=(1,),
            in_specs=[
                pl.BlockSpec(memory_space=pltpu.HBM),
                *([anywhere] * len(operands)),
            ],
            out_specs=[anywhere] * X,
            scratch_shapes=[
                pltpu.VMEM((row_count, slots, BLK, BLK), own.dtype),
                pltpu.VMEM(pool.shape, pool.dtype),
                pltpu.VMEM((rows, cols), jnp.float32),
                pltpu.VMEM((X - 1, rows, cols), jnp.bfloat16),
                pltpu.SemaphoreType.DMA((row_count, slots)),
                pltpu.SemaphoreType.DMA((POOL_COPIES,)),
                pltpu.SemaphoreType.DMA((X,)),
            ],
        ),
        out_shape=[
            jax.ShapeDtypeStruct((rows, cols), jnp.bfloat16 if t else jnp.float32)
            for t in range(X)
        ],
        compiler_params=params(),
        cost_estimate=pl.CostEstimate(
            flops=2 * rows * cols * slots * BLK, bytes_accessed=9 << 20, transcendentals=0
        ),
        name="alpha_partials",
    )(core, lists, sizes, pool, *operands)


def to_their_rows(parts):
    sent = [lax.ppermute(parts[d], "alpha", shift_x(X - d)) for d in range(1, X)]
    return [parts[0], *sent]


def on_device(coeffs, a_blocks, a_list, a_count, b_blocks, b_list, b_count):
    operators, local_rows, slots, _ = a_blocks.shape
    local_cols = coeffs.shape[1]
    row_blocks = local_rows // BLK
    col_blocks = local_cols // BLK
    alpha_here = lax.axis_index("alpha")
    beta_here = lax.axis_index("beta")
    x_here = alpha_here // Z
    z_here = alpha_here % Z
    core_here = beta_here % CORES
    slot_ids = jnp.arange(slots, dtype=jnp.int32)

    local = b_list.reshape(operators, NBETA, col_blocks * slots) - beta_here * col_blocks
    inside = (local >= 0) & (local < col_blocks)
    lowest = jnp.min(jnp.where(inside, local, col_blocks - 1), axis=(0, 2))
    highest = jnp.max(jnp.where(inside, local, 0), axis=(0, 2))
    wanted = jnp.stack([lowest, highest], axis=1).reshape(NBETA * FROM_B)

    mine = lax.dynamic_slice_in_dim(b_list, beta_here * col_blocks, col_blocks, 1)
    beta_counts = lax.dynamic_slice_in_dim(b_count, beta_here * col_blocks, col_blocks, 1)
    owner = mine // col_blocks
    local_id = mine % col_blocks
    is_owner = owner[..., None] == jnp.arange(NBETA, dtype=jnp.int32)
    first = jnp.min(jnp.where(is_owner, local_id[..., None], col_blocks - 1), axis=(0, 1, 2))
    first_here = jnp.sum(jnp.where(is_owner, first, 0), axis=-1)
    beta_place = owner * FROM_B + (local_id != first_here).astype(jnp.int32)

    order = (x_here - jnp.arange(X, dtype=jnp.int32)) % X
    lists = a_list.reshape(operators, X, Z, row_blocks, slots)
    lists = lax.dynamic_index_in_dim(lists, z_here, 2, keepdims=False)
    counts = a_count.reshape(operators, X, Z, row_blocks)
    counts = lax.dynamic_index_in_dim(counts, z_here, 2, keepdims=False)
    per_x = Z * row_blocks
    here = (slot_ids < counts[..., None]) & (lists // per_x == x_here)
    code = slot_ids * per_x + lists % per_x
    earlier = slot_ids[:, None] > slot_ids
    rank = jnp.sum((here[..., None, :] & earlier).astype(jnp.int32), axis=-1)
    at_rank = here[..., None, :] & (rank[..., None, :] == slot_ids[:, None])
    lists = jnp.sum(jnp.where(at_rank, code[..., None, :], 0), axis=-1)
    sizes = jnp.sum(here.astype(jnp.int32), axis=-1)
    pick = order[:, None] == jnp.arange(X, dtype=jnp.int32)
    lists = jnp.sum(jnp.where(pick[None, :, :, None, None], lists[:, None], 0), axis=2)
    sizes = jnp.sum(jnp.where(pick[None, :, :, None], sizes[:, None], 0), axis=2)
    lists = lists.reshape(operators, X * row_blocks, slots)
    sizes = sizes.reshape(operators, X * row_blocks)

    a_slots = a_blocks.transpose(0, 2, 1, 3)
    b_slots = b_blocks.transpose(0, 2, 1, 3)
    a_half = lax.dynamic_index_in_dim(a_slots, core_here, 0, keepdims=False)
    near = [lax.ppermute(a_half, "alpha", shift_x(d)) for d in (1, 2)]
    a_half, beta_place, beta_counts, lists, sizes = lax.optimization_barrier(
        (a_half, beta_place, beta_counts, lists, sizes)
    )
    near.append(lax.ppermute(a_half, "alpha", shift_x(3)))
    far = [lax.ppermute(part, "beta", SWAP_CORES) for part in near]
    core = core_here.reshape(1)

    c_along_z = lax.all_gather(coeffs, "alpha", axis=0, tiled=True, axis_index_groups=Z_GROUPS)
    sent = pack(wanted, coeffs)
    pool_c = lax.all_to_all(sent, "beta", split_axis=0, concat_axis=0, tiled=True)
    d_one = beta_product(1, beta_place, beta_counts, pool_c, b_slots, (), jnp.bfloat16)
    c_along_z, d_one, near, far = lax.optimization_barrier((c_along_z, d_one, near, far))

    inter_parts = alpha_partials(0, core, lists, sizes, c_along_z, a_slots, near, far)
    sent = sum_pack(wanted, to_their_rows(inter_parts))
    pool_inter = lax.all_to_all(sent, "beta", split_axis=0, concat_axis=0, tiled=True)

    d_along_z = lax.all_gather(d_one, "alpha", axis=0, tiled=True, axis_index_groups=Z_GROUPS)
    sigma_parts = alpha_partials(
        1, core, lists, sizes, d_along_z, a_slots, near, far, after=(sent,)
    )
    sigma_one = to_their_rows(sigma_parts)
    return beta_product(0, beta_place, beta_counts, pool_inter, b_slots, sigma_one, jnp.float32)


def solution(mesh):
    in_specs = (
        P("alpha", "beta"),
        P(None, "alpha", None, None),
        P(),
        P(),
        P(None, "beta", None, None),
        P(),
        P(),
    )
    return jax.shard_map(
        on_device, mesh=mesh, in_specs=in_specs, out_specs=P("alpha", "beta"), check_vma=False
    )
```

time: 337 us -> 188 us (0.56)
  blocking collectives: 111 us -> 0 us
  local copies, waits for them, and re-layouts: 58.1 us -> 3.53 us
  starting transfers between devices: 21.4 us -> 65.8 us
  waiting for transfers between devices: 95.9 us -> 68.4 us
  other arithmetic: 9.16 us -> 3.9 us
  Pallas kernels: 26.5 us -> 31.7 us
    all_to_all x2 -> x0, blocking collectives: 111 us -> none  [the longest x1 62.9 us: on_device(): lax.all_to_all(sent, 'beta', split_axis=0, concat_axis=0, tiled=True)]
    all_gather x1, waiting for transfers between devices: 47.4 us -> 0.02 us  [on_device(): lax.all_gather(coeffs, 'alpha', axis=0, tiled=True, axis_index_groups=Z_G...]
    ppermute x4 -> x12, starting transfers between devices: 10.7 us -> 49.1 us  [the longest x3 23.1 us: on_device(): far = [lax.ppermute(part, 'beta', SWAP_CORES) for part in near]]
    unnamed x38 -> x22, local copies, waits for them, and re-layouts: 27.2 us -> 2.11 us
    broadcast_in_dim x3 -> x0, local copies, waits for them, and re-layouts: 18.6 us -> none  [on_device(): jnp.where(beta_valid[:, :, None, :, None], b_blocks.reshape(operators, co...]
    all_to_all x1 -> x2, waiting for transfers between devices: 5.48 us -> 21.7 us  [on_device(): lax.all_to_all(sent, 'beta', split_axis=0, concat_axis=0, tiled=True)]
    reshape x2 -> x1, local copies, waits for them, and re-layouts: 11 us -> 0.09 us  [on_device(): sizes = sizes.reshape(operators, X * row_blocks)]
    select_n x2 -> x0, other arithmetic: 6.98 us -> none  [the longest x1 6.9 us: on_device(): jnp.where(beta_valid[:, :, None, :, None], b_blocks.reshape(operators, co...]
  transfers between devices with their start and end apart: 8 -> 16, of which waited for: 7 -> 8; matrix products, arithmetic and copies ran while one was open for 14% -> 3% of each run, Pallas kernels for 4% -> 14%
where the time goes in v2:
time: 188 us; the launch traced here: 187 us
  waiting for transfers between devices  68.4 us (36%)
  starting transfers between devices  65.8 us (35%)
  Pallas kernels  31.7 us (17%)
  between operations  13.8 us (7%)
  other arithmetic  3.9 us (2%)
  local copies, waits for them, and re-layouts  3.53 us (2%)
    ppermute x3, starting transfers between devices, on_device(): far = [lax.ppermute(part, 'beta', SWAP_CORES) for part in near]  23.1 us
    ppermute x6, waiting for transfers between devices, to_their_rows(): lax.ppermute(parts[d], 'alpha', shift_x(X - d))  23.1 us
    all_to_all x2, waiting for transfers between devices, on_device(): lax.all_to_all(sent, 'beta', split_axis=0, concat_axis=0, tiled=True)  21.7 us
    ppermute x6, starting transfers between devices, to_their_rows(): lax.ppermute(parts[d], 'alpha', shift_x(X - d))  18.5 us
    all_to_all x2, starting transfers between devices, on_device(): lax.all_to_all(sent, 'beta', split_axis=0, concat_axis=0, tiled=True)  16.7 us
    pallas_call x2, Pallas kernels, alpha_partials(): pl.pallas_call(functools.partial(alpha_kernel, op), grid_spec=pltpu.Prefe...  14.7 us
    ppermute x1, waiting for transfers between devices, on_device(): near.append(lax.ppermute(a_half, 'alpha', shift_x(3)))  11.9 us
    pallas_call x2, Pallas kernels, beta_product(): pl.pallas_call(functools.partial(beta_kernel, op), grid_spec=pltpu.Prefet...  11.2 us
  transfers between devices with their start and end apart: 16, of which 8 were waited for; matrix products, arithmetic and copies ran while one was open for 3% of the time, Pallas kernels for 14%

profile of v2, /device:TPU:1, one launch (start us, length us, event | category | flops | bytes accessed | tf_op | source)
XLA Modules:
  0.0 187.2 jit_solution(10718411130864488856)
XLA Ops:
  9.7 2.3 %pack.1 = bf16[32,256,128]{2,1,0:T(8,128)(2,1)} custom-call(s32[32]{0:T(128)S(1)} %reshape.168.wanted, bf16[256,1024]{1,0:T(8,128)(2,1)S(1)} %copy-done.1), custom_call_target="tpu_custom_call" | custom-call | bytes 5242880 | tf_op jit(solution)/shard_map/pack/pallas_call | solution.py:47
  12.0 11.2 %all-to-all-start = ((bf16[32,256,128]{2,1,0:T(8,128)(2,1)}), bf16[32,256,128]{2,1,0:T(8,128)(2,1)}, u32[]{:S(2)}, u32[]{:S(2)}) async-start(bf16[32,256,128]{2,1,0:T(8,128)(2,1)} %pack.1), calls=%async_computation | async-start | bytes 4194304 | tf_op jit(solution)/shard_map/all_to_all | solution.py:407
  27.5 2.0 %collective-permute-start.2 = (bf16[11,256,128]{2,1,0:T(8,128)(2,1)S(1)}, bf16[11,256,128]{2,1,0:T(8,128)(2,1)S(1)}, u32[]{:S(2)}, u32[]{:S(2)}) collective-permute-start(bf16[11,256,128]{2,1,0:T(8,128)(2,1)S(1)} %dynamic-slice_bitcast_fusion), channel_id=1, source_target_pairs={{0,384},{16,400},{32,416},{48,432},{64,448},{80,464},{96,480},{112... | collective-permute-start | bytes 2162696 | tf_op jit(solution)/shard_map/ppermute | solution.py:401
  29.5 3.3 %collective-permute-start = (bf16[11,256,128]{2,1,0:T(8,128)(2,1)S(1)}, bf16[11,256,128]{2,1,0:T(8,128)(2,1)S(1)}, u32[]{:S(2)}, u32[]{:S(2)}) collective-permute-start(bf16[11,256,128]{2,1,0:T(8,128)(2,1)S(1)} %dynamic-slice_bitcast_fusion), channel_id=1, source_target_pairs={{0,128},{16,144},{32,160},{48,176},{64,192},{80,208},{96,224},{112... | collective-permute-start | bytes 2162696 | tf_op jit(solution)/shard_map/ppermute | solution.py:397
  32.8 2.2 %collective-permute-start.1 = (bf16[11,256,128]{2,1,0:T(8,128)(2,1)S(1)}, bf16[11,256,128]{2,1,0:T(8,128)(2,1)S(1)}, u32[]{:S(2)}, u32[]{:S(2)}) collective-permute-start(bf16[11,256,128]{2,1,0:T(8,128)(2,1)S(1)} %dynamic-slice_bitcast_fusion), channel_id=1, source_target_pairs={{0,256},{16,272},{32,288},{48,304},{64,320},{80,336},{96,352},{112... | collective-permute-start | bytes 2162696 | tf_op jit(solution)/shard_map/ppermute | solution.py:397
  35.1 11.9 %collective-permute-done.2.rest_2_ = bf16[11,256,128]{2,1,0:T(8,128)(2,1)S(1)} collective-permute-done((bf16[11,256,128]{2,1,0:T(8,128)(2,1)S(1)}, bf16[11,256,128]{2,1,0:T(8,128)(2,1)S(1)}, u32[]{:S(2)}, u32[]{:S(2)}) %collective-permute-start.2) | collective-permute-done | bytes 720928 | tf_op jit(solution)/shard_map/ppermute | solution.py:401
  47.0 3.6 %collective-permute-start.5 = (bf16[11,256,128]{2,1,0:T(8,128)(2,1)S(1)}, bf16[11,256,128]{2,1,0:T(8,128)(2,1)S(1)}, u32[]{:S(2)}, u32[]{:S(2)}) collective-permute-start(bf16[11,256,128]{2,1,0:T(8,128)(2,1)S(1)} %collective-permute-done.2.rest_2_), channel_id=1, source_target_pairs={{0,1},{1,0},{2,3},{3,2},{4,5},{5,4},{6,7},{7,6},{8,9},{9,8},{10,11... | collective-permute-start | bytes 2162696 | tf_op jit(solution)/shard_map/ppermute | solution.py:402
  50.9 17.6 %collective-permute-start.3 = (bf16[11,256,128]{2,1,0:T(8,128)(2,1)S(1)}, bf16[11,256,128]{2,1,0:T(8,128)(2,1)}, u32[]{:S(2)}, u32[]{:S(2)}) collective-permute-start(bf16[11,256,128]{2,1,0:T(8,128)(2,1)S(1)} %collective-permute-done.rest_0_), channel_id=1, source_target_pairs={{0,1},{1,0},{2,3},{3,2},{4,5},{5,4},{6,7},{7,6},{8,9},{9,8},{10,11... | collective-permute-start | bytes 2162696 | tf_op jit(solution)/shard_map/ppermute | solution.py:402
  72.2 5.4 %beta_product.2 = bf16[256,1024]{1,0:T(8,128)(2,1)} custom-call(s32[2,8,11]{2,1,0:T(8,128)S(1)} %convert_add_fusion.place, s32[2,8]{1,0:T(2,128)S(1)} %constant_dynamic-slice_fusion.1.count, bf16[32,256,128]{2,1,0:T(8,128)(2,1)} %all-to-all-done.pool_any, bf16[2,11,1024,128]{3,2,1,0:T(8,128)(2,1)} %bitcast.18), custom_call_target="tpu_custom_call" | custom-call | flops 738197504 | bytes 7340032 | tf_op jit(solution)/shard_map/beta_product/pallas_call | solution.py:179
  78.6 7.4 %alpha_partials.2 = (f32[256,1024]{1,0:T(8,128)}, bf16[256,1024]{1,0:T(8,128)(2,1)S(1)}, bf16[256,1024]{1,0:T(8,128)(2,1)S(1)}, bf16[256,1024]{1,0:T(8,128)(2,1)S(1)}) custom-call(s32[1]{0:T(128)} %bitcast.8.core, s32[2,8,11]{2,1,0:T(8,128)S(1)} %bitcast.16, s32[2,8]{1,0:T(2,128)S(1)} %reshape.167.sizes, bf16[16,128,1024]{2,1,0:T(8,128)(2,1)} %bitcast.22, ...), custom_call_target="tpu_custom_call" | custom-call | flops 738197504 | bytes 9437184 | tf_op jit(solution)/shard_map/alpha_partials/pallas_call | solution.py:311
  87.9 2.5 %collective-permute-start.7 = (bf16[256,1024]{1,0:T(8,128)(2,1)S(1)}, bf16[256,1024]{1,0:T(8,128)(2,1)S(1)}, u32[]{:S(2)}, u32[]{:S(2)}) collective-permute-start(bf16[256,1024]{1,0:T(8,128)(2,1)S(1)} %get-tuple-element.40), channel_id=1, source_target_pairs={{0,256},{16,272},{32,288},{48,304},{64,320},{80,336},{96,352},{112... | collective-permute-start | bytes 1572872 | tf_op jit(solution)/shard_map/ppermute | solution.py:344
  90.3 3.0 %collective-permute-start.8 = (bf16[256,1024]{1,0:T(8,128)(2,1)S(1)}, bf16[256,1024]{1,0:T(8,128)(2,1)S(1)}, u32[]{:S(2)}, u32[]{:S(2)}) collective-permute-start(bf16[256,1024]{1,0:T(8,128)(2,1)S(1)} %get-tuple-element.41), channel_id=1, source_target_pairs={{0,128},{16,144},{32,160},{48,176},{64,192},{80,208},{96,224},{112... | collective-permute-start | bytes 1572872 | tf_op jit(solution)/shard_map/ppermute | solution.py:344
  93.4 7.7 %collective-permute-done.6.refs_1_ = bf16[256,1024]{1,0:T(8,128)(2,1)S(1)} collective-permute-done((bf16[256,1024]{1,0:T(8,128)(2,1)S(1)}, bf16[256,1024]{1,0:T(8,128)(2,1)S(1)}, u32[]{:S(2)}, u32[]{:S(2)}) %collective-permute-start.6) | collective-permute-done | bytes 524320 | tf_op jit(solution)/shard_map/ppermute | solution.py:344
  101.1 3.2 %collective-permute-done.7.refs_2_ = bf16[256,1024]{1,0:T(8,128)(2,1)S(1)} collective-permute-done((bf16[256,1024]{1,0:T(8,128)(2,1)S(1)}, bf16[256,1024]{1,0:T(8,128)(2,1)S(1)}, u32[]{:S(2)}, u32[]{:S(2)}) %collective-permute-start.7) | collective-permute-done | bytes 524320 | tf_op jit(solution)/shard_map/ppermute | solution.py:344
  104.2 12.2 %collective-permute-done.8.refs_3_ = bf16[256,1024]{1,0:T(8,128)(2,1)S(1)} collective-permute-done((bf16[256,1024]{1,0:T(8,128)(2,1)S(1)}, bf16[256,1024]{1,0:T(8,128)(2,1)S(1)}, u32[]{:S(2)}, u32[]{:S(2)}) %collective-permute-start.8) | collective-permute-done | bytes 524320 | tf_op jit(solution)/shard_map/ppermute | solution.py:344
  116.5 3.5 %sum_pack.1.rest_6_ = bf16[32,256,128]{2,1,0:T(8,128)(2,1)} custom-call(s32[32]{0:T(128)S(1)} %reshape.168.wanted, f32[256,1024]{1,0:T(8,128)} %get-tuple-element.38.refs_0_, bf16[256,1024]{1,0:T(8,128)(2,1)S(1)} %collective-permute-done.6.refs_1_, bf16[256,1024]{1,0:T(8,128)(2,1)S(1)} %collective-permute-done.7.refs_2_, ...), custom_call_target="tpu_custom_call" | custom-call | flops 1048576 | bytes 6291456 | tf_op jit(solution)/shard_map/sum_pack/pallas_call | solution.py:90
  120.0 5.5 %all-to-all-start.1 = ((bf16[32,256,128]{2,1,0:T(8,128)(2,1)}), bf16[32,256,128]{2,1,0:T(8,128)(2,1)}, u32[]{:S(2)}, u32[]{:S(2)}) async-start(bf16[32,256,128]{2,1,0:T(8,128)(2,1)} %sum_pack.1.rest_6_), calls=%async_computation.1 | async-start | bytes 4194304 | tf_op jit(solution)/shard_map/all_to_all | solution.py:413
  125.5 10.7 %all-gather.5.cloned.1.call-done = bf16[2048,1024]{1,0:T(8,128)(2,1)} async-done(((bf16[256,1024]{1,0:T(8,128)(2,1)}), bf16[2048,1024]{1,0:T(8,128)(2,1)}) %all-gather.5.cloned.1.call-update) | async-done | bytes 4194320 | tf_op jit(solution)/shard_map/all_gather | solution.py:415
  136.1 7.4 %alpha_partials.3 = (f32[256,1024]{1,0:T(8,128)}, bf16[256,1024]{1,0:T(8,128)(2,1)S(1)}, bf16[256,1024]{1,0:T(8,128)(2,1)S(1)}, bf16[256,1024]{1,0:T(8,128)(2,1)S(1)}) custom-call(s32[1]{0:T(128)} %bitcast.8.core, s32[2,8,11]{2,1,0:T(8,128)S(1)} %bitcast.17, s32[2,8]{1,0:T(2,128)S(1)} %reshape.167.sizes, bf16[16,128,1024]{2,1,0:T(8,128)(2,1)} %bitcast.23, ...), custom_call_target="tpu_custom_call" | custom-call | flops 738197504 | bytes 9437184 | tf_op jit(solution)/shard_map/alpha_partials/pallas_call | solution.py:311
  143.5 4.6 %collective-permute-start.10 = (bf16[256,1024]{1,0:T(8,128)(2,1)S(1)}, bf16[256,1024]{1,0:T(8,128)(2,1)S(1)}, u32[]{:S(2)}, u32[]{:S(2)}) collective-permute-start(bf16[256,1024]{1,0:T(8,128)(2,1)S(1)} %get-tuple-element.45), channel_id=1, source_target_pairs={{0,256},{16,272},{32,288},{48,304},{64,320},{80,336},{96,352},{112... | collective-permute-start | bytes 1572872 | tf_op jit(solution)/shard_map/ppermute | solution.py:344
  148.1 2.3 %collective-permute-start.11 = (bf16[256,1024]{1,0:T(8,128)(2,1)S(1)}, bf16[256,1024]{1,0:T(8,128)(2,1)S(1)}, u32[]{:S(2)}, u32[]{:S(2)}) collective-permute-start(bf16[256,1024]{1,0:T(8,128)(2,1)S(1)} %get-tuple-element.46), channel_id=1, source_target_pairs={{0,128},{16,144},{32,160},{48,176},{64,192},{80,208},{96,224},{112... | collective-permute-start | bytes 1572872 | tf_op jit(solution)/shard_map/ppermute | solution.py:344
  150.5 4.2 %collective-permute-start.9 = (bf16[256,1024]{1,0:T(8,128)(2,1)S(1)}, bf16[256,1024]{1,0:T(8,128)(2,1)S(1)}, u32[]{:S(2)}, u32[]{:S(2)}) collective-permute-start(bf16[256,1024]{1,0:T(8,128)(2,1)S(1)} %get-tuple-element.44), channel_id=1, source_target_pairs={{0,384},{16,400},{32,416},{48,432},{64,448},{80,464},{96,480},{112... | collective-permute-start | bytes 1572872 | tf_op jit(solution)/shard_map/ppermute | solution.py:344
  154.6 19.9 %all-to-all-done.1.pool_any = bf16[32,256,128]{2,1,0:T(8,128)(2,1)} async-done(((bf16[32,256,128]{2,1,0:T(8,128)(2,1)}), bf16[32,256,128]{2,1,0:T(8,128)(2,1)}, u32[]{:S(2)}, u32[]{:S(2)}) %all-to-all-start.1) | async-done | bytes 2097184 | tf_op jit(solution)/shard_map/all_to_all | solution.py:413
  174.6 5.8 %beta_product.3 = f32[256,1024]{1,0:T(8,128)} custom-call(s32[2,8,11]{2,1,0:T(8,128)S(1)} %convert_add_fusion.place, s32[2,8]{1,0:T(2,128)S(1)} %constant_dynamic-slice_fusion.1.count, bf16[32,256,128]{2,1,0:T(8,128)(2,1)} %all-to-all-done.1.pool_any, bf16[2,11,1024,128]{3,2,1,0:T(8,128)(2,1)} %bitcast.19, f32[256,1024]{1,0:T(8,128)} %get-tuple-element.43.rest_0_, ...), custom_call_target="tpu_custom_call" | custom-call | flops 738197504 | bytes 7340032 | tf_op jit(solution)/shard_map/beta_product/pallas_call | solution.py:179
  (73 shorter events, 14.2 us)
Async XLA Ops:
  6.5 20.7 %copy-start = (s32[2,128]{1,0:T(2,128)S(1)}, s32[2,128]{1,0:T(2,128)}, u32[]{:S(2)}) copy-start(s32[2,128]{1,0:T(2,128)} %param.13) | copy-start | bytes 3076
  6.5 71.2 %all-gather.3.cloned.1.call-start = ((), (), s32[]{:S(2)}) async-start(), calls=%async_computation.2 | async-start | bytes 4718592 | tf_op jit(solution)/shard_map/all_gather | solution.py:405
  11.9 11.3 %copy-start.8 = (s32[2,64,11]{1,0,2:T(2,128)S(1)}, s32[2,64,11]{1,0,2:T(2,128)}, u32[]{:S(2)}) copy-start(s32[2,64,11]{1,0,2:T(2,128)} %param.9) | copy-start | bytes 16900
  11.9 11.4 %copy-start.9 = (s32[2,64]{1,0:T(2,128)S(1)}, s32[2,64]{1,0:T(2,128)}, u32[]{:S(2)}) copy-start(s32[2,64]{1,0:T(2,128)} %param.10) | copy-start | bytes 1540
  11.9 14.2 %copy-start.7 = (s32[2,128,11]{1,0,2:T(2,128)S(1)}, s32[2,128,11]{1,0,2:T(2,128)}, u32[]{:S(2)}) copy-start(s32[2,128,11]{1,0,2:T(2,128)} %param.12) | copy-start | bytes 33796
  12.0 15.5 %copy-start.2 = (bf16[2,256,11,128]{3,1,2,0:T(8,128)(2,1)S(1)}, bf16[2,256,11,128]{3,1,2,0:T(8,128)(2,1)}, u32[]{:S(2)}) copy-start(bf16[2,256,11,128]{3,1,2,0:T(8,128)(2,1)} %param.8) | copy-start | bytes 4325380
  12.0 60.3 %all-to-all-start = ((bf16[32,256,128]{2,1,0:T(8,128)(2,1)}), bf16[32,256,128]{2,1,0:T(8,128)(2,1)}, u32[]{:S(2)}, u32[]{:S(2)}) async-start(bf16[32,256,128]{2,1,0:T(8,128)(2,1)} %pack.1), calls=%async_computation | async-start | bytes 4194304 | tf_op jit(solution)/shard_map/all_to_all | solution.py:407
  23.2 113.0 %all-gather.5.cloned.1.call-start = ((), (), s32[]{:S(2)}) async-start(), calls=%async_computation.3 | async-start | bytes 4718592 | tf_op jit(solution)/shard_map/all_gather | solution.py:415
  27.5 19.4 %collective-permute-start.2 = (bf16[11,256,128]{2,1,0:T(8,128)(2,1)S(1)}, bf16[11,256,128]{2,1,0:T(8,128)(2,1)S(1)}, u32[]{:S(2)}, u32[]{:S(2)}) collective-permute-start(bf16[11,256,128]{2,1,0:T(8,128)(2,1)S(1)} %dynamic-slice_bitcast_fusion), channel_id=1, source_target_pairs={{0,384},{16,400},{32,416},{48,432},{64,448},{80,464},{96,480},{112... | collective-permute-start | bytes 2162696 | tf_op jit(solution)/shard_map/ppermute | solution.py:401
  29.5 21.4 %collective-permute-start = (bf16[11,256,128]{2,1,0:T(8,128)(2,1)S(1)}, bf16[11,256,128]{2,1,0:T(8,128)(2,1)S(1)}, u32[]{:S(2)}, u32[]{:S(2)}) collective-permute-start(bf16[11,256,128]{2,1,0:T(8,128)(2,1)S(1)} %dynamic-slice_bitcast_fusion), channel_id=1, source_target_pairs={{0,128},{16,144},{32,160},{48,176},{64,192},{80,208},{96,224},{112... | collective-permute-start | bytes 2162696 | tf_op jit(solution)/shard_map/ppermute | solution.py:397
  32.8 35.7 %collective-permute-start.1 = (bf16[11,256,128]{2,1,0:T(8,128)(2,1)S(1)}, bf16[11,256,128]{2,1,0:T(8,128)(2,1)S(1)}, u32[]{:S(2)}, u32[]{:S(2)}) collective-permute-start(bf16[11,256,128]{2,1,0:T(8,128)(2,1)S(1)} %dynamic-slice_bitcast_fusion), channel_id=1, source_target_pairs={{0,256},{16,272},{32,288},{48,304},{64,320},{80,336},{96,352},{112... | collective-permute-start | bytes 2162696 | tf_op jit(solution)/shard_map/ppermute | solution.py:397
  47.0 30.7 %copy-start.3 = (bf16[11,256,128]{2,1,0:T(8,128)(2,1)}, bf16[11,256,128]{2,1,0:T(8,128)(2,1)S(1)}, u32[]{:S(2)}) copy-start(bf16[11,256,128]{2,1,0:T(8,128)(2,1)S(1)} %collective-permute-done.2.rest_2_) | copy-start | bytes 2162692
  47.0 30.7 %collective-permute-start.5 = (bf16[11,256,128]{2,1,0:T(8,128)(2,1)S(1)}, bf16[11,256,128]{2,1,0:T(8,128)(2,1)S(1)}, u32[]{:S(2)}, u32[]{:S(2)}) collective-permute-start(bf16[11,256,128]{2,1,0:T(8,128)(2,1)S(1)} %collective-permute-done.2.rest_2_), channel_id=1, source_target_pairs={{0,1},{1,0},{2,3},{3,2},{4,5},{5,4},{6,7},{7,6},{8,9},{9,8},{10,11... | collective-permute-start | bytes 2162696 | tf_op jit(solution)/shard_map/ppermute | solution.py:402
  50.9 26.8 %copy-start.4 = (bf16[11,256,128]{2,1,0:T(8,128)(2,1)}, bf16[11,256,128]{2,1,0:T(8,128)(2,1)S(1)}, u32[]{:S(2)}) copy-start(bf16[11,256,128]{2,1,0:T(8,128)(2,1)S(1)} %collective-permute-done.rest_0_) | copy-start | bytes 2162692
  50.9 26.8 %collective-permute-start.3 = (bf16[11,256,128]{2,1,0:T(8,128)(2,1)S(1)}, bf16[11,256,128]{2,1,0:T(8,128)(2,1)}, u32[]{:S(2)}, u32[]{:S(2)}) collective-permute-start(bf16[11,256,128]{2,1,0:T(8,128)(2,1)S(1)} %collective-permute-done.rest_0_), channel_id=1, source_target_pairs={{0,1},{1,0},{2,3},{3,2},{4,5},{5,4},{6,7},{7,6},{8,9},{9,8},{10,11... | collective-permute-start | bytes 2162696 | tf_op jit(solution)/shard_map/ppermute | solution.py:402
  68.5 9.1 %copy-start.5 = (bf16[11,256,128]{2,1,0:T(8,128)(2,1)}, bf16[11,256,128]{2,1,0:T(8,128)(2,1)S(1)}, u32[]{:S(2)}) copy-start(bf16[11,256,128]{2,1,0:T(8,128)(2,1)S(1)} %collective-permute-done.1.rest_1_) | copy-start | bytes 2162692
  68.5 9.2 %collective-permute-start.4 = (bf16[11,256,128]{2,1,0:T(8,128)(2,1)S(1)}, bf16[11,256,128]{2,1,0:T(8,128)(2,1)}, u32[]{:S(2)}, u32[]{:S(2)}) collective-permute-start(bf16[11,256,128]{2,1,0:T(8,128)(2,1)S(1)} %collective-permute-done.1.rest_1_), channel_id=1, source_target_pairs={{0,1},{1,0},{2,3},{3,2},{4,5},{5,4},{6,7},{7,6},{8,9},{9,8},{10,11... | collective-permute-start | bytes 2162696 | tf_op jit(solution)/shard_map/ppermute | solution.py:402
  86.0 15.1 %collective-permute-start.6 = (bf16[256,1024]{1,0:T(8,128)(2,1)S(1)}, bf16[256,1024]{1,0:T(8,128)(2,1)S(1)}, u32[]{:S(2)}, u32[]{:S(2)}) collective-permute-start(bf16[256,1024]{1,0:T(8,128)(2,1)S(1)} %get-tuple-element.39), channel_id=1, source_target_pairs={{0,384},{16,400},{32,416},{48,432},{64,448},{80,464},{96,480},{112... | collective-permute-start | bytes 1572872 | tf_op jit(solution)/shard_map/ppermute | solution.py:344
  87.9 16.4 %collective-permute-start.7 = (bf16[256,1024]{1,0:T(8,128)(2,1)S(1)}, bf16[256,1024]{1,0:T(8,128)(2,1)S(1)}, u32[]{:S(2)}, u32[]{:S(2)}) collective-permute-start(bf16[256,1024]{1,0:T(8,128)(2,1)S(1)} %get-tuple-element.40), channel_id=1, source_target_pairs={{0,256},{16,272},{32,288},{48,304},{64,320},{80,336},{96,352},{112... | collective-permute-start | bytes 1572872 | tf_op jit(solution)/shard_map/ppermute | solution.py:344
  90.3 26.1 %collective-permute-start.8 = (bf16[256,1024]{1,0:T(8,128)(2,1)S(1)}, bf16[256,1024]{1,0:T(8,128)(2,1)S(1)}, u32[]{:S(2)}, u32[]{:S(2)}) collective-permute-start(bf16[256,1024]{1,0:T(8,128)(2,1)S(1)} %get-tuple-element.41), channel_id=1, source_target_pairs={{0,128},{16,144},{32,160},{48,176},{64,192},{80,208},{96,224},{112... | collective-permute-start | bytes 1572872 | tf_op jit(solution)/shard_map/ppermute | solution.py:344
  120.0 54.6 %all-to-all-start.1 = ((bf16[32,256,128]{2,1,0:T(8,128)(2,1)}), bf16[32,256,128]{2,1,0:T(8,128)(2,1)}, u32[]{:S(2)}, u32[]{:S(2)}) async-start(bf16[32,256,128]{2,1,0:T(8,128)(2,1)} %sum_pack.1.rest_6_), calls=%async_computation.1 | async-start | bytes 4194304 | tf_op jit(solution)/shard_map/all_to_all | solution.py:413
  143.5 31.0 %collective-permute-start.10 = (bf16[256,1024]{1,0:T(8,128)(2,1)S(1)}, bf16[256,1024]{1,0:T(8,128)(2,1)S(1)}, u32[]{:S(2)}, u32[]{:S(2)}) collective-permute-start(bf16[256,1024]{1,0:T(8,128)(2,1)S(1)} %get-tuple-element.45), channel_id=1, source_target_pairs={{0,256},{16,272},{32,288},{48,304},{64,320},{80,336},{96,352},{112... | collective-permute-start | bytes 1572872 | tf_op jit(solution)/shard_map/ppermute | solution.py:344
  148.1 26.4 %collective-permute-start.11 = (bf16[256,1024]{1,0:T(8,128)(2,1)S(1)}, bf16[256,1024]{1,0:T(8,128)(2,1)S(1)}, u32[]{:S(2)}, u32[]{:S(2)}) collective-permute-start(bf16[256,1024]{1,0:T(8,128)(2,1)S(1)} %get-tuple-element.46), channel_id=1, source_target_pairs={{0,128},{16,144},{32,160},{48,176},{64,192},{80,208},{96,224},{112... | collective-permute-start | bytes 1572872 | tf_op jit(solution)/shard_map/ppermute | solution.py:344
  150.5 24.1 %collective-permute-start.9 = (bf16[256,1024]{1,0:T(8,128)(2,1)S(1)}, bf16[256,1024]{1,0:T(8,128)(2,1)S(1)}, u32[]{:S(2)}, u32[]{:S(2)}) collective-permute-start(bf16[256,1024]{1,0:T(8,128)(2,1)S(1)} %get-tuple-element.44), channel_id=1, source_target_pairs={{0,384},{16,400},{32,416},{48,432},{64,448},{80,464},{96,480},{112... | collective-permute-start | bytes 1572872 | tf_op jit(solution)/shard_map/ppermute | solution.py:344
  (2 other events, 2.0 us)
Sparse Core Ops, SparseCore 0:
  9.4 63.7 all-gather.2
  77.9 58.2 all-gather.4

commit v3 on v2

--- a/solution.py
+++ b/solution.py
@@ -12,7 +12,7 @@
 NBETA = Y * CORES
 BLK = 128
 FROM_B = 2
-VMEM_LIMIT = 52 * 1024 * 1024
+VMEM_LIMIT = 50 * 1024 * 1024
 
 Z_GROUPS = [[x * Z + z for z in range(Z)] for x in range(X)]
 X_GROUPS = [[x * Z + z for x in range(X)] for z in range(Z)]
@@ -64,7 +64,7 @@
 
 
 def sum_pack_kernel(wanted, *refs):
-    parts, (out_ref, inter, sems) = refs[:X], refs[X:]
+    parts, (out_ref, inter, sems) = refs[:-3], refs[-3:]
     step = pl.program_id(0)
     per_step = parts[0].shape[1] // BLK
     for b in range(per_step):
@@ -92,7 +92,7 @@
         grid_spec=pltpu.PrefetchScalarGridSpec(
             num_scalar_prefetch=1,
             grid=(steps,),
-            in_specs=[pl.BlockSpec((rows, cols // steps), lambda i, w: (0, i))] * X,
+            in_specs=[pl.BlockSpec((rows, cols // steps), lambda i, w: (0, i))] * len(parts),
             out_specs=pl.BlockSpec(memory_space=pl.ANY),
             scratch_shapes=[
                 pltpu.VMEM((cols // BLK, rows, BLK), jnp.bfloat16),
@@ -208,53 +208,56 @@
 POOL_COPIES = 4
 
 
-def alpha_kernel(op, core, lists, sizes, pool_any, own, *rest):
+def alpha_kernel(op, steps, core, lists, sizes, pool_any, own, *rest):
     near, far = rest[: X - 1], rest[X - 1 : 2 * (X - 1)]
-    outs = rest[-X - 7 : -7]
-    factors, pool_ref, own_out, sent_out, factor_sems, pool_sems, out_sems = rest[-7:]
+    outs = rest[-len(steps) - 6 : -6]
+    factors, pool_ref, results, factor_sems, pool_sems, out_sems = rest[-6:]
     row_count, slots, _, _ = factors.shape
-    blocks = row_count // X
+    blocks = row_count // len(steps)
     pool_blocks = pool_ref.shape[0]
-    order = [*range(1, X), 0]
 
     def pool_copy(i):
         span = pl.ds(i * (pool_blocks // POOL_COPIES), pool_blocks // POOL_COPIES)
         return pltpu.make_async_copy(pool_any.at[span], pool_ref.at[span], pool_sems.at[i])
 
-    def out_copy(t):
-        source = sent_out.at[t - 1] if t else own_out
-        return pltpu.make_async_copy(source, outs[t], out_sems.at[t])
-
-    def fetch(source, t):
+    def out_copy(i):
+        return pltpu.make_async_copy(results[i], outs[i], out_sems.at[i])
+
+    def fetch(source, i):
         for b in range(blocks):
-            row = t * blocks + b
+            listed, row = steps[i] * blocks + b, i * blocks + b
 
             def start(q, carry):
                 pltpu.make_async_copy(
-                    source.at[lists[op, row, q] // pool_blocks, pl.ds(b * BLK, BLK), :],
+                    source.at[lists[op, listed, q] // pool_blocks, pl.ds(b * BLK, BLK), :],
                     factors.at[row, q],
                     factor_sems.at[row, q],
                 ).start()
                 return carry
 
-            lax.fori_loop(0, sizes[op, row], start, 0)
+            lax.fori_loop(0, sizes[op, listed], start, 0)
 
     for i in range(POOL_COPIES):
         pool_copy(i).start()
 
     @pl.when(core[0] == op)
     def _():
-        for t in range(1, X):
-            fetch(near[t - 1], t)
+        for i, t in enumerate(steps):
+            if t:
+                fetch(near[t - 1], i)
 
     @pl.when(core[0] != op)
     def _():
-        for t in range(1, X):
-            fetch(far[t - 1], t)
-
-    fetch(own.at[op], 0)
-    largest = sizes[op, 0]
+        for i, t in enumerate(steps):
+            if t:
+                fetch(far[t - 1], i)
+
+    for i, t in enumerate(steps):
+        if not t:
+            fetch(own.at[op], i)
+    largest = jnp.int32(0)
     for row in range(row_count):
+        listed = steps[row // blocks] * blocks + row % blocks
 
         def arrive(q, carry):
             pltpu.make_async_copy(
@@ -262,32 +265,28 @@
             ).wait()
             return carry
 
-        lax.fori_loop(0, sizes[op, row], arrive, 0)
-        largest = jnp.maximum(largest, sizes[op, row])
+        lax.fori_loop(0, sizes[op, listed], arrive, 0)
+        largest = jnp.maximum(largest, sizes[op, listed])
     for i in range(POOL_COPIES):
         pool_copy(i).wait()
 
     def multiply(depth):
-        for t in order:
+        for i, t in enumerate(steps):
             for b in range(blocks):
-                row = t * blocks + b
-                size = sizes[op, row]
+                listed, row = t * blocks + b, i * blocks + b
+                size = sizes[op, listed]
                 left = [
                     jnp.where(q < size, factors[row, q], jnp.zeros((), factors.dtype))
                     for q in range(depth)
                 ]
-                right = [pool_ref[lists[op, row, q] % pool_blocks] for q in range(depth)]
+                right = [pool_ref[lists[op, listed, q] % pool_blocks] for q in range(depth)]
                 total = jnp.dot(
                     jnp.concatenate(left, axis=1),
                     jnp.concatenate(right, axis=0),
                     preferred_element_type=jnp.float32,
                 )
-                rows = slice(b * BLK, (b + 1) * BLK)
-                if t:
-                    sent_out[t - 1, rows, :] = total.astype(sent_out.dtype)
-                else:
-                    own_out[rows, :] = total
-            out_copy(t).start()
+                results[i][b * BLK : (b + 1) * BLK, :] = total.astype(results[i].dtype)
+            out_copy(i).start()
 
     @pl.when(largest <= FEW)
     def _():
@@ -297,52 +296,71 @@
     def _():
         multiply(slots)
 
-    for t in order:
-        out_copy(t).wait()
-
-
-def alpha_partials(op, core, lists, sizes, gathered, own, near, far, after=()):
+    for i in range(len(steps)):
+        out_copy(i).wait()
+
+
+def alpha_products(op, steps, core, lists, sizes, gathered, own, near, far, after):
     _, slots, rows, _ = own.shape
     cols = gathered.shape[1]
     pool = gathered.reshape(gathered.shape[0] // BLK, BLK, cols)
     operands = [own, *near, *far, *after]
-    row_count = X * rows // BLK
+    row_count = len(steps) * rows // BLK
     anywhere = pl.BlockSpec(memory_space=pl.ANY)
+    types = [jnp.bfloat16 if t else jnp.float32 for t in steps]
     return pl.pallas_call(
-        functools.partial(alpha_kernel, op),
+        functools.partial(alpha_kernel, op, steps),
         grid_spec=pltpu.PrefetchScalarGridSpec(
             num_scalar_prefetch=3,
             grid=(1,),
-            in_specs=[
-                pl.BlockSpec(memory_space=pltpu.HBM),
-                *([anywhere] * len(operands)),
-            ],
-            out_specs=[anywhere] * X,
+            in_specs=[anywhere] * (1 + len(operands)),
+            out_specs=[anywhere] * len(steps),
             scratch_shapes=[
                 pltpu.VMEM((row_count, slots, BLK, BLK), own.dtype),
                 pltpu.VMEM(pool.shape, pool.dtype),
-                pltpu.VMEM((rows, cols), jnp.float32),
-                pltpu.VMEM((X - 1, rows, cols), jnp.bfloat16),
+                [pltpu.VMEM((rows, cols), kind) for kind in types],
                 pltpu.SemaphoreType.DMA((row_count, slots)),
                 pltpu.SemaphoreType.DMA((POOL_COPIES,)),
-                pltpu.SemaphoreType.DMA((X,)),
+                pltpu.SemaphoreType.DMA((len(steps),)),
             ],
         ),
-        out_shape=[
-            jax.ShapeDtypeStruct((rows, cols), jnp.bfloat16 if t else jnp.float32)
-            for t in range(X)
-        ],
+        out_shape=[jax.ShapeDtypeStruct((rows, cols), kind) for kind in types],
         compiler_params=params(),
         cost_estimate=pl.CostEstimate(
-            flops=2 * rows * cols * slots * BLK, bytes_accessed=9 << 20, transcendentals=0
-        ),
-        name="alpha_partials",
+            flops=rows * cols * slots * BLK, bytes_accessed=12 << 20, transcendentals=0
+        ),
+        name="alpha_products",
     )(core, lists, sizes, pool, *operands)
 
 
-def to_their_rows(parts):
-    sent = [lax.ppermute(parts[d], "alpha", shift_x(X - d)) for d in range(1, X)]
-    return [parts[0], *sent]
+def alpha_sums(op, core, lists, sizes, gathered, own, near, far, after=()):
+    common = (core, lists, sizes, gathered, own, near, far)
+    (across,) = alpha_products(op, (2,), *common, after)
+    after_one, before_one, here = alpha_products(op, (1, 3, 0), *common, (across,))
+    from_across = lax.ppermute(across, "alpha", shift_x(X - 2))
+    sent = [
+        lax.ppermute(part, "alpha", shift_x(X - d)) for d, part in ((1, after_one), (3, before_one))
+    ]
+    return [fold(here, from_across), *sent]
+
+
+def fold_kernel(here_ref, other_ref, out_ref):
+    out_ref[...] = here_ref[...] + other_ref[...].astype(jnp.float32)
+
+
+def fold(here, other):
+    rows, cols = here.shape
+    by_rows = pl.BlockSpec((rows // 2, cols), lambda i: (i, 0))
+    return pl.pallas_call(
+        fold_kernel,
+        grid=(2,),
+        in_specs=[by_rows] * 2,
+        out_specs=by_rows,
+        out_shape=jax.ShapeDtypeStruct(here.shape, jnp.float32),
+        compiler_params=params(),
+        cost_estimate=pl.CostEstimate(flops=1 << 20, bytes_accessed=48 << 20, transcendentals=0),
+        name="fold",
+    )(here, other)
 
 
 def on_device(coeffs, a_blocks, a_list, a_count, b_blocks, b_list, b_count):
@@ -408,15 +426,14 @@
     d_one = beta_product(1, beta_place, beta_counts, pool_c, b_slots, (), jnp.bfloat16)
     c_along_z, d_one, near, far = lax.optimization_barrier((c_along_z, d_one, near, far))
 
-    inter_parts = alpha_partials(0, core, lists, sizes, c_along_z, a_slots, near, far)
-    sent = sum_pack(wanted, to_their_rows(inter_parts))
+    inter_parts = alpha_sums(0, core, lists, sizes, c_along_z, a_slots, near, far)
+    sent = sum_pack(wanted, inter_parts)
     pool_inter = lax.all_to_all(sent, "beta", split_axis=0, concat_axis=0, tiled=True)
 
     d_along_z = lax.all_gather(d_one, "alpha", axis=0, tiled=True, axis_index_groups=Z_GROUPS)
-    sigma_parts = alpha_partials(
+    sigma_one = alpha_sums(
         1, core, lists, sizes, d_along_z, a_slots, near, far, after=(sent,)
     )
-    sigma_one = to_their_rows(sigma_parts)
     return beta_product(0, beta_place, beta_counts, pool_inter, b_slots, sigma_one, jnp.float32)
 
 

time: 188 us -> 183 us (0.973)
  waiting for transfers between devices: 68.4 us -> 56.2 us
  Pallas kernels: 31.7 us -> 35.9 us
    all_to_all x2, waiting for transfers between devices: 21.7 us -> 11.5 us  [on_device(): lax.all_to_all(sent, 'beta', split_axis=0, concat_axis=0, tiled=True)]
    ppermute x6, waiting for transfers between devices: 23.1 us -> 13.8 us  [the longest x4 11.3 us: alpha_sums(): lax.ppermute(part, 'alpha', shift_x(X - d))]
    all_gather x1, waiting for transfers between devices: 10.7 us -> 17.9 us  [on_device(): lax.all_gather(d_one, 'alpha', axis=0, tiled=True, axis_index_groups=Z_GR...]
    pallas_call x2 -> x6, Pallas kernels: 14.7 us -> 20.4 us  [the longest x4 20.2 us: alpha_products(): pl.pallas_call(functools.partial(alpha_kernel, op, steps), grid_spec=pltp...]
  transfers between devices with their start and end apart: 16 -> 16, of which waited for: 8 -> 9; matrix products, arithmetic and copies ran while one was open for 3% -> 3% of each run, Pallas kernels for 14% -> 17%
where the time goes in v3:
time: 183 us; the launch traced here: 181 us
  starting transfers between devices  66.2 us (36%)
  waiting for transfers between devices  56.2 us (31%)
  Pallas kernels  35.9 us (20%)
  between operations  13.8 us (8%)
  local copies, waits for them, and re-layouts  5.16 us (3%)
  other arithmetic  3.9 us (2%)
    ppermute x3, starting transfers between devices, on_device(): far = [lax.ppermute(part, 'beta', SWAP_CORES) for part in near]  23.1 us
    pallas_call x4, Pallas kernels, alpha_products(): pl.pallas_call(functools.partial(alpha_kernel, op, steps), grid_spec=pltp...  20.2 us
    all_gather x1, waiting for transfers between devices, on_device(): lax.all_gather(d_one, 'alpha', axis=0, tiled=True, axis_index_groups=Z_GR...  17.9 us
    all_to_all x2, starting transfers between devices, on_device(): lax.all_to_all(sent, 'beta', split_axis=0, concat_axis=0, tiled=True)  17.9 us
    ppermute x1, waiting for transfers between devices, on_device(): near.append(lax.ppermute(a_half, 'alpha', shift_x(3)))  11.9 us
    all_to_all x2, waiting for transfers between devices, on_device(): lax.all_to_all(sent, 'beta', split_axis=0, concat_axis=0, tiled=True)  11.5 us
    ppermute x4, waiting for transfers between devices, alpha_sums(): lax.ppermute(part, 'alpha', shift_x(X - d))  11.3 us
    pallas_call x2, Pallas kernels, beta_product(): pl.pallas_call(functools.partial(beta_kernel, op), grid_spec=pltpu.Prefet...  10.8 us
  transfers between devices with their start and end apart: 16, of which 9 were waited for; matrix products, arithmetic and copies ran while one was open for 3% of the time, Pallas kernels for 17%

profile of v3, /device:TPU:1, one launch (start us, length us, event | category | flops | bytes accessed | tf_op | source)
XLA Modules:
  0.0 181.2 jit_solution(13438235817635999731)
XLA Ops:
  9.7 2.3 %pack.1 = bf16[32,256,128]{2,1,0:T(8,128)(2,1)} custom-call(s32[32]{0:T(128)S(1)} %reshape.170.wanted, bf16[256,1024]{1,0:T(8,128)(2,1)S(1)} %copy-done.3), custom_call_target="tpu_custom_call" | custom-call | bytes 5242880 | tf_op jit(solution)/shard_map/pack/pallas_call | solution.py:47
  12.0 11.2 %all-to-all-start = ((bf16[32,256,128]{2,1,0:T(8,128)(2,1)}), bf16[32,256,128]{2,1,0:T(8,128)(2,1)}, u32[]{:S(2)}, u32[]{:S(2)}) async-start(bf16[32,256,128]{2,1,0:T(8,128)(2,1)} %pack.1), calls=%async_computation | async-start | bytes 4194304 | tf_op jit(solution)/shard_map/all_to_all | solution.py:425
  29.5 3.3 %collective-permute-start = (bf16[11,256,128]{2,1,0:T(8,128)(2,1)S(1)}, bf16[11,256,128]{2,1,0:T(8,128)(2,1)S(1)}, u32[]{:S(2)}, u32[]{:S(2)}) collective-permute-start(bf16[11,256,128]{2,1,0:T(8,128)(2,1)S(1)} %dynamic-slice_bitcast_fusion), channel_id=1, source_target_pairs={{0,128},{16,144},{32,160},{48,176},{64,192},{80,208},{96,224},{112... | collective-permute-start | bytes 2162696 | tf_op jit(solution)/shard_map/ppermute | solution.py:415
  32.8 2.2 %collective-permute-start.1 = (bf16[11,256,128]{2,1,0:T(8,128)(2,1)S(1)}, bf16[11,256,128]{2,1,0:T(8,128)(2,1)S(1)}, u32[]{:S(2)}, u32[]{:S(2)}) collective-permute-start(bf16[11,256,128]{2,1,0:T(8,128)(2,1)S(1)} %dynamic-slice_bitcast_fusion), channel_id=1, source_target_pairs={{0,256},{16,272},{32,288},{48,304},{64,320},{80,336},{96,352},{112... | collective-permute-start | bytes 2162696 | tf_op jit(solution)/shard_map/ppermute | solution.py:415
  35.1 11.9 %collective-permute-done.2.rest_2_ = bf16[11,256,128]{2,1,0:T(8,128)(2,1)S(1)} collective-permute-done((bf16[11,256,128]{2,1,0:T(8,128)(2,1)S(1)}, bf16[11,256,128]{2,1,0:T(8,128)(2,1)S(1)}, u32[]{:S(2)}, u32[]{:S(2)}) %collective-permute-start.2) | collective-permute-done | bytes 720928 | tf_op jit(solution)/shard_map/ppermute | solution.py:419
  47.0 3.6 %collective-permute-start.5 = (bf16[11,256,128]{2,1,0:T(8,128)(2,1)S(1)}, bf16[11,256,128]{2,1,0:T(8,128)(2,1)}, u32[]{:S(2)}, u32[]{:S(2)}) collective-permute-start(bf16[11,256,128]{2,1,0:T(8,128)(2,1)S(1)} %collective-permute-done.2.rest_2_), channel_id=1, source_target_pairs={{0,1},{1,0},{2,3},{3,2},{4,5},{5,4},{6,7},{7,6},{8,9},{9,8},{10,11... | collective-permute-start | bytes 2162696 | tf_op jit(solution)/shard_map/ppermute | solution.py:420
  50.9 17.6 %collective-permute-start.3 = (bf16[11,256,128]{2,1,0:T(8,128)(2,1)S(1)}, bf16[11,256,128]{2,1,0:T(8,128)(2,1)S(1)}, u32[]{:S(2)}, u32[]{:S(2)}) collective-permute-start(bf16[11,256,128]{2,1,0:T(8,128)(2,1)S(1)} %collective-permute-done.rest_0_), channel_id=1, source_target_pairs={{0,1},{1,0},{2,3},{3,2},{4,5},{5,4},{6,7},{7,6},{8,9},{9,8},{10,11... | collective-permute-start | bytes 2162696 | tf_op jit(solution)/shard_map/ppermute | solution.py:420
  72.2 5.3 %beta_product.2 = bf16[256,1024]{1,0:T(8,128)(2,1)} custom-call(s32[2,8,11]{2,1,0:T(8,128)S(1)} %convert_add_fusion.place, s32[2,8]{1,0:T(2,128)S(1)} %constant_dynamic-slice_fusion.1.count, bf16[32,256,128]{2,1,0:T(8,128)(2,1)} %all-to-all-done.pool_any, bf16[2,11,1024,128]{3,2,1,0:T(8,128)(2,1)} %bitcast.24), custom_call_target="tpu_custom_call" | custom-call | flops 738197504 | bytes 7340032 | tf_op jit(solution)/shard_map/beta_product/pallas_call | solution.py:179
  77.7 3.7 %alpha_products.4.rest_6_ = bf16[256,1024]{1,0:T(8,128)(2,1)S(1)} custom-call(s32[1]{0:T(128)} %bitcast.8.core, s32[2,8,11]{2,1,0:T(8,128)S(1)} %bitcast.16, s32[2,8]{1,0:T(2,128)S(1)} %reshape.169.sizes, bf16[16,128,1024]{2,1,0:T(8,128)(2,1)} %bitcast.26, bf16[2,11,256,128]{3,2,1,0:T(8,128)(2,1)} %bitcast.20, ...), custom_call_target="tpu_custom_call" | custom-call | flops 369098752 | bytes 12582912 | tf_op jit(solution)/shard_map/alpha_products/pallas_call | solution.py:311
  83.6 6.4 %alpha_products.5 = (bf16[256,1024]{1,0:T(8,128)(2,1)S(1)}, bf16[256,1024]{1,0:T(8,128)(2,1)S(1)}, f32[256,1024]{1,0:T(8,128)}) custom-call(s32[1]{0:T(128)} %bitcast.8.core, s32[2,8,11]{2,1,0:T(8,128)S(1)} %bitcast.17, s32[2,8]{1,0:T(2,128)S(1)} %reshape.169.sizes, bf16[16,128,1024]{2,1,0:T(8,128)(2,1)} %bitcast.27, bf16[2,11,256,128]{3,2,1,0:T(8,128)(2,1)} %bitcast.21, ...), custom_call_target="tpu_custom_call" | custom-call | flops 369098752 | bytes 12582912 | tf_op jit(solution)/shard_map/alpha_products/pallas_call | solution.py:311
  90.0 2.7 %collective-permute-start.7 = (bf16[256,1024]{1,0:T(8,128)(2,1)S(1)}, bf16[256,1024]{1,0:T(8,128)(2,1)S(1)}, u32[]{:S(2)}, u32[]{:S(2)}) collective-permute-start(bf16[256,1024]{1,0:T(8,128)(2,1)S(1)} %get-tuple-element.37), channel_id=1, source_target_pairs={{0,384},{16,400},{32,416},{48,432},{64,448},{80,464},{96,480},{112... | collective-permute-start | bytes 1572872 | tf_op jit(solution)/shard_map/ppermute | solution.py:342
  92.8 2.7 %collective-permute-start.8 = (bf16[256,1024]{1,0:T(8,128)(2,1)S(1)}, bf16[256,1024]{1,0:T(8,128)(2,1)S(1)}, u32[]{:S(2)}, u32[]{:S(2)}) collective-permute-start(bf16[256,1024]{1,0:T(8,128)(2,1)S(1)} %get-tuple-element.38), channel_id=1, source_target_pairs={{0,128},{16,144},{32,160},{48,176},{64,192},{80,208},{96,224},{112... | collective-permute-start | bytes 1572872 | tf_op jit(solution)/shard_map/ppermute | solution.py:342
  95.5 2.4 %collective-permute-done.6.other_ref = bf16[256,1024]{1,0:T(8,128)(2,1)S(1)} collective-permute-done((bf16[256,1024]{1,0:T(8,128)(2,1)S(1)}, bf16[256,1024]{1,0:T(8,128)(2,1)S(1)}, u32[]{:S(2)}, u32[]{:S(2)}) %collective-permute-start.6) | collective-permute-done | bytes 524320 | tf_op jit(solution)/shard_map/ppermute | solution.py:340
  99.3 7.7 %collective-permute-done.7.refs_1_ = bf16[256,1024]{1,0:T(8,128)(2,1)S(1)} collective-permute-done((bf16[256,1024]{1,0:T(8,128)(2,1)S(1)}, bf16[256,1024]{1,0:T(8,128)(2,1)S(1)}, u32[]{:S(2)}, u32[]{:S(2)}) %collective-permute-start.7) | collective-permute-done | bytes 524320 | tf_op jit(solution)/shard_map/ppermute | solution.py:342
  108.9 2.5 %sum_pack.1.rest_6_ = bf16[32,256,128]{2,1,0:T(8,128)(2,1)} custom-call(s32[32]{0:T(128)S(1)} %reshape.170.wanted, f32[256,1024]{1,0:T(8,128)S(1)} %fold.2.refs_0_, bf16[256,1024]{1,0:T(8,128)(2,1)S(1)} %collective-permute-done.7.refs_1_, bf16[256,1024]{1,0:T(8,128)(2,1)S(1)} %collective-permute-done.8.refs_2_), custom_call_target="tpu_custom_call" | custom-call | flops 1048576 | bytes 6291456 | tf_op jit(solution)/shard_map/sum_pack/pallas_call | solution.py:90
  111.4 6.7 %all-to-all-start.1 = ((bf16[32,256,128]{2,1,0:T(8,128)(2,1)}), bf16[32,256,128]{2,1,0:T(8,128)(2,1)}, u32[]{:S(2)}, u32[]{:S(2)}) async-start(bf16[32,256,128]{2,1,0:T(8,128)(2,1)} %sum_pack.1.rest_6_), calls=%async_computation.1 | async-start | bytes 4194304 | tf_op jit(solution)/shard_map/all_to_all | solution.py:431
  118.2 17.9 %all-gather.5.cloned.1.call-done = bf16[2048,1024]{1,0:T(8,128)(2,1)} async-done(((bf16[256,1024]{1,0:T(8,128)(2,1)}), bf16[2048,1024]{1,0:T(8,128)(2,1)}) %all-gather.5.cloned.1.call-update) | async-done | bytes 4194320 | tf_op jit(solution)/shard_map/all_gather | solution.py:433
  136.1 3.7 %alpha_products.6.rest_6_ = bf16[256,1024]{1,0:T(8,128)(2,1)S(1)} custom-call(s32[1]{0:T(128)} %bitcast.8.core, s32[2,8,11]{2,1,0:T(8,128)S(1)} %bitcast.18, s32[2,8]{1,0:T(2,128)S(1)} %reshape.169.sizes, bf16[16,128,1024]{2,1,0:T(8,128)(2,1)} %bitcast.28, bf16[2,11,256,128]{3,2,1,0:T(8,128)(2,1)} %bitcast.22, ...), custom_call_target="tpu_custom_call" | custom-call | flops 369098752 | bytes 12582912 | tf_op jit(solution)/shard_map/alpha_products/pallas_call | solution.py:311
  139.8 4.6 %collective-permute-start.9 = (bf16[256,1024]{1,0:T(8,128)(2,1)S(1)}, bf16[256,1024]{1,0:T(8,128)(2,1)S(1)}, u32[]{:S(2)}, u32[]{:S(2)}) collective-permute-start(bf16[256,1024]{1,0:T(8,128)(2,1)S(1)} %alpha_products.6.rest_6_), channel_id=1, source_target_pairs={{0,256},{16,272},{32,288},{48,304},{64,320},{80,336},{96,352},{112... | collective-permute-start | bytes 1572872 | tf_op jit(solution)/shard_map/ppermute | solution.py:340
  144.4 6.3 %alpha_products.7 = (bf16[256,1024]{1,0:T(8,128)(2,1)S(1)}, bf16[256,1024]{1,0:T(8,128)(2,1)S(1)}, f32[256,1024]{1,0:T(8,128)}) custom-call(s32[1]{0:T(128)} %bitcast.8.core, s32[2,8,11]{2,1,0:T(8,128)S(1)} %bitcast.19, s32[2,8]{1,0:T(2,128)S(1)} %reshape.169.sizes, bf16[16,128,1024]{2,1,0:T(8,128)(2,1)} %bitcast.29, bf16[2,11,256,128]{3,2,1,0:T(8,128)(2,1)} %bitcast.23, ...), custom_call_target="tpu_custom_call" | custom-call | flops 369098752 | bytes 12582912 | tf_op jit(solution)/shard_map/alpha_products/pallas_call | solution.py:311
  150.8 2.9 %collective-permute-start.10 = (bf16[256,1024]{1,0:T(8,128)(2,1)S(1)}, bf16[256,1024]{1,0:T(8,128)(2,1)S(1)}, u32[]{:S(2)}, u32[]{:S(2)}) collective-permute-start(bf16[256,1024]{1,0:T(8,128)(2,1)S(1)} %get-tuple-element.41), channel_id=1, source_target_pairs={{0,384},{16,400},{32,416},{48,432},{64,448},{80,464},{96,480},{112... | collective-permute-start | bytes 1572872 | tf_op jit(solution)/shard_map/ppermute | solution.py:342
  153.6 2.4 %collective-permute-start.11 = (bf16[256,1024]{1,0:T(8,128)(2,1)S(1)}, bf16[256,1024]{1,0:T(8,128)(2,1)S(1)}, u32[]{:S(2)}, u32[]{:S(2)}) collective-permute-start(bf16[256,1024]{1,0:T(8,128)(2,1)S(1)} %get-tuple-element.42), channel_id=1, source_target_pairs={{0,128},{16,144},{32,160},{48,176},{64,192},{80,208},{96,224},{112... | collective-permute-start | bytes 1572872 | tf_op jit(solution)/shard_map/ppermute | solution.py:342
  157.5 9.8 %all-to-all-done.1.pool_any = bf16[32,256,128]{2,1,0:T(8,128)(2,1)} async-done(((bf16[32,256,128]{2,1,0:T(8,128)(2,1)}), bf16[32,256,128]{2,1,0:T(8,128)(2,1)}, u32[]{:S(2)}, u32[]{:S(2)}) %all-to-all-start.1) | async-done | bytes 2097184 | tf_op jit(solution)/shard_map/all_to_all | solution.py:431
  168.9 5.4 %beta_product.3 = f32[256,1024]{1,0:T(8,128)} custom-call(s32[2,8,11]{2,1,0:T(8,128)S(1)} %convert_add_fusion.place, s32[2,8]{1,0:T(2,128)S(1)} %constant_dynamic-slice_fusion.1.count, bf16[32,256,128]{2,1,0:T(8,128)(2,1)} %all-to-all-done.1.pool_any, bf16[2,11,1024,128]{3,2,1,0:T(8,128)(2,1)} %bitcast.25, f32[256,1024]{1,0:T(8,128)S(1)} %fold.3.rest_0_, ...), custom_call_target="tpu_custom_call" | custom-call | flops 738197504 | bytes 7340032 | tf_op jit(solution)/shard_map/beta_product/pallas_call | solution.py:179
  (77 shorter events, 21.9 us)
Async XLA Ops:
  6.5 20.7 %copy-start = (s32[2,128]{1,0:T(2,128)S(1)}, s32[2,128]{1,0:T(2,128)}, u32[]{:S(2)}) copy-start(s32[2,128]{1,0:T(2,128)} %param.13) | copy-start | bytes 3076
  6.5 71.1 %all-gather.3.cloned.1.call-start = ((), (), s32[]{:S(2)}) async-start(), calls=%async_computation.2 | async-start | bytes 4718592 | tf_op jit(solution)/shard_map/all_gather | solution.py:423
  11.9 11.3 %copy-start.8 = (s32[2,64,11]{1,0,2:T(2,128)S(1)}, s32[2,64,11]{1,0,2:T(2,128)}, u32[]{:S(2)}) copy-start(s32[2,64,11]{1,0,2:T(2,128)} %param.9) | copy-start | bytes 16900
  11.9 11.4 %copy-start.9 = (s32[2,64]{1,0:T(2,128)S(1)}, s32[2,64]{1,0:T(2,128)}, u32[]{:S(2)}) copy-start(s32[2,64]{1,0:T(2,128)} %param.10) | copy-start | bytes 1540
  11.9 14.2 %copy-start.7 = (s32[2,128,11]{1,0,2:T(2,128)S(1)}, s32[2,128,11]{1,0,2:T(2,128)}, u32[]{:S(2)}) copy-start(s32[2,128,11]{1,0,2:T(2,128)} %param.12) | copy-start | bytes 33796
  12.0 15.5 %copy-start.6 = (bf16[2,256,11,128]{3,1,2,0:T(8,128)(2,1)S(1)}, bf16[2,256,11,128]{3,1,2,0:T(8,128)(2,1)}, u32[]{:S(2)}) copy-start(bf16[2,256,11,128]{3,1,2,0:T(8,128)(2,1)} %param.8) | copy-start | bytes 4325380
  12.0 60.3 %all-to-all-start = ((bf16[32,256,128]{2,1,0:T(8,128)(2,1)}), bf16[32,256,128]{2,1,0:T(8,128)(2,1)}, u32[]{:S(2)}, u32[]{:S(2)}) async-start(bf16[32,256,128]{2,1,0:T(8,128)(2,1)} %pack.1), calls=%async_computation | async-start | bytes 4194304 | tf_op jit(solution)/shard_map/all_to_all | solution.py:425
  23.2 112.9 %all-gather.5.cloned.1.call-start = ((), (), s32[]{:S(2)}) async-start(), calls=%async_computation.3 | async-start | bytes 4718592 | tf_op jit(solution)/shard_map/all_gather | solution.py:433
  27.5 19.4 %collective-permute-start.2 = (bf16[11,256,128]{2,1,0:T(8,128)(2,1)S(1)}, bf16[11,256,128]{2,1,0:T(8,128)(2,1)S(1)}, u32[]{:S(2)}, u32[]{:S(2)}) collective-permute-start(bf16[11,256,128]{2,1,0:T(8,128)(2,1)S(1)} %dynamic-slice_bitcast_fusion), channel_id=1, source_target_pairs={{0,384},{16,400},{32,416},{48,432},{64,448},{80,464},{96,480},{112... | collective-permute-start | bytes 2162696 | tf_op jit(solution)/shard_map/ppermute | solution.py:419
  29.5 21.4 %collective-permute-start = (bf16[11,256,128]{2,1,0:T(8,128)(2,1)S(1)}, bf16[11,256,128]{2,1,0:T(8,128)(2,1)S(1)}, u32[]{:S(2)}, u32[]{:S(2)}) collective-permute-start(bf16[11,256,128]{2,1,0:T(8,128)(2,1)S(1)} %dynamic-slice_bitcast_fusion), channel_id=1, source_target_pairs={{0,128},{16,144},{32,160},{48,176},{64,192},{80,208},{96,224},{112... | collective-permute-start | bytes 2162696 | tf_op jit(solution)/shard_map/ppermute | solution.py:415
  32.8 35.7 %collective-permute-start.1 = (bf16[11,256,128]{2,1,0:T(8,128)(2,1)S(1)}, bf16[11,256,128]{2,1,0:T(8,128)(2,1)S(1)}, u32[]{:S(2)}, u32[]{:S(2)}) collective-permute-start(bf16[11,256,128]{2,1,0:T(8,128)(2,1)S(1)} %dynamic-slice_bitcast_fusion), channel_id=1, source_target_pairs={{0,256},{16,272},{32,288},{48,304},{64,320},{80,336},{96,352},{112... | collective-permute-start | bytes 2162696 | tf_op jit(solution)/shard_map/ppermute | solution.py:415
  47.0 30.6 %collective-permute-start.5 = (bf16[11,256,128]{2,1,0:T(8,128)(2,1)S(1)}, bf16[11,256,128]{2,1,0:T(8,128)(2,1)}, u32[]{:S(2)}, u32[]{:S(2)}) collective-permute-start(bf16[11,256,128]{2,1,0:T(8,128)(2,1)S(1)} %collective-permute-done.2.rest_2_), channel_id=1, source_target_pairs={{0,1},{1,0},{2,3},{3,2},{4,5},{5,4},{6,7},{7,6},{8,9},{9,8},{10,11... | collective-permute-start | bytes 2162696 | tf_op jit(solution)/shard_map/ppermute | solution.py:420
  50.9 26.7 %collective-permute-start.3 = (bf16[11,256,128]{2,1,0:T(8,128)(2,1)S(1)}, bf16[11,256,128]{2,1,0:T(8,128)(2,1)S(1)}, u32[]{:S(2)}, u32[]{:S(2)}) collective-permute-start(bf16[11,256,128]{2,1,0:T(8,128)(2,1)S(1)} %collective-permute-done.rest_0_), channel_id=1, source_target_pairs={{0,1},{1,0},{2,3},{3,2},{4,5},{5,4},{6,7},{7,6},{8,9},{9,8},{10,11... | collective-permute-start | bytes 2162696 | tf_op jit(solution)/shard_map/ppermute | solution.py:420
  68.5 9.1 %collective-permute-start.4 = (bf16[11,256,128]{2,1,0:T(8,128)(2,1)S(1)}, bf16[11,256,128]{2,1,0:T(8,128)(2,1)}, u32[]{:S(2)}, u32[]{:S(2)}) collective-permute-start(bf16[11,256,128]{2,1,0:T(8,128)(2,1)S(1)} %collective-permute-done.1.rest_1_), channel_id=1, source_target_pairs={{0,1},{1,0},{2,3},{3,2},{4,5},{5,4},{6,7},{7,6},{8,9},{9,8},{10,11... | collective-permute-start | bytes 2162696 | tf_op jit(solution)/shard_map/ppermute | solution.py:420
  77.6 3.8 %copy-start.1 = (bf16[11,256,128]{2,1,0:T(8,128)(2,1)}, bf16[11,256,128]{2,1,0:T(8,128)(2,1)S(1)}, u32[]{:S(2)}) copy-start(bf16[11,256,128]{2,1,0:T(8,128)(2,1)S(1)} %collective-permute-done.3.rest_3_) | copy-start | bytes 2162692
  81.4 16.5 %collective-permute-start.6 = (bf16[256,1024]{1,0:T(8,128)(2,1)S(1)}, bf16[256,1024]{1,0:T(8,128)(2,1)S(1)}, u32[]{:S(2)}, u32[]{:S(2)}) collective-permute-start(bf16[256,1024]{1,0:T(8,128)(2,1)S(1)} %alpha_products.4.rest_6_), channel_id=1, source_target_pairs={{0,256},{16,272},{32,288},{48,304},{64,320},{80,336},{96,352},{112... | collective-permute-start | bytes 1572872 | tf_op jit(solution)/shard_map/ppermute | solution.py:340
  90.0 17.0 %collective-permute-start.7 = (bf16[256,1024]{1,0:T(8,128)(2,1)S(1)}, bf16[256,1024]{1,0:T(8,128)(2,1)S(1)}, u32[]{:S(2)}, u32[]{:S(2)}) collective-permute-start(bf16[256,1024]{1,0:T(8,128)(2,1)S(1)} %get-tuple-element.37), channel_id=1, source_target_pairs={{0,384},{16,400},{32,416},{48,432},{64,448},{80,464},{96,480},{112... | collective-permute-start | bytes 1572872 | tf_op jit(solution)/shard_map/ppermute | solution.py:342
  92.8 16.1 %collective-permute-start.8 = (bf16[256,1024]{1,0:T(8,128)(2,1)S(1)}, bf16[256,1024]{1,0:T(8,128)(2,1)S(1)}, u32[]{:S(2)}, u32[]{:S(2)}) collective-permute-start(bf16[256,1024]{1,0:T(8,128)(2,1)S(1)} %get-tuple-element.38), channel_id=1, source_target_pairs={{0,128},{16,144},{32,160},{48,176},{64,192},{80,208},{96,224},{112... | collective-permute-start | bytes 1572872 | tf_op jit(solution)/shard_map/ppermute | solution.py:342
  97.9 1.2 copy-start.5
  111.4 24.7 %copy-start.2 = (bf16[11,256,128]{2,1,0:T(8,128)(2,1)S(1)}, bf16[11,256,128]{2,1,0:T(8,128)(2,1)}, u32[]{:S(2)}) copy-start(bf16[11,256,128]{2,1,0:T(8,128)(2,1)} %copy-done.1) | copy-start | bytes 2162692
  111.4 55.8 %all-to-all-start.1 = ((bf16[32,256,128]{2,1,0:T(8,128)(2,1)}), bf16[32,256,128]{2,1,0:T(8,128)(2,1)}, u32[]{:S(2)}, u32[]{:S(2)}) async-start(bf16[32,256,128]{2,1,0:T(8,128)(2,1)} %sum_pack.1.rest_6_), calls=%async_computation.1 | async-start | bytes 4194304 | tf_op jit(solution)/shard_map/all_to_all | solution.py:431
  139.8 16.3 %collective-permute-start.9 = (bf16[256,1024]{1,0:T(8,128)(2,1)S(1)}, bf16[256,1024]{1,0:T(8,128)(2,1)S(1)}, u32[]{:S(2)}, u32[]{:S(2)}) collective-permute-start(bf16[256,1024]{1,0:T(8,128)(2,1)S(1)} %alpha_products.6.rest_6_), channel_id=1, source_target_pairs={{0,256},{16,272},{32,288},{48,304},{64,320},{80,336},{96,352},{112... | collective-permute-start | bytes 1572872 | tf_op jit(solution)/shard_map/ppermute | solution.py:340
  150.8 16.4 %collective-permute-start.10 = (bf16[256,1024]{1,0:T(8,128)(2,1)S(1)}, bf16[256,1024]{1,0:T(8,128)(2,1)S(1)}, u32[]{:S(2)}, u32[]{:S(2)}) collective-permute-start(bf16[256,1024]{1,0:T(8,128)(2,1)S(1)} %get-tuple-element.41), channel_id=1, source_target_pairs={{0,384},{16,400},{32,416},{48,432},{64,448},{80,464},{96,480},{112... | collective-permute-start | bytes 1572872 | tf_op jit(solution)/shard_map/ppermute | solution.py:342
  153.6 15.3 %collective-permute-start.11 = (bf16[256,1024]{1,0:T(8,128)(2,1)S(1)}, bf16[256,1024]{1,0:T(8,128)(2,1)S(1)}, u32[]{:S(2)}, u32[]{:S(2)}) collective-permute-start(bf16[256,1024]{1,0:T(8,128)(2,1)S(1)} %get-tuple-element.42), channel_id=1, source_target_pairs={{0,128},{16,144},{32,160},{48,176},{64,192},{80,208},{96,224},{112... | collective-permute-start | bytes 1572872 | tf_op jit(solution)/shard_map/ppermute | solution.py:342
  (2 other events, 2.3 us)
Sparse Core Ops, SparseCore 0:
  9.4 63.7 all-gather.2
  77.8 58.2 all-gather.4

commit v4 on v3

--- a/solution.py
+++ b/solution.py
@@ -25,8 +25,8 @@
 SWAP_CORES = [(y * CORES + c, y * CORES + 1 - c) for y in range(Y) for c in range(CORES)]
 
 
-def params():
-    return pltpu.CompilerParams(vmem_limit_bytes=VMEM_LIMIT)
+def params(limit=VMEM_LIMIT):
+    return pltpu.CompilerParams(vmem_limit_bytes=limit)
 
 
 def pack_kernel(wanted, c_ref, out_ref, blocks, sems):
@@ -57,7 +57,7 @@
             ],
         ),
         out_shape=jax.ShapeDtypeStruct((total, rows, BLK), c.dtype),
-        compiler_params=params(),
+        compiler_params=params(60 * 1024 * 1024),
         cost_estimate=pl.CostEstimate(flops=0, bytes_accessed=5 << 20, transcendentals=0),
         name="pack",
     )(wanted, c)
@@ -205,20 +205,15 @@
 
 
 FEW = 6
-POOL_COPIES = 4
 
 
 def alpha_kernel(op, steps, core, lists, sizes, pool_any, own, *rest):
     near, far = rest[: X - 1], rest[X - 1 : 2 * (X - 1)]
     outs = rest[-len(steps) - 6 : -6]
-    factors, pool_ref, results, factor_sems, pool_sems, out_sems = rest[-6:]
+    factors, listed_blocks, results, factor_sems, block_sems, out_sems = rest[-6:]
     row_count, slots, _, _ = factors.shape
     blocks = row_count // len(steps)
-    pool_blocks = pool_ref.shape[0]
-
-    def pool_copy(i):
-        span = pl.ds(i * (pool_blocks // POOL_COPIES), pool_blocks // POOL_COPIES)
-        return pltpu.make_async_copy(pool_any.at[span], pool_ref.at[span], pool_sems.at[i])
+    pool_blocks = pool_any.shape[0]
 
     def out_copy(i):
         return pltpu.make_async_copy(results[i], outs[i], out_sems.at[i])
@@ -228,17 +223,20 @@
             listed, row = steps[i] * blocks + b, i * blocks + b
 
             def start(q, carry):
+                code = lists[op, listed, q]
                 pltpu.make_async_copy(
-                    source.at[lists[op, listed, q] // pool_blocks, pl.ds(b * BLK, BLK), :],
+                    pool_any.at[code % pool_blocks],
+                    listed_blocks.at[row, q],
+                    block_sems.at[row, q],
+                ).start()
+                pltpu.make_async_copy(
+                    source.at[code // pool_blocks, pl.ds(b * BLK, BLK), :],
                     factors.at[row, q],
                     factor_sems.at[row, q],
                 ).start()
                 return carry
 
             lax.fori_loop(0, sizes[op, listed], start, 0)
-
-    for i in range(POOL_COPIES):
-        pool_copy(i).start()
 
     @pl.when(core[0] == op)
     def _():
@@ -263,12 +261,13 @@
             pltpu.make_async_copy(
                 own.at[op, 0, pl.ds(0, BLK), :], factors.at[row, q], factor_sems.at[row, q]
             ).wait()
+            pltpu.make_async_copy(
+                pool_any.at[0], listed_blocks.at[row, q], block_sems.at[row, q]
+            ).wait()
             return carry
 
         lax.fori_loop(0, sizes[op, listed], arrive, 0)
         largest = jnp.maximum(largest, sizes[op, listed])
-    for i in range(POOL_COPIES):
-        pool_copy(i).wait()
 
     def multiply(depth):
         for i, t in enumerate(steps):
@@ -279,7 +278,12 @@
                     jnp.where(q < size, factors[row, q], jnp.zeros((), factors.dtype))
                     for q in range(depth)
                 ]
-                right = [pool_ref[lists[op, listed, q] % pool_blocks] for q in range(depth)]
+                right = [
+                    jnp.where(
+                        q < size, listed_blocks[row, q], jnp.zeros((), listed_blocks.dtype)
+                    )
+                    for q in range(depth)
+                ]
                 total = jnp.dot(
                     jnp.concatenate(left, axis=1),
                     jnp.concatenate(right, axis=0),
@@ -317,10 +321,10 @@
             out_specs=[anywhere] * len(steps),
             scratch_shapes=[
                 pltpu.VMEM((row_count, slots, BLK, BLK), own.dtype),
-                pltpu.VMEM(pool.shape, pool.dtype),
+                pltpu.VMEM((row_count, slots, BLK, cols), pool.dtype),
                 [pltpu.VMEM((rows, cols), kind) for kind in types],
                 pltpu.SemaphoreType.DMA((row_count, slots)),
-                pltpu.SemaphoreType.DMA((POOL_COPIES,)),
+                pltpu.SemaphoreType.DMA((row_count, slots)),
                 pltpu.SemaphoreType.DMA((len(steps),)),
             ],
         ),
@@ -336,7 +340,8 @@
 def alpha_sums(op, core, lists, sizes, gathered, own, near, far, after=()):
     common = (core, lists, sizes, gathered, own, near, far)
     (across,) = alpha_products(op, (2,), *common, after)
-    after_one, before_one, here = alpha_products(op, (1, 3, 0), *common, (across,))
+    after_one, before_one = alpha_products(op, (1, 3), *common, (across,))
+    (here,) = alpha_products(op, (0,), *common, (after_one,))
     from_across = lax.ppermute(across, "alpha", shift_x(X - 2))
     sent = [
         lax.ppermute(part, "alpha", shift_x(X - d)) for d, part in ((1, after_one), (3, before_one))
@@ -344,23 +349,26 @@
     return [fold(here, from_across), *sent]
 
 
-def fold_kernel(here_ref, other_ref, out_ref):
-    out_ref[...] = here_ref[...] + other_ref[...].astype(jnp.float32)
-
-
-def fold(here, other):
-    rows, cols = here.shape
+def fold_kernel(first_ref, *refs):
+    total = first_ref[...]
+    for ref in refs[:-1]:
+        total += ref[...].astype(jnp.float32)
+    refs[-1][...] = total
+
+
+def fold(first, *others):
+    rows, cols = first.shape
     by_rows = pl.BlockSpec((rows // 2, cols), lambda i: (i, 0))
     return pl.pallas_call(
         fold_kernel,
         grid=(2,),
-        in_specs=[by_rows] * 2,
+        in_specs=[by_rows] * (1 + len(others)),
         out_specs=by_rows,
-        out_shape=jax.ShapeDtypeStruct(here.shape, jnp.float32),
+        out_shape=jax.ShapeDtypeStruct(first.shape, jnp.float32),
         compiler_params=params(),
         cost_estimate=pl.CostEstimate(flops=1 << 20, bytes_accessed=48 << 20, transcendentals=0),
         name="fold",
-    )(here, other)
+    )(first, *others)
 
 
 def on_device(coeffs, a_blocks, a_list, a_count, b_blocks, b_list, b_count):
@@ -431,10 +439,11 @@
     pool_inter = lax.all_to_all(sent, "beta", split_axis=0, concat_axis=0, tiled=True)
 
     d_along_z = lax.all_gather(d_one, "alpha", axis=0, tiled=True, axis_index_groups=Z_GROUPS)
-    sigma_one = alpha_sums(
+    sigma_here, *sigma_sent = alpha_sums(
         1, core, lists, sizes, d_along_z, a_slots, near, far, after=(sent,)
     )
-    return beta_product(0, beta_place, beta_counts, pool_inter, b_slots, sigma_one, jnp.float32)
+    sigma = beta_product(0, beta_place, beta_counts, pool_inter, b_slots, (sigma_here,), jnp.float32)
+    return fold(sigma, *sigma_sent)
 
 
 def solution(mesh):

time: 183 us -> 181 us (0.989)
  Pallas kernels: 35.9 us -> 42.1 us
  waiting for transfers between devices: 56.2 us -> 51.2 us
    pallas_call x4 -> x6, Pallas kernels: 20.2 us -> 24.7 us  [alpha_products(): pl.pallas_call(functools.partial(alpha_kernel, op, steps), grid_spec=pltp...]
    all_to_all x2, waiting for transfers between devices: 11.5 us -> 8.96 us  [on_device(): lax.all_to_all(sent, 'beta', split_axis=0, concat_axis=0, tiled=True)]
    ppermute x2, waiting for transfers between devices: 2.43 us -> 0.49 us  [alpha_sums(): from_across = lax.ppermute(across, 'alpha', shift_x(X - 2))]
    unnamed x22 -> x24, local copies, waits for them, and re-layouts: 3.73 us -> 2.7 us
  transfers between devices with their start and end apart: 16 -> 16, of which waited for: 9 -> 8; matrix products, arithmetic and copies ran while one was open for 3% -> 3% of each run, Pallas kernels for 17% -> 23%
where the time goes in v4:
time: 181 us; the launch traced here: 180 us
  starting transfers between devices  64.7 us (36%)
  waiting for transfers between devices  51.2 us (28%)
  Pallas kernels  42.1 us (23%)
  between operations  13.9 us (8%)
  local copies, waits for them, and re-layouts  4.64 us (3%)
  other arithmetic  3.9 us (2%)
    pallas_call x6, Pallas kernels, alpha_products(): pl.pallas_call(functools.partial(alpha_kernel, op, steps), grid_spec=pltp...  24.7 us
    ppermute x3, starting transfers between devices, on_device(): far = [lax.ppermute(part, 'beta', SWAP_CORES) for part in near]  23.1 us
    all_gather x1, waiting for transfers between devices, on_device(): lax.all_gather(d_one, 'alpha', axis=0, tiled=True, axis_index_groups=Z_GR...  18.2 us
    all_to_all x2, starting transfers between devices, on_device(): lax.all_to_all(sent, 'beta', split_axis=0, concat_axis=0, tiled=True)  16.7 us
    ppermute x1, waiting for transfers between devices, on_device(): near.append(lax.ppermute(a_half, 'alpha', shift_x(3)))  11.9 us
    ppermute x4, waiting for transfers between devices, alpha_sums(): lax.ppermute(part, 'alpha', shift_x(X - d))  10.6 us
    ppermute x4, starting transfers between devices, alpha_sums(): lax.ppermute(part, 'alpha', shift_x(X - d))  10.6 us
    pallas_call x2, Pallas kernels, beta_product(): pl.pallas_call(functools.partial(beta_kernel, op), grid_spec=pltpu.Prefet...  10.2 us
  transfers between devices with their start and end apart: 16, of which 8 were waited for; matrix products, arithmetic and copies ran while one was open for 3% of the time, Pallas kernels for 23%

profile of v4, /device:TPU:1, one launch (start us, length us, event | category | flops | bytes accessed | tf_op | source)
XLA Modules:
  0.0 180.4 jit_solution(7201783783402868896)
XLA Ops:
  9.1 3.4 %pack.1 = bf16[32,256,128]{2,1,0:T(8,128)(2,1)} custom-call(s32[32]{0:T(128)} %reshape.172.wanted, bf16[256,1024]{1,0:T(8,128)(2,1)} %c_ref.1), custom_call_target="tpu_custom_call" | custom-call | bytes 5242880 | tf_op jit(solution)/shard_map/pack/pallas_call | solution.py:47
  12.6 11.2 %all-to-all-start = ((bf16[32,256,128]{2,1,0:T(8,128)(2,1)}), bf16[32,256,128]{2,1,0:T(8,128)(2,1)}, u32[]{:S(2)}, u32[]{:S(2)}) async-start(bf16[32,256,128]{2,1,0:T(8,128)(2,1)} %pack.1), calls=%async_computation | async-start | bytes 4194304 | tf_op jit(solution)/shard_map/all_to_all | solution.py:433
  30.1 3.3 %collective-permute-start = (bf16[11,256,128]{2,1,0:T(8,128)(2,1)S(1)}, bf16[11,256,128]{2,1,0:T(8,128)(2,1)S(1)}, u32[]{:S(2)}, u32[]{:S(2)}) collective-permute-start(bf16[11,256,128]{2,1,0:T(8,128)(2,1)S(1)} %dynamic-slice_bitcast_fusion), channel_id=1, source_target_pairs={{0,128},{16,144},{32,160},{48,176},{64,192},{80,208},{96,224},{112... | collective-permute-start | bytes 2162696 | tf_op jit(solution)/shard_map/ppermute | solution.py:423
  33.5 2.2 %collective-permute-start.1 = (bf16[11,256,128]{2,1,0:T(8,128)(2,1)S(1)}, bf16[11,256,128]{2,1,0:T(8,128)(2,1)S(1)}, u32[]{:S(2)}, u32[]{:S(2)}) collective-permute-start(bf16[11,256,128]{2,1,0:T(8,128)(2,1)S(1)} %dynamic-slice_bitcast_fusion), channel_id=1, source_target_pairs={{0,256},{16,272},{32,288},{48,304},{64,320},{80,336},{96,352},{112... | collective-permute-start | bytes 2162696 | tf_op jit(solution)/shard_map/ppermute | solution.py:423
  35.7 11.9 %collective-permute-done.2.rest_2_ = bf16[11,256,128]{2,1,0:T(8,128)(2,1)S(1)} collective-permute-done((bf16[11,256,128]{2,1,0:T(8,128)(2,1)S(1)}, bf16[11,256,128]{2,1,0:T(8,128)(2,1)S(1)}, u32[]{:S(2)}, u32[]{:S(2)}) %collective-permute-start.2) | collective-permute-done | bytes 720928 | tf_op jit(solution)/shard_map/ppermute | solution.py:427
  47.6 3.6 %collective-permute-start.5 = (bf16[11,256,128]{2,1,0:T(8,128)(2,1)S(1)}, bf16[11,256,128]{2,1,0:T(8,128)(2,1)}, u32[]{:S(2)}, u32[]{:S(2)}) collective-permute-start(bf16[11,256,128]{2,1,0:T(8,128)(2,1)S(1)} %collective-permute-done.2.rest_2_), channel_id=1, source_target_pairs={{0,1},{1,0},{2,3},{3,2},{4,5},{5,4},{6,7},{7,6},{8,9},{9,8},{10,11... | collective-permute-start | bytes 2162696 | tf_op jit(solution)/shard_map/ppermute | solution.py:428
  51.5 17.6 %collective-permute-start.3 = (bf16[11,256,128]{2,1,0:T(8,128)(2,1)S(1)}, bf16[11,256,128]{2,1,0:T(8,128)(2,1)S(1)}, u32[]{:S(2)}, u32[]{:S(2)}) collective-permute-start(bf16[11,256,128]{2,1,0:T(8,128)(2,1)S(1)} %collective-permute-done.rest_0_), channel_id=1, source_target_pairs={{0,1},{1,0},{2,3},{3,2},{4,5},{5,4},{6,7},{7,6},{8,9},{9,8},{10,11... | collective-permute-start | bytes 2162696 | tf_op jit(solution)/shard_map/ppermute | solution.py:428
  72.9 5.4 %beta_product.2 = bf16[256,1024]{1,0:T(8,128)(2,1)} custom-call(s32[2,8,11]{2,1,0:T(8,128)S(1)} %convert_add_fusion.place, s32[2,8]{1,0:T(2,128)S(1)} %constant_dynamic-slice_fusion.1.count, bf16[32,256,128]{2,1,0:T(8,128)(2,1)} %all-to-all-done.pool_any, bf16[2,11,1024,128]{3,2,1,0:T(8,128)(2,1)} %bitcast.34), custom_call_target="tpu_custom_call" | custom-call | flops 738197504 | bytes 7340032 | tf_op jit(solution)/shard_map/beta_product/pallas_call | solution.py:179
  78.3 3.7 %alpha_products.6.rest_6_ = bf16[256,1024]{1,0:T(8,128)(2,1)S(1)} custom-call(s32[1]{0:T(128)} %bitcast.8.core, s32[2,8,11]{2,1,0:T(8,128)S(1)} %bitcast.16, s32[2,8]{1,0:T(2,128)S(1)} %reshape.171.sizes, bf16[16,128,1024]{2,1,0:T(8,128)(2,1)} %bitcast.28, bf16[2,11,256,128]{3,2,1,0:T(8,128)(2,1)} %bitcast.22, ...), custom_call_target="tpu_custom_call" | custom-call | flops 369098752 | bytes 12582912 | tf_op jit(solution)/shard_map/alpha_products/pallas_call | solution.py:315
  84.0 4.7 %alpha_products.7 = (bf16[256,1024]{1,0:T(8,128)(2,1)S(1)}, bf16[256,1024]{1,0:T(8,128)(2,1)S(1)}) custom-call(s32[1]{0:T(128)} %bitcast.8.core, s32[2,8,11]{2,1,0:T(8,128)S(1)} %bitcast.17, s32[2,8]{1,0:T(2,128)S(1)} %reshape.171.sizes, bf16[16,128,1024]{2,1,0:T(8,128)(2,1)} %bitcast.29, bf16[2,11,256,128]{3,2,1,0:T(8,128)(2,1)} %bitcast.23, ...), custom_call_target="tpu_custom_call" | custom-call | flops 369098752 | bytes 12582912 | tf_op jit(solution)/shard_map/alpha_products/pallas_call | solution.py:315
  90.6 3.4 %collective-permute-start.8 = (bf16[256,1024]{1,0:T(8,128)(2,1)S(1)}, bf16[256,1024]{1,0:T(8,128)(2,1)S(1)}, u32[]{:S(2)}, u32[]{:S(2)}) collective-permute-start(bf16[256,1024]{1,0:T(8,128)(2,1)S(1)} %get-tuple-element.35), channel_id=1, source_target_pairs={{0,128},{16,144},{32,160},{48,176},{64,192},{80,208},{96,224},{112... | collective-permute-start | bytes 1572872 | tf_op jit(solution)/shard_map/ppermute | solution.py:347
  94.0 4.2 %alpha_products.8.first_ref = f32[256,1024]{1,0:T(8,128)} custom-call(s32[1]{0:T(128)} %bitcast.8.core, s32[2,8,11]{2,1,0:T(8,128)S(1)} %bitcast.18, s32[2,8]{1,0:T(2,128)S(1)} %reshape.171.sizes, bf16[16,128,1024]{2,1,0:T(8,128)(2,1)} %bitcast.30, bf16[2,11,256,128]{3,2,1,0:T(8,128)(2,1)} %bitcast.24, ...), custom_call_target="tpu_custom_call" | custom-call | flops 369098752 | bytes 12582912 | tf_op jit(solution)/shard_map/alpha_products/pallas_call | solution.py:315
  100.0 7.1 %collective-permute-done.7.refs_1_ = bf16[256,1024]{1,0:T(8,128)(2,1)S(1)} collective-permute-done((bf16[256,1024]{1,0:T(8,128)(2,1)S(1)}, bf16[256,1024]{1,0:T(8,128)(2,1)S(1)}, u32[]{:S(2)}, u32[]{:S(2)}) %collective-permute-start.7) | collective-permute-done | bytes 524320 | tf_op jit(solution)/shard_map/ppermute | solution.py:347
  107.1 3.6 %collective-permute-done.8.refs_2_ = bf16[256,1024]{1,0:T(8,128)(2,1)S(1)} collective-permute-done((bf16[256,1024]{1,0:T(8,128)(2,1)S(1)}, bf16[256,1024]{1,0:T(8,128)(2,1)S(1)}, u32[]{:S(2)}, u32[]{:S(2)}) %collective-permute-start.8) | collective-permute-done | bytes 524320 | tf_op jit(solution)/shard_map/ppermute | solution.py:347
  110.6 2.5 %sum_pack.1.rest_6_ = bf16[32,256,128]{2,1,0:T(8,128)(2,1)} custom-call(s32[32]{0:T(128)S(1)} %copy-done.6, f32[256,1024]{1,0:T(8,128)S(1)} %fold.3.refs_0_, bf16[256,1024]{1,0:T(8,128)(2,1)S(1)} %collective-permute-done.7.refs_1_, bf16[256,1024]{1,0:T(8,128)(2,1)S(1)} %collective-permute-done.8.refs_2_), custom_call_target="tpu_custom_call" | custom-call | flops 1048576 | bytes 6291456 | tf_op jit(solution)/shard_map/sum_pack/pallas_call | solution.py:90
  113.1 5.5 %all-to-all-start.1 = ((bf16[32,256,128]{2,1,0:T(8,128)(2,1)}), bf16[32,256,128]{2,1,0:T(8,128)(2,1)}, u32[]{:S(2)}, u32[]{:S(2)}) async-start(bf16[32,256,128]{2,1,0:T(8,128)(2,1)} %sum_pack.1.rest_6_), calls=%async_computation.1 | async-start | bytes 4194304 | tf_op jit(solution)/shard_map/all_to_all | solution.py:439
  118.6 18.2 %all-gather.5.cloned.1.call-done = bf16[2048,1024]{1,0:T(8,128)(2,1)} async-done(((bf16[256,1024]{1,0:T(8,128)(2,1)}), bf16[2048,1024]{1,0:T(8,128)(2,1)}) %all-gather.5.cloned.1.call-update) | async-done | bytes 4194320 | tf_op jit(solution)/shard_map/all_gather | solution.py:441
  136.8 3.2 %alpha_products.9.rest_6_ = bf16[256,1024]{1,0:T(8,128)(2,1)S(1)} custom-call(s32[1]{0:T(128)} %bitcast.8.core, s32[2,8,11]{2,1,0:T(8,128)S(1)} %bitcast.19, s32[2,8]{1,0:T(2,128)S(1)} %reshape.171.sizes, bf16[16,128,1024]{2,1,0:T(8,128)(2,1)} %bitcast.31, bf16[2,11,256,128]{3,2,1,0:T(8,128)(2,1)} %bitcast.25, ...), custom_call_target="tpu_custom_call" | custom-call | flops 369098752 | bytes 12582912 | tf_op jit(solution)/shard_map/alpha_products/pallas_call | solution.py:315
  140.0 4.9 %collective-permute-start.9 = (bf16[256,1024]{1,0:T(8,128)(2,1)S(1)}, bf16[256,1024]{1,0:T(8,128)(2,1)S(1)}, u32[]{:S(2)}, u32[]{:S(2)}) collective-permute-start(bf16[256,1024]{1,0:T(8,128)(2,1)S(1)} %alpha_products.9.rest_6_), channel_id=1, source_target_pairs={{0,256},{16,272},{32,288},{48,304},{64,320},{80,336},{96,352},{112... | collective-permute-start | bytes 1572872 | tf_op jit(solution)/shard_map/ppermute | solution.py:345
  144.9 5.0 %alpha_products.10 = (bf16[256,1024]{1,0:T(8,128)(2,1)}, bf16[256,1024]{1,0:T(8,128)(2,1)}) custom-call(s32[1]{0:T(128)} %bitcast.8.core, s32[2,8,11]{2,1,0:T(8,128)S(1)} %bitcast.20, s32[2,8]{1,0:T(2,128)S(1)} %reshape.171.sizes, bf16[16,128,1024]{2,1,0:T(8,128)(2,1)} %bitcast.32, bf16[2,11,256,128]{3,2,1,0:T(8,128)(2,1)} %bitcast.26, ...), custom_call_target="tpu_custom_call" | custom-call | flops 369098752 | bytes 12582912 | tf_op jit(solution)/shard_map/alpha_products/pallas_call | solution.py:315
  152.0 3.2 %collective-permute-start.11 = (bf16[256,1024]{1,0:T(8,128)(2,1)}, bf16[256,1024]{1,0:T(8,128)(2,1)S(1)}, u32[]{:S(2)}, u32[]{:S(2)}) collective-permute-start(bf16[256,1024]{1,0:T(8,128)(2,1)} %get-tuple-element.38), channel_id=1, source_target_pairs={{0,128},{16,144},{32,160},{48,176},{64,192},{80,208},{96,224},{112... | collective-permute-start | bytes 1572872 | tf_op jit(solution)/shard_map/ppermute | solution.py:347
  155.2 3.9 %alpha_products.11.first_ref = f32[256,1024]{1,0:T(8,128)} custom-call(s32[1]{0:T(128)} %bitcast.8.core, s32[2,8,11]{2,1,0:T(8,128)S(1)} %bitcast.21, s32[2,8]{1,0:T(2,128)S(1)} %reshape.171.sizes, bf16[16,128,1024]{2,1,0:T(8,128)(2,1)} %bitcast.33, bf16[2,11,256,128]{3,2,1,0:T(8,128)(2,1)} %bitcast.27, ...), custom_call_target="tpu_custom_call" | custom-call | flops 369098752 | bytes 12582912 | tf_op jit(solution)/shard_map/alpha_products/pallas_call | solution.py:315
  160.5 7.2 %all-to-all-done.1.pool_any = bf16[32,256,128]{2,1,0:T(8,128)(2,1)} async-done(((bf16[32,256,128]{2,1,0:T(8,128)(2,1)}), bf16[32,256,128]{2,1,0:T(8,128)(2,1)}, u32[]{:S(2)}, u32[]{:S(2)}) %all-to-all-start.1) | async-done | bytes 2097184 | tf_op jit(solution)/shard_map/all_to_all | solution.py:439
  167.7 4.8 %beta_product.3.first_ref = f32[256,1024]{1,0:T(8,128)S(1)} custom-call(s32[2,8,11]{2,1,0:T(8,128)S(1)} %convert_add_fusion.place, s32[2,8]{1,0:T(2,128)S(1)} %constant_dynamic-slice_fusion.1.count, bf16[32,256,128]{2,1,0:T(8,128)(2,1)} %all-to-all-done.1.pool_any, bf16[2,11,1024,128]{3,2,1,0:T(8,128)(2,1)} %bitcast.35, f32[256,1024]{1,0:T(8,128)S(1)} %fold.4.rest_0_), custom_call_target="tpu_custom_call" | custom-call | flops 738197504 | bytes 7340032 | tf_op jit(solution)/shard_map/beta_product/pallas_call | solution.py:179
  (82 shorter events, 23.0 us)
Async XLA Ops:
  6.5 21.3 %copy-start = (s32[2,128]{1,0:T(2,128)S(1)}, s32[2,128]{1,0:T(2,128)}, u32[]{:S(2)}) copy-start(s32[2,128]{1,0:T(2,128)} %param.13) | copy-start | bytes 3076
  6.5 71.8 %all-gather.3.cloned.1.call-start = ((), (), s32[]{:S(2)}) async-start(), calls=%async_computation.2 | async-start | bytes 4718592 | tf_op jit(solution)/shard_map/all_gather | solution.py:431
  12.6 11.3 %copy-start.9 = (s32[2,64,11]{1,0,2:T(2,128)S(1)}, s32[2,64,11]{1,0,2:T(2,128)}, u32[]{:S(2)}) copy-start(s32[2,64,11]{1,0,2:T(2,128)} %param.9) | copy-start | bytes 16900
  12.6 11.4 %copy-start.10 = (s32[2,64]{1,0:T(2,128)S(1)}, s32[2,64]{1,0:T(2,128)}, u32[]{:S(2)}) copy-start(s32[2,64]{1,0:T(2,128)} %param.10) | copy-start | bytes 1540
  12.6 14.2 %copy-start.8 = (s32[2,128,11]{1,0,2:T(2,128)S(1)}, s32[2,128,11]{1,0,2:T(2,128)}, u32[]{:S(2)}) copy-start(s32[2,128,11]{1,0,2:T(2,128)} %param.12) | copy-start | bytes 33796
  12.6 15.5 %copy-start.7 = (bf16[2,256,11,128]{3,1,2,0:T(8,128)(2,1)S(1)}, bf16[2,256,11,128]{3,1,2,0:T(8,128)(2,1)}, u32[]{:S(2)}) copy-start(bf16[2,256,11,128]{3,1,2,0:T(8,128)(2,1)} %param.8) | copy-start | bytes 4325380
  12.6 60.3 %all-to-all-start = ((bf16[32,256,128]{2,1,0:T(8,128)(2,1)}), bf16[32,256,128]{2,1,0:T(8,128)(2,1)}, u32[]{:S(2)}, u32[]{:S(2)}) async-start(bf16[32,256,128]{2,1,0:T(8,128)(2,1)} %pack.1), calls=%async_computation | async-start | bytes 4194304 | tf_op jit(solution)/shard_map/all_to_all | solution.py:433
  23.8 113.0 %all-gather.5.cloned.1.call-start = ((), (), s32[]{:S(2)}) async-start(), calls=%async_computation.3 | async-start | bytes 4718592 | tf_op jit(solution)/shard_map/all_gather | solution.py:441
  28.2 19.4 %collective-permute-start.2 = (bf16[11,256,128]{2,1,0:T(8,128)(2,1)S(1)}, bf16[11,256,128]{2,1,0:T(8,128)(2,1)S(1)}, u32[]{:S(2)}, u32[]{:S(2)}) collective-permute-start(bf16[11,256,128]{2,1,0:T(8,128)(2,1)S(1)} %dynamic-slice_bitcast_fusion), channel_id=1, source_target_pairs={{0,384},{16,400},{32,416},{48,432},{64,448},{80,464},{96,480},{112... | collective-permute-start | bytes 2162696 | tf_op jit(solution)/shard_map/ppermute | solution.py:427
  30.1 21.4 %collective-permute-start = (bf16[11,256,128]{2,1,0:T(8,128)(2,1)S(1)}, bf16[11,256,128]{2,1,0:T(8,128)(2,1)S(1)}, u32[]{:S(2)}, u32[]{:S(2)}) collective-permute-start(bf16[11,256,128]{2,1,0:T(8,128)(2,1)S(1)} %dynamic-slice_bitcast_fusion), channel_id=1, source_target_pairs={{0,128},{16,144},{32,160},{48,176},{64,192},{80,208},{96,224},{112... | collective-permute-start | bytes 2162696 | tf_op jit(solution)/shard_map/ppermute | solution.py:423
  33.5 35.7 %collective-permute-start.1 = (bf16[11,256,128]{2,1,0:T(8,128)(2,1)S(1)}, bf16[11,256,128]{2,1,0:T(8,128)(2,1)S(1)}, u32[]{:S(2)}, u32[]{:S(2)}) collective-permute-start(bf16[11,256,128]{2,1,0:T(8,128)(2,1)S(1)} %dynamic-slice_bitcast_fusion), channel_id=1, source_target_pairs={{0,256},{16,272},{32,288},{48,304},{64,320},{80,336},{96,352},{112... | collective-permute-start | bytes 2162696 | tf_op jit(solution)/shard_map/ppermute | solution.py:423
  47.6 30.6 %collective-permute-start.5 = (bf16[11,256,128]{2,1,0:T(8,128)(2,1)S(1)}, bf16[11,256,128]{2,1,0:T(8,128)(2,1)}, u32[]{:S(2)}, u32[]{:S(2)}) collective-permute-start(bf16[11,256,128]{2,1,0:T(8,128)(2,1)S(1)} %collective-permute-done.2.rest_2_), channel_id=1, source_target_pairs={{0,1},{1,0},{2,3},{3,2},{4,5},{5,4},{6,7},{7,6},{8,9},{9,8},{10,11... | collective-permute-start | bytes 2162696 | tf_op jit(solution)/shard_map/ppermute | solution.py:428
  51.5 26.7 %collective-permute-start.3 = (bf16[11,256,128]{2,1,0:T(8,128)(2,1)S(1)}, bf16[11,256,128]{2,1,0:T(8,128)(2,1)S(1)}, u32[]{:S(2)}, u32[]{:S(2)}) collective-permute-start(bf16[11,256,128]{2,1,0:T(8,128)(2,1)S(1)} %collective-permute-done.rest_0_), channel_id=1, source_target_pairs={{0,1},{1,0},{2,3},{3,2},{4,5},{5,4},{6,7},{7,6},{8,9},{9,8},{10,11... | collective-permute-start | bytes 2162696 | tf_op jit(solution)/shard_map/ppermute | solution.py:428
  69.2 9.1 %collective-permute-start.4 = (bf16[11,256,128]{2,1,0:T(8,128)(2,1)S(1)}, bf16[11,256,128]{2,1,0:T(8,128)(2,1)}, u32[]{:S(2)}, u32[]{:S(2)}) collective-permute-start(bf16[11,256,128]{2,1,0:T(8,128)(2,1)S(1)} %collective-permute-done.1.rest_1_), channel_id=1, source_target_pairs={{0,1},{1,0},{2,3},{3,2},{4,5},{5,4},{6,7},{7,6},{8,9},{9,8},{10,11... | collective-permute-start | bytes 2162696 | tf_op jit(solution)/shard_map/ppermute | solution.py:428
  82.0 16.6 %collective-permute-start.6 = (bf16[256,1024]{1,0:T(8,128)(2,1)S(1)}, bf16[256,1024]{1,0:T(8,128)(2,1)S(1)}, u32[]{:S(2)}, u32[]{:S(2)}) collective-permute-start(bf16[256,1024]{1,0:T(8,128)(2,1)S(1)} %alpha_products.6.rest_6_), channel_id=1, source_target_pairs={{0,256},{16,272},{32,288},{48,304},{64,320},{80,336},{96,352},{112... | collective-permute-start | bytes 1572872 | tf_op jit(solution)/shard_map/ppermute | solution.py:345
  84.0 10.0 %copy-start.2 = (bf16[11,256,128]{2,1,0:T(8,128)(2,1)S(1)}, bf16[11,256,128]{2,1,0:T(8,128)(2,1)}, u32[]{:S(2)}) copy-start(bf16[11,256,128]{2,1,0:T(8,128)(2,1)} %copy-done.1) | copy-start | bytes 2162692
  88.7 18.4 %collective-permute-start.7 = (bf16[256,1024]{1,0:T(8,128)(2,1)S(1)}, bf16[256,1024]{1,0:T(8,128)(2,1)S(1)}, u32[]{:S(2)}, u32[]{:S(2)}) collective-permute-start(bf16[256,1024]{1,0:T(8,128)(2,1)S(1)} %get-tuple-element.34.rest_6_), channel_id=1, source_target_pairs={{0,384},{16,400},{32,416},{48,432},{64,448},{80,464},{96,480},{112... | collective-permute-start | bytes 1572872 | tf_op jit(solution)/shard_map/ppermute | solution.py:347
  90.6 20.0 %collective-permute-start.8 = (bf16[256,1024]{1,0:T(8,128)(2,1)S(1)}, bf16[256,1024]{1,0:T(8,128)(2,1)S(1)}, u32[]{:S(2)}, u32[]{:S(2)}) collective-permute-start(bf16[256,1024]{1,0:T(8,128)(2,1)S(1)} %get-tuple-element.35), channel_id=1, source_target_pairs={{0,128},{16,144},{32,160},{48,176},{64,192},{80,208},{96,224},{112... | collective-permute-start | bytes 1572872 | tf_op jit(solution)/shard_map/ppermute | solution.py:347
  99.9 10.7 %copy-start.6 = (s32[32]{0:T(128)S(1)}, s32[32]{0:T(128)}, u32[]{:S(2)}) copy-start(s32[32]{0:T(128)} %reshape.172.wanted) | copy-start | bytes 388
  113.1 54.5 %all-to-all-start.1 = ((bf16[32,256,128]{2,1,0:T(8,128)(2,1)}), bf16[32,256,128]{2,1,0:T(8,128)(2,1)}, u32[]{:S(2)}, u32[]{:S(2)}) async-start(bf16[32,256,128]{2,1,0:T(8,128)(2,1)} %sum_pack.1.rest_6_), calls=%async_computation.1 | async-start | bytes 4194304 | tf_op jit(solution)/shard_map/all_to_all | solution.py:439
  140.0 15.2 %copy-start.3 = (bf16[11,256,128]{2,1,0:T(8,128)(2,1)S(1)}, bf16[11,256,128]{2,1,0:T(8,128)(2,1)}, u32[]{:S(2)}) copy-start(bf16[11,256,128]{2,1,0:T(8,128)(2,1)} %copy-done.1) | copy-start | bytes 2162692
  140.0 19.1 %collective-permute-start.9 = (bf16[256,1024]{1,0:T(8,128)(2,1)S(1)}, bf16[256,1024]{1,0:T(8,128)(2,1)S(1)}, u32[]{:S(2)}, u32[]{:S(2)}) collective-permute-start(bf16[256,1024]{1,0:T(8,128)(2,1)S(1)} %alpha_products.9.rest_6_), channel_id=1, source_target_pairs={{0,256},{16,272},{32,288},{48,304},{64,320},{80,336},{96,352},{112... | collective-permute-start | bytes 1572872 | tf_op jit(solution)/shard_map/ppermute | solution.py:345
  149.9 22.6 %collective-permute-start.10 = (bf16[256,1024]{1,0:T(8,128)(2,1)}, bf16[256,1024]{1,0:T(8,128)(2,1)S(1)}, u32[]{:S(2)}, u32[]{:S(2)}) collective-permute-start(bf16[256,1024]{1,0:T(8,128)(2,1)} %get-tuple-element.37.rest_6_), channel_id=1, source_target_pairs={{0,384},{16,400},{32,416},{48,432},{64,448},{80,464},{96,480},{112... | collective-permute-start | bytes 1572872 | tf_op jit(solution)/shard_map/ppermute | solution.py:347
  152.0 20.5 %collective-permute-start.11 = (bf16[256,1024]{1,0:T(8,128)(2,1)}, bf16[256,1024]{1,0:T(8,128)(2,1)S(1)}, u32[]{:S(2)}, u32[]{:S(2)}) collective-permute-start(bf16[256,1024]{1,0:T(8,128)(2,1)} %get-tuple-element.38), channel_id=1, source_target_pairs={{0,128},{16,144},{32,160},{48,176},{64,192},{80,208},{96,224},{112... | collective-permute-start | bytes 1572872 | tf_op jit(solution)/shard_map/ppermute | solution.py:347
  (3 other events, 6.2 us)
Sparse Core Ops, SparseCore 0:
  9.4 63.7 all-gather.2
  78.5 58.2 all-gather.4

commit v5 on v4

--- a/solution.py
+++ b/solution.py
@@ -29,13 +29,13 @@
     return pltpu.CompilerParams(vmem_limit_bytes=limit)
 
 
-def pack_kernel(wanted, c_ref, out_ref, blocks, sems):
+def pack_kernel(lowest, highest, c_ref, out_ref, blocks, sems):
     for b in range(blocks.shape[0]):
         blocks[b] = c_ref[:, b * BLK : (b + 1) * BLK]
 
     def each(action):
         for t in range(NBETA * FROM_B):
-            action(pltpu.make_async_copy(blocks.at[wanted[t]], out_ref.at[t], sems.at[t]))
+            action(pltpu.make_async_copy(blocks.at[(lowest, highest)[t % FROM_B][t // FROM_B]], out_ref.at[t], sems.at[t]))
 
     each(lambda copy: copy.start())
     each(lambda copy: copy.wait())
@@ -47,9 +47,9 @@
     return pl.pallas_call(
         pack_kernel,
         grid_spec=pltpu.PrefetchScalarGridSpec(
-            num_scalar_prefetch=1,
+            num_scalar_prefetch=2,
             grid=(1,),
-            in_specs=[pl.BlockSpec(c.shape, lambda i, w: (0, 0))],
+            in_specs=[pl.BlockSpec(c.shape, lambda i, low, high: (0, 0))],
             out_specs=pl.BlockSpec(memory_space=pl.ANY),
             scratch_shapes=[
                 pltpu.VMEM((cols // BLK, rows, BLK), c.dtype),
@@ -60,10 +60,10 @@
         compiler_params=params(60 * 1024 * 1024),
         cost_estimate=pl.CostEstimate(flops=0, bytes_accessed=5 << 20, transcendentals=0),
         name="pack",
-    )(wanted, c)
-
-
-def sum_pack_kernel(wanted, *refs):
+    )(*wanted, c)
+
+
+def sum_pack_kernel(lowest, highest, *refs):
     parts, (out_ref, inter, sems) = refs[:-3], refs[-3:]
     step = pl.program_id(0)
     per_step = parts[0].shape[1] // BLK
@@ -76,7 +76,7 @@
 
     def each(action):
         for t in range(NBETA * FROM_B):
-            action(pltpu.make_async_copy(inter.at[wanted[t]], out_ref.at[t], sems.at[t]))
+            action(pltpu.make_async_copy(inter.at[(lowest, highest)[t % FROM_B][t // FROM_B]], out_ref.at[t], sems.at[t]))
 
     @pl.when(step == pl.num_programs(0) - 1)
     def _():
@@ -90,9 +90,9 @@
     return pl.pallas_call(
         sum_pack_kernel,
         grid_spec=pltpu.PrefetchScalarGridSpec(
-            num_scalar_prefetch=1,
+            num_scalar_prefetch=2,
             grid=(steps,),
-            in_specs=[pl.BlockSpec((rows, cols // steps), lambda i, w: (0, i))] * len(parts),
+            in_specs=[pl.BlockSpec((rows, cols // steps), lambda i, low, high: (0, i))] * len(parts),
             out_specs=pl.BlockSpec(memory_space=pl.ANY),
             scratch_shapes=[
                 pltpu.VMEM((cols // BLK, rows, BLK), jnp.bfloat16),
@@ -103,7 +103,7 @@
         compiler_params=params(),
         cost_estimate=pl.CostEstimate(flops=1 << 20, bytes_accessed=6 << 20, transcendentals=0),
         name="sum_pack",
-    )(wanted, *parts)
+    )(*wanted, *parts)
 
 
 def beta_kernel(op, place, count, pool_any, b_any, *rest):
@@ -387,7 +387,7 @@
     inside = (local >= 0) & (local < col_blocks)
     lowest = jnp.min(jnp.where(inside, local, col_blocks - 1), axis=(0, 2))
     highest = jnp.max(jnp.where(inside, local, 0), axis=(0, 2))
-    wanted = jnp.stack([lowest, highest], axis=1).reshape(NBETA * FROM_B)
+    wanted = (lowest, highest)
 
     mine = lax.dynamic_slice_in_dim(b_list, beta_here * col_blocks, col_blocks, 1)
     beta_counts = lax.dynamic_slice_in_dim(b_count, beta_here * col_blocks, col_blocks, 1)

time: 181 us -> 182 us (level)
  transfers between devices with their start and end apart: 16 -> 16, of which waited for: 8 -> 8; matrix products, arithmetic and copies ran while one was open for 3% -> 4% of each run, Pallas kernels for 23% -> 23%
where the time goes in v5:
time: 182 us; the launch traced here: 181 us
  starting transfers between devices  64.7 us (36%)
  waiting for transfers between devices  51.2 us (28%)
  Pallas kernels  42.4 us (23%)
  between operations  13.9 us (8%)
  other arithmetic  4.95 us (3%)
  local copies, waits for them, and re-layouts  3.96 us (2%)
    pallas_call x6, Pallas kernels, alpha_products(): pl.pallas_call(functools.partial(alpha_kernel, op, steps), grid_spec=pltp...  25 us
    ppermute x3, starting transfers between devices, on_device(): far = [lax.ppermute(part, 'beta', SWAP_CORES) for part in near]  23.1 us
    all_gather x1, waiting for transfers between devices, on_device(): lax.all_gather(d_one, 'alpha', axis=0, tiled=True, axis_index_groups=Z_GR...  17.8 us
    all_to_all x2, starting transfers between devices, on_device(): lax.all_to_all(sent, 'beta', split_axis=0, concat_axis=0, tiled=True)  16.7 us
    ppermute x1, waiting for transfers between devices, on_device(): near.append(lax.ppermute(a_half, 'alpha', shift_x(3)))  11.9 us
    ppermute x4, waiting for transfers between devices, alpha_sums(): lax.ppermute(part, 'alpha', shift_x(X - d))  10.7 us
    ppermute x4, starting transfers between devices, alpha_sums(): lax.ppermute(part, 'alpha', shift_x(X - d))  10.6 us
    pallas_call x2, Pallas kernels, beta_product(): pl.pallas_call(functools.partial(beta_kernel, op), grid_spec=pltpu.Prefet...  10.2 us
  transfers between devices with their start and end apart: 16, of which 8 were waited for; matrix products, arithmetic and copies ran while one was open for 4% of the time, Pallas kernels for 23%

profile of v5, /device:TPU:1, one launch (start us, length us, event | category | flops | bytes accessed | tf_op | source)
XLA Modules:
  0.0 181.1 jit_solution(2687968857255368471)
XLA Ops:
  9.5 3.4 %pack.1 = bf16[32,256,128]{2,1,0:T(8,128)(2,1)} custom-call(s32[16]{0:T(128)} %reduce_min.28.lowest, s32[16]{0:T(128)} %reduce_max.18.highest, bf16[256,1024]{1,0:T(8,128)(2,1)} %c_ref.1), custom_call_target="tpu_custom_call" | custom-call | bytes 5242880 | tf_op jit(solution)/shard_map/pack/pallas_call | solution.py:47
  13.0 11.2 %all-to-all-start = ((bf16[32,256,128]{2,1,0:T(8,128)(2,1)}), bf16[32,256,128]{2,1,0:T(8,128)(2,1)}, u32[]{:S(2)}, u32[]{:S(2)}) async-start(bf16[32,256,128]{2,1,0:T(8,128)(2,1)} %pack.1), calls=%async_computation | async-start | bytes 4194304 | tf_op jit(solution)/shard_map/all_to_all | solution.py:433
  30.5 3.3 %collective-permute-start = (bf16[11,256,128]{2,1,0:T(8,128)(2,1)S(1)}, bf16[11,256,128]{2,1,0:T(8,128)(2,1)S(1)}, u32[]{:S(2)}, u32[]{:S(2)}) collective-permute-start(bf16[11,256,128]{2,1,0:T(8,128)(2,1)S(1)} %dynamic-slice_bitcast_fusion), channel_id=1, source_target_pairs={{0,128},{16,144},{32,160},{48,176},{64,192},{80,208},{96,224},{112... | collective-permute-start | bytes 2162696 | tf_op jit(solution)/shard_map/ppermute | solution.py:423
  36.0 11.9 %collective-permute-done.2.rest_2_ = bf16[11,256,128]{2,1,0:T(8,128)(2,1)S(1)} collective-permute-done((bf16[11,256,128]{2,1,0:T(8,128)(2,1)S(1)}, bf16[11,256,128]{2,1,0:T(8,128)(2,1)S(1)}, u32[]{:S(2)}, u32[]{:S(2)}) %collective-permute-start.2) | collective-permute-done | bytes 720928 | tf_op jit(solution)/shard_map/ppermute | solution.py:427
  48.0 3.6 %collective-permute-start.5 = (bf16[11,256,128]{2,1,0:T(8,128)(2,1)S(1)}, bf16[11,256,128]{2,1,0:T(8,128)(2,1)}, u32[]{:S(2)}, u32[]{:S(2)}) collective-permute-start(bf16[11,256,128]{2,1,0:T(8,128)(2,1)S(1)} %collective-permute-done.2.rest_2_), channel_id=1, source_target_pairs={{0,1},{1,0},{2,3},{3,2},{4,5},{5,4},{6,7},{7,6},{8,9},{9,8},{10,11... | collective-permute-start | bytes 2162696 | tf_op jit(solution)/shard_map/ppermute | solution.py:428
  51.9 17.6 %collective-permute-start.3 = (bf16[11,256,128]{2,1,0:T(8,128)(2,1)S(1)}, bf16[11,256,128]{2,1,0:T(8,128)(2,1)S(1)}, u32[]{:S(2)}, u32[]{:S(2)}) collective-permute-start(bf16[11,256,128]{2,1,0:T(8,128)(2,1)S(1)} %collective-permute-done.rest_0_), channel_id=1, source_target_pairs={{0,1},{1,0},{2,3},{3,2},{4,5},{5,4},{6,7},{7,6},{8,9},{9,8},{10,11... | collective-permute-start | bytes 2162696 | tf_op jit(solution)/shard_map/ppermute | solution.py:428
  73.2 5.3 %beta_product.2 = bf16[256,1024]{1,0:T(8,128)(2,1)} custom-call(s32[2,8,11]{2,1,0:T(8,128)S(1)} %convert_add_fusion.place, s32[2,8]{1,0:T(2,128)S(1)} %constant_dynamic-slice_fusion.1.count, bf16[32,256,128]{2,1,0:T(8,128)(2,1)} %all-to-all-done.pool_any, bf16[2,11,1024,128]{3,2,1,0:T(8,128)(2,1)} %bitcast.32), custom_call_target="tpu_custom_call" | custom-call | flops 738197504 | bytes 7340032 | tf_op jit(solution)/shard_map/beta_product/pallas_call | solution.py:179
  78.7 4.0 %alpha_products.6.rest_6_ = bf16[256,1024]{1,0:T(8,128)(2,1)S(1)} custom-call(s32[1]{0:T(128)} %bitcast.6.core, s32[2,8,11]{2,1,0:T(8,128)S(1)} %bitcast.14, s32[2,8]{1,0:T(2,128)S(1)} %reshape.168.sizes, bf16[16,128,1024]{2,1,0:T(8,128)(2,1)} %bitcast.26, bf16[2,11,256,128]{3,2,1,0:T(8,128)(2,1)} %bitcast.20, ...), custom_call_target="tpu_custom_call" | custom-call | flops 369098752 | bytes 12582912 | tf_op jit(solution)/shard_map/alpha_products/pallas_call | solution.py:315
  84.6 4.8 %alpha_products.7 = (bf16[256,1024]{1,0:T(8,128)(2,1)S(1)}, bf16[256,1024]{1,0:T(8,128)(2,1)S(1)}) custom-call(s32[1]{0:T(128)} %bitcast.6.core, s32[2,8,11]{2,1,0:T(8,128)S(1)} %bitcast.15, s32[2,8]{1,0:T(2,128)S(1)} %reshape.168.sizes, bf16[16,128,1024]{2,1,0:T(8,128)(2,1)} %bitcast.27, bf16[2,11,256,128]{3,2,1,0:T(8,128)(2,1)} %bitcast.21, ...), custom_call_target="tpu_custom_call" | custom-call | flops 369098752 | bytes 12582912 | tf_op jit(solution)/shard_map/alpha_products/pallas_call | solution.py:315
  89.4 2.3 %collective-permute-start.7 = (bf16[256,1024]{1,0:T(8,128)(2,1)S(1)}, bf16[256,1024]{1,0:T(8,128)(2,1)S(1)}, u32[]{:S(2)}, u32[]{:S(2)}) collective-permute-start(bf16[256,1024]{1,0:T(8,128)(2,1)S(1)} %get-tuple-element.34.rest_6_), channel_id=1, source_target_pairs={{0,384},{16,400},{32,416},{48,432},{64,448},{80,464},{96,480},{112... | collective-permute-start | bytes 1572872 | tf_op jit(solution)/shard_map/ppermute | solution.py:347
  91.7 3.0 %collective-permute-start.8 = (bf16[256,1024]{1,0:T(8,128)(2,1)S(1)}, bf16[256,1024]{1,0:T(8,128)(2,1)S(1)}, u32[]{:S(2)}, u32[]{:S(2)}) collective-permute-start(bf16[256,1024]{1,0:T(8,128)(2,1)S(1)} %get-tuple-element.35), channel_id=1, source_target_pairs={{0,128},{16,144},{32,160},{48,176},{64,192},{80,208},{96,224},{112... | collective-permute-start | bytes 1572872 | tf_op jit(solution)/shard_map/ppermute | solution.py:347
  94.7 4.3 %alpha_products.8.first_ref = f32[256,1024]{1,0:T(8,128)} custom-call(s32[1]{0:T(128)} %bitcast.6.core, s32[2,8,11]{2,1,0:T(8,128)S(1)} %bitcast.16, s32[2,8]{1,0:T(2,128)S(1)} %reshape.168.sizes, bf16[16,128,1024]{2,1,0:T(8,128)(2,1)} %bitcast.28, bf16[2,11,256,128]{3,2,1,0:T(8,128)(2,1)} %bitcast.22, ...), custom_call_target="tpu_custom_call" | custom-call | flops 369098752 | bytes 12582912 | tf_op jit(solution)/shard_map/alpha_products/pallas_call | solution.py:315
  100.6 6.7 %collective-permute-done.7.refs_1_ = bf16[256,1024]{1,0:T(8,128)(2,1)S(1)} collective-permute-done((bf16[256,1024]{1,0:T(8,128)(2,1)S(1)}, bf16[256,1024]{1,0:T(8,128)(2,1)S(1)}, u32[]{:S(2)}, u32[]{:S(2)}) %collective-permute-start.7) | collective-permute-done | bytes 524320 | tf_op jit(solution)/shard_map/ppermute | solution.py:347
  107.3 4.0 %collective-permute-done.8.refs_2_ = bf16[256,1024]{1,0:T(8,128)(2,1)S(1)} collective-permute-done((bf16[256,1024]{1,0:T(8,128)(2,1)S(1)}, bf16[256,1024]{1,0:T(8,128)(2,1)S(1)}, u32[]{:S(2)}, u32[]{:S(2)}) %collective-permute-start.8) | collective-permute-done | bytes 524320 | tf_op jit(solution)/shard_map/ppermute | solution.py:347
  111.2 2.5 %sum_pack.1.rest_6_ = bf16[32,256,128]{2,1,0:T(8,128)(2,1)} custom-call(s32[16]{0:T(128)S(1)} %copy-done.7, s32[16]{0:T(128)S(1)} %copy-done.6, f32[256,1024]{1,0:T(8,128)S(1)} %fold.3.refs_0_, bf16[256,1024]{1,0:T(8,128)(2,1)S(1)} %collective-permute-done.7.refs_1_, bf16[256,1024]{1,0:T(8,128)(2,1)S(1)} %collective-permute-done.8.refs_2_), custom_call_target="tpu_custom_call" | custom-call | flops 1048576 | bytes 6291456 | tf_op jit(solution)/shard_map/sum_pack/pallas_call | solution.py:90
  113.8 5.5 %all-to-all-start.1 = ((bf16[32,256,128]{2,1,0:T(8,128)(2,1)}), bf16[32,256,128]{2,1,0:T(8,128)(2,1)}, u32[]{:S(2)}, u32[]{:S(2)}) async-start(bf16[32,256,128]{2,1,0:T(8,128)(2,1)} %sum_pack.1.rest_6_), calls=%async_computation.1 | async-start | bytes 4194304 | tf_op jit(solution)/shard_map/all_to_all | solution.py:439
  119.2 17.8 %all-gather.5.cloned.1.call-done = bf16[2048,1024]{1,0:T(8,128)(2,1)} async-done(((bf16[256,1024]{1,0:T(8,128)(2,1)}), bf16[2048,1024]{1,0:T(8,128)(2,1)}) %all-gather.5.cloned.1.call-update) | async-done | bytes 4194320 | tf_op jit(solution)/shard_map/all_gather | solution.py:441
  137.1 3.0 %alpha_products.9.rest_6_ = bf16[256,1024]{1,0:T(8,128)(2,1)S(1)} custom-call(s32[1]{0:T(128)} %bitcast.6.core, s32[2,8,11]{2,1,0:T(8,128)S(1)} %bitcast.17, s32[2,8]{1,0:T(2,128)S(1)} %reshape.168.sizes, bf16[16,128,1024]{2,1,0:T(8,128)(2,1)} %bitcast.29, bf16[2,11,256,128]{3,2,1,0:T(8,128)(2,1)} %bitcast.23, ...), custom_call_target="tpu_custom_call" | custom-call | flops 369098752 | bytes 12582912 | tf_op jit(solution)/shard_map/alpha_products/pallas_call | solution.py:315
  140.1 4.8 %collective-permute-start.9 = (bf16[256,1024]{1,0:T(8,128)(2,1)S(1)}, bf16[256,1024]{1,0:T(8,128)(2,1)S(1)}, u32[]{:S(2)}, u32[]{:S(2)}) collective-permute-start(bf16[256,1024]{1,0:T(8,128)(2,1)S(1)} %alpha_products.9.rest_6_), channel_id=1, source_target_pairs={{0,256},{16,272},{32,288},{48,304},{64,320},{80,336},{96,352},{112... | collective-permute-start | bytes 1572872 | tf_op jit(solution)/shard_map/ppermute | solution.py:345
  144.9 5.1 %alpha_products.10 = (bf16[256,1024]{1,0:T(8,128)(2,1)}, bf16[256,1024]{1,0:T(8,128)(2,1)}) custom-call(s32[1]{0:T(128)} %bitcast.6.core, s32[2,8,11]{2,1,0:T(8,128)S(1)} %bitcast.18, s32[2,8]{1,0:T(2,128)S(1)} %reshape.168.sizes, bf16[16,128,1024]{2,1,0:T(8,128)(2,1)} %bitcast.30, bf16[2,11,256,128]{3,2,1,0:T(8,128)(2,1)} %bitcast.24, ...), custom_call_target="tpu_custom_call" | custom-call | flops 369098752 | bytes 12582912 | tf_op jit(solution)/shard_map/alpha_products/pallas_call | solution.py:315
  150.0 3.0 %collective-permute-start.10 = (bf16[256,1024]{1,0:T(8,128)(2,1)}, bf16[256,1024]{1,0:T(8,128)(2,1)S(1)}, u32[]{:S(2)}, u32[]{:S(2)}) collective-permute-start(bf16[256,1024]{1,0:T(8,128)(2,1)} %get-tuple-element.37.rest_6_), channel_id=1, source_target_pairs={{0,384},{16,400},{32,416},{48,432},{64,448},{80,464},{96,480},{112... | collective-permute-start | bytes 1572872 | tf_op jit(solution)/shard_map/ppermute | solution.py:347
  155.3 3.9 %alpha_products.11.first_ref = f32[256,1024]{1,0:T(8,128)} custom-call(s32[1]{0:T(128)} %bitcast.6.core, s32[2,8,11]{2,1,0:T(8,128)S(1)} %bitcast.19, s32[2,8]{1,0:T(2,128)S(1)} %reshape.168.sizes, bf16[16,128,1024]{2,1,0:T(8,128)(2,1)} %bitcast.31, bf16[2,11,256,128]{3,2,1,0:T(8,128)(2,1)} %bitcast.25, ...), custom_call_target="tpu_custom_call" | custom-call | flops 369098752 | bytes 12582912 | tf_op jit(solution)/shard_map/alpha_products/pallas_call | solution.py:315
  160.6 7.7 %all-to-all-done.1.pool_any = bf16[32,256,128]{2,1,0:T(8,128)(2,1)} async-done(((bf16[32,256,128]{2,1,0:T(8,128)(2,1)}), bf16[32,256,128]{2,1,0:T(8,128)(2,1)}, u32[]{:S(2)}, u32[]{:S(2)}) %all-to-all-start.1) | async-done | bytes 2097184 | tf_op jit(solution)/shard_map/all_to_all | solution.py:439
  168.3 4.8 %beta_product.3.first_ref = f32[256,1024]{1,0:T(8,128)S(1)} custom-call(s32[2,8,11]{2,1,0:T(8,128)S(1)} %convert_add_fusion.place, s32[2,8]{1,0:T(2,128)S(1)} %constant_dynamic-slice_fusion.1.count, bf16[32,256,128]{2,1,0:T(8,128)(2,1)} %all-to-all-done.1.pool_any, bf16[2,11,1024,128]{3,2,1,0:T(8,128)(2,1)} %bitcast.33, f32[256,1024]{1,0:T(8,128)S(1)} %fold.4.rest_0_), custom_call_target="tpu_custom_call" | custom-call | flops 738197504 | bytes 7340032 | tf_op jit(solution)/shard_map/beta_product/pallas_call | solution.py:179
  (81 shorter events, 23.6 us)
Async XLA Ops:
  6.5 21.7 %copy-start = (s32[2,128]{1,0:T(2,128)S(1)}, s32[2,128]{1,0:T(2,128)}, u32[]{:S(2)}) copy-start(s32[2,128]{1,0:T(2,128)} %param.13) | copy-start | bytes 3076
  6.5 72.1 %all-gather.3.cloned.1.call-start = ((), (), s32[]{:S(2)}) async-start(), calls=%async_computation.2 | async-start | bytes 4718592 | tf_op jit(solution)/shard_map/all_gather | solution.py:431
  12.9 11.3 %copy-start.10 = (s32[2,64,11]{1,0,2:T(2,128)S(1)}, s32[2,64,11]{1,0,2:T(2,128)}, u32[]{:S(2)}) copy-start(s32[2,64,11]{1,0,2:T(2,128)} %param.9) | copy-start | bytes 16900
  12.9 11.4 %copy-start.11 = (s32[2,64]{1,0:T(2,128)S(1)}, s32[2,64]{1,0:T(2,128)}, u32[]{:S(2)}) copy-start(s32[2,64]{1,0:T(2,128)} %param.10) | copy-start | bytes 1540
  12.9 14.2 %copy-start.9 = (s32[2,128,11]{1,0,2:T(2,128)S(1)}, s32[2,128,11]{1,0,2:T(2,128)}, u32[]{:S(2)}) copy-start(s32[2,128,11]{1,0,2:T(2,128)} %param.12) | copy-start | bytes 33796
  12.9 15.5 %copy-start.8 = (bf16[2,256,11,128]{3,1,2,0:T(8,128)(2,1)S(1)}, bf16[2,256,11,128]{3,1,2,0:T(8,128)(2,1)}, u32[]{:S(2)}) copy-start(bf16[2,256,11,128]{3,1,2,0:T(8,128)(2,1)} %param.8) | copy-start | bytes 4325380
  13.0 60.3 %all-to-all-start = ((bf16[32,256,128]{2,1,0:T(8,128)(2,1)}), bf16[32,256,128]{2,1,0:T(8,128)(2,1)}, u32[]{:S(2)}, u32[]{:S(2)}) async-start(bf16[32,256,128]{2,1,0:T(8,128)(2,1)} %pack.1), calls=%async_computation | async-start | bytes 4194304 | tf_op jit(solution)/shard_map/all_to_all | solution.py:433
  24.1 112.9 %all-gather.5.cloned.1.call-start = ((), (), s32[]{:S(2)}) async-start(), calls=%async_computation.3 | async-start | bytes 4718592 | tf_op jit(solution)/shard_map/all_gather | solution.py:441
  28.5 19.4 %collective-permute-start.2 = (bf16[11,256,128]{2,1,0:T(8,128)(2,1)S(1)}, bf16[11,256,128]{2,1,0:T(8,128)(2,1)S(1)}, u32[]{:S(2)}, u32[]{:S(2)}) collective-permute-start(bf16[11,256,128]{2,1,0:T(8,128)(2,1)S(1)} %dynamic-slice_bitcast_fusion), channel_id=1, source_target_pairs={{0,384},{16,400},{32,416},{48,432},{64,448},{80,464},{96,480},{112... | collective-permute-start | bytes 2162696 | tf_op jit(solution)/shard_map/ppermute | solution.py:427
  30.5 21.4 %collective-permute-start = (bf16[11,256,128]{2,1,0:T(8,128)(2,1)S(1)}, bf16[11,256,128]{2,1,0:T(8,128)(2,1)S(1)}, u32[]{:S(2)}, u32[]{:S(2)}) collective-permute-start(bf16[11,256,128]{2,1,0:T(8,128)(2,1)S(1)} %dynamic-slice_bitcast_fusion), channel_id=1, source_target_pairs={{0,128},{16,144},{32,160},{48,176},{64,192},{80,208},{96,224},{112... | collective-permute-start | bytes 2162696 | tf_op jit(solution)/shard_map/ppermute | solution.py:423
  33.8 35.7 %collective-permute-start.1 = (bf16[11,256,128]{2,1,0:T(8,128)(2,1)S(1)}, bf16[11,256,128]{2,1,0:T(8,128)(2,1)S(1)}, u32[]{:S(2)}, u32[]{:S(2)}) collective-permute-start(bf16[11,256,128]{2,1,0:T(8,128)(2,1)S(1)} %dynamic-slice_bitcast_fusion), channel_id=1, source_target_pairs={{0,256},{16,272},{32,288},{48,304},{64,320},{80,336},{96,352},{112... | collective-permute-start | bytes 2162696 | tf_op jit(solution)/shard_map/ppermute | solution.py:423
  48.0 30.6 %collective-permute-start.5 = (bf16[11,256,128]{2,1,0:T(8,128)(2,1)S(1)}, bf16[11,256,128]{2,1,0:T(8,128)(2,1)}, u32[]{:S(2)}, u32[]{:S(2)}) collective-permute-start(bf16[11,256,128]{2,1,0:T(8,128)(2,1)S(1)} %collective-permute-done.2.rest_2_), channel_id=1, source_target_pairs={{0,1},{1,0},{2,3},{3,2},{4,5},{5,4},{6,7},{7,6},{8,9},{9,8},{10,11... | collective-permute-start | bytes 2162696 | tf_op jit(solution)/shard_map/ppermute | solution.py:428
  51.9 26.7 %collective-permute-start.3 = (bf16[11,256,128]{2,1,0:T(8,128)(2,1)S(1)}, bf16[11,256,128]{2,1,0:T(8,128)(2,1)S(1)}, u32[]{:S(2)}, u32[]{:S(2)}) collective-permute-start(bf16[11,256,128]{2,1,0:T(8,128)(2,1)S(1)} %collective-permute-done.rest_0_), channel_id=1, source_target_pairs={{0,1},{1,0},{2,3},{3,2},{4,5},{5,4},{6,7},{7,6},{8,9},{9,8},{10,11... | collective-permute-start | bytes 2162696 | tf_op jit(solution)/shard_map/ppermute | solution.py:428
  69.5 9.1 %collective-permute-start.4 = (bf16[11,256,128]{2,1,0:T(8,128)(2,1)S(1)}, bf16[11,256,128]{2,1,0:T(8,128)(2,1)}, u32[]{:S(2)}, u32[]{:S(2)}) collective-permute-start(bf16[11,256,128]{2,1,0:T(8,128)(2,1)S(1)} %collective-permute-done.1.rest_1_), channel_id=1, source_target_pairs={{0,1},{1,0},{2,3},{3,2},{4,5},{5,4},{6,7},{7,6},{8,9},{9,8},{10,11... | collective-permute-start | bytes 2162696 | tf_op jit(solution)/shard_map/ppermute | solution.py:428
  82.6 16.5 %collective-permute-start.6 = (bf16[256,1024]{1,0:T(8,128)(2,1)S(1)}, bf16[256,1024]{1,0:T(8,128)(2,1)S(1)}, u32[]{:S(2)}, u32[]{:S(2)}) collective-permute-start(bf16[256,1024]{1,0:T(8,128)(2,1)S(1)} %alpha_products.6.rest_6_), channel_id=1, source_target_pairs={{0,256},{16,272},{32,288},{48,304},{64,320},{80,336},{96,352},{112... | collective-permute-start | bytes 1572872 | tf_op jit(solution)/shard_map/ppermute | solution.py:345
  89.4 17.9 %collective-permute-start.7 = (bf16[256,1024]{1,0:T(8,128)(2,1)S(1)}, bf16[256,1024]{1,0:T(8,128)(2,1)S(1)}, u32[]{:S(2)}, u32[]{:S(2)}) collective-permute-start(bf16[256,1024]{1,0:T(8,128)(2,1)S(1)} %get-tuple-element.34.rest_6_), channel_id=1, source_target_pairs={{0,384},{16,400},{32,416},{48,432},{64,448},{80,464},{96,480},{112... | collective-permute-start | bytes 1572872 | tf_op jit(solution)/shard_map/ppermute | solution.py:347
  91.7 19.5 %collective-permute-start.8 = (bf16[256,1024]{1,0:T(8,128)(2,1)S(1)}, bf16[256,1024]{1,0:T(8,128)(2,1)S(1)}, u32[]{:S(2)}, u32[]{:S(2)}) collective-permute-start(bf16[256,1024]{1,0:T(8,128)(2,1)S(1)} %get-tuple-element.35), channel_id=1, source_target_pairs={{0,128},{16,144},{32,160},{48,176},{64,192},{80,208},{96,224},{112... | collective-permute-start | bytes 1572872 | tf_op jit(solution)/shard_map/ppermute | solution.py:347
  100.4 10.8 %copy-start.6 = (s32[16]{0:T(128)S(1)}, s32[16]{0:T(128)}, u32[]{:S(2)}) copy-start(s32[16]{0:T(128)} %reduce_max.18.highest) | copy-start | bytes 196
  100.4 10.8 %copy-start.7 = (s32[16]{0:T(128)S(1)}, s32[16]{0:T(128)}, u32[]{:S(2)}) copy-start(s32[16]{0:T(128)} %reduce_min.28.lowest) | copy-start | bytes 196
  113.8 54.5 %all-to-all-start.1 = ((bf16[32,256,128]{2,1,0:T(8,128)(2,1)}), bf16[32,256,128]{2,1,0:T(8,128)(2,1)}, u32[]{:S(2)}, u32[]{:S(2)}) async-start(bf16[32,256,128]{2,1,0:T(8,128)(2,1)} %sum_pack.1.rest_6_), calls=%async_computation.1 | async-start | bytes 4194304 | tf_op jit(solution)/shard_map/all_to_all | solution.py:439
  140.0 15.3 %copy-start.3 = (bf16[11,256,128]{2,1,0:T(8,128)(2,1)S(1)}, bf16[11,256,128]{2,1,0:T(8,128)(2,1)}, u32[]{:S(2)}) copy-start(bf16[11,256,128]{2,1,0:T(8,128)(2,1)} %copy-done.1) | copy-start | bytes 2162692
  140.1 19.2 %collective-permute-start.9 = (bf16[256,1024]{1,0:T(8,128)(2,1)S(1)}, bf16[256,1024]{1,0:T(8,128)(2,1)S(1)}, u32[]{:S(2)}, u32[]{:S(2)}) collective-permute-start(bf16[256,1024]{1,0:T(8,128)(2,1)S(1)} %alpha_products.9.rest_6_), channel_id=1, source_target_pairs={{0,256},{16,272},{32,288},{48,304},{64,320},{80,336},{96,352},{112... | collective-permute-start | bytes 1572872 | tf_op jit(solution)/shard_map/ppermute | solution.py:345
  150.0 23.1 %collective-permute-start.10 = (bf16[256,1024]{1,0:T(8,128)(2,1)}, bf16[256,1024]{1,0:T(8,128)(2,1)S(1)}, u32[]{:S(2)}, u32[]{:S(2)}) collective-permute-start(bf16[256,1024]{1,0:T(8,128)(2,1)} %get-tuple-element.37.rest_6_), channel_id=1, source_target_pairs={{0,384},{16,400},{32,416},{48,432},{64,448},{80,464},{96,480},{112... | collective-permute-start | bytes 1572872 | tf_op jit(solution)/shard_map/ppermute | solution.py:347
  153.1 20.1 %collective-permute-start.11 = (bf16[256,1024]{1,0:T(8,128)(2,1)}, bf16[256,1024]{1,0:T(8,128)(2,1)S(1)}, u32[]{:S(2)}, u32[]{:S(2)}) collective-permute-start(bf16[256,1024]{1,0:T(8,128)(2,1)} %get-tuple-element.38), channel_id=1, source_target_pairs={{0,128},{16,144},{32,160},{48,176},{64,192},{80,208},{96,224},{112... | collective-permute-start | bytes 1572872 | tf_op jit(solution)/shard_map/ppermute | solution.py:347
  (4 other events, 16.7 us)
Sparse Core Ops, SparseCore 0:
  9.4 63.7 all-gather.2
  78.8 58.2 all-gather.4
